TPU v7x, 32 devices: a whole 2x2x4 slice. The times are simulated.
32 devices in a mesh: expert: 8 (over z, y), fsdp: 2 (over x), replica: 2 (over core).
Axes of the slice: x: 2, y: 2, z: 4, core: 2. Of those that a mesh axis runs over, the one named last changes fastest.
Arguments:
- out_grad: bfloat16 [4096, 2048], P(('expert', 'fsdp', 'replica')), may hold values from -6 to 6
- hidden_saved: bfloat16 [4096, 8, 768], P(('expert', 'fsdp', 'replica')), may hold values from -6 to 6
- gate_probs: float32 [4096, 8], P(('expert', 'fsdp', 'replica')), may hold values from 0.05 to 0.5
- expert_ids: int32 [4096, 8], P(('expert', 'fsdp', 'replica')), may hold values from 0 to 15, all different within a row; in each aligned block of 128 rows (0 to 127, 128 to 255, ...) at most 128 rows name the same one
- weight_q: bfloat16 [16, 768, 2048], P('expert', 'fsdp'), may hold values from -0.21875 to 0.21875
- weight_exp: int32 [16, 768, 16], P('expert', 'fsdp'), may hold values from -1 to 1
- master: float32 [16, 768, 2048], P('expert', ('fsdp', 'replica')), may hold values from -0.21875 to 0.21875
- moment1: bfloat16 [16, 768, 2048], P('expert', ('fsdp', 'replica')), may hold values from -6 to 6
- moment2: bfloat16 [16, 768, 2048], P('expert', ('fsdp', 'replica')), may hold values from 0.099609375 to 10
Outputs:
- hidden_grad: bfloat16 [4096, 8, 768], P(('expert', 'fsdp', 'replica'))
- gate_grad: float32 [4096, 8], P(('expert', 'fsdp', 'replica'))
- master_new: float32 [16, 768, 2048], P('expert', ('fsdp', 'replica'))
- moment1_new: bfloat16 [16, 768, 2048], P('expert', ('fsdp', 'replica'))
- moment2_new: bfloat16 [16, 768, 2048], P('expert', ('fsdp', 'replica'))
Inputs may be any that keep to these rules, and one draw needn't show every extreme that they name: `expert_ids`: each token names 8 different experts; the tokens of one device name any one expert at most 128 times.
All inputs are finite; a program needn't handle non-finite values.
Results may differ from a plain program's by a relative error of at most 0.0051.
Values may be sent and summed in bfloat16 or wider, within the bound.
No kernel may reach another device: no remote copies, remote signals or barrier semaphores. Data moves between devices by JAX's collectives and lax.ppermute only.
A program may use at most 128 MiB of HBM per device.

v0:
```python
import jax
import jax.numpy as jnp
from jax import lax
from jax.sharding import PartitionSpec as P


def body(
    out_grad, hidden_saved, gate_probs, expert_ids, weight_q, weight_exp, master, moment1, moment2
):
    tokens_here, top_count = expert_ids.shape
    experts_here, rows_here, model_width = weight_q.shape
    hidden_width = hidden_saved.shape[2]
    expert_groups = lax.axis_size("expert")
    experts_all = expert_groups * experts_here
    capacity = min(tokens_here, 2 * tokens_here * top_count // experts_all)
    routes = tokens_here * top_count
    flat_ids = expert_ids.reshape(-1)
    onehot = (flat_ids[:, None] == jnp.arange(experts_all, dtype=jnp.int32)[None, :]).astype(
        jnp.int32
    )
    rank_in_expert = jnp.sum(jnp.cumsum(onehot, axis=0) * onehot, axis=1) - 1
    slot_index = flat_ids * capacity + rank_in_expert
    route_of_slot = (
        jnp.full((experts_all * capacity,), routes, jnp.int32)
        .at[slot_index]
        .set(jnp.arange(routes, dtype=jnp.int32))
    )
    filled = route_of_slot < routes
    clamped = jnp.minimum(route_of_slot, routes - 1)
    weighted = (
        (gate_probs[..., None] * hidden_saved.astype(jnp.float32))
        .astype(jnp.bfloat16)
        .reshape(routes, hidden_width)
    )
    zero_value = jnp.zeros((), jnp.bfloat16)
    dy_send = jnp.where(filled[:, None], out_grad[clamped // top_count], zero_value)
    weighted_send = jnp.where(filled[:, None], weighted[clamped], zero_value)
    dy_send = dy_send.reshape(expert_groups, experts_here, capacity, model_width)
    weighted_send = weighted_send.reshape(expert_groups, experts_here, capacity, hidden_width)
    recv_dy, recv_weighted = (
        lax.all_to_all(dy_send, "expert", split_axis=0, concat_axis=0, tiled=True),
        lax.all_to_all(weighted_send, "expert", split_axis=0, concat_axis=0, tiled=True),
    )
    scales = jnp.exp2(weight_exp.astype(jnp.float32))
    blocks = weight_exp.shape[2]
    weight_local = (
        (
            weight_q.astype(jnp.float32).reshape(
                experts_here, rows_here, blocks, model_width // blocks
            )
            * scales[..., None]
        )
        .reshape(experts_here, rows_here, model_width)
        .astype(jnp.bfloat16)
    )
    back_rows = jnp.einsum(
        "secd,efd->secf",
        recv_dy,
        lax.all_gather(weight_local, "fsdp", axis=1, tiled=True),
        preferred_element_type=jnp.float32,
    ).astype(jnp.bfloat16)
    returned = lax.all_to_all(back_rows, "expert", split_axis=0, concat_axis=0, tiled=True)
    back_route = returned.reshape(experts_all * capacity, hidden_width)[slot_index].reshape(
        tokens_here, top_count, hidden_width
    )
    back_float = back_route.astype(jnp.float32)
    hidden_grad = (gate_probs[..., None] * back_float).astype(jnp.bfloat16)
    gate_grad = jnp.sum(hidden_saved.astype(jnp.float32) * back_float, axis=-1)
    partial_grad = jnp.einsum(
        "secf,secd->efd", recv_weighted, recv_dy, preferred_element_type=jnp.float32
    )
    gradient = lax.psum_scatter(partial_grad, ("fsdp", "replica"), scatter_dimension=1, tiled=True)
    first = 0.9 * moment1.astype(jnp.float32) + 0.1 * gradient
    second = 0.95 * moment2.astype(jnp.float32) + 0.05 * gradient * gradient
    update = first / (1.0 - 0.9**20) / (jnp.sqrt(second / (1.0 - 0.95**20)) + 1e-08) + 0.1 * master
    master_new = master - 0.001 * update
    return (
        hidden_grad,
        gate_grad,
        master_new,
        first.astype(jnp.bfloat16),
        second.astype(jnp.bfloat16),
    )


def solution(mesh):
    in_specs = (
        P(("expert", "fsdp", "replica"), None),
        P(("expert", "fsdp", "replica"), None, None),
        P(("expert", "fsdp", "replica"), None),
        P(("expert", "fsdp", "replica"), None),
        P("expert", "fsdp", None),
        P("expert", "fsdp", None),
        P("expert", ("fsdp", "replica"), None),
        P("expert", ("fsdp", "replica"), None),
        P("expert", ("fsdp", "replica"), None),
    )
    out_specs = (
        P(("expert", "fsdp", "replica"), None, None),
        P(("expert", "fsdp", "replica"), None),
        P("expert", ("fsdp", "replica"), None),
        P("expert", ("fsdp", "replica"), None),
        P("expert", ("fsdp", "replica"), None),
    )
    return jax.shard_map(body, mesh=mesh, in_specs=in_specs, out_specs=out_specs, check_vma=False)
```

profile of v0, /device:TPU:8, one launch (start us, length us, event | category | flops | bytes accessed | tf_op | source)
XLA Modules:
  0.0 539.8 jit_solution(2937176001825923603)
XLA Ops:
  7.2 0.7 broadcast_multiply_fusion
  7.9 0.8 copy.33
  8.9 0.1 copy.32
  9.0 0.1 mul.86
  9.1 4.5 reduce-window.6
  13.7 0.1 copy.35
  14.1 4.3 scatter_custom_fusion
  18.5 11.0 %gather_fusion = bf16[2048,2048]{1,0:T(8,128)(2,1)} fusion(bf16[128,2048]{1,0:T(8,128)(2,1)S(1)} %copy-done, s32[2048]{0:T(1024)S(1)} %get-tuple-element.17), kind=kCustom, calls=%fused_computation | custom fusion | bytes 16785408 | tf_op jit(solution)/shard_map/gather | solution.py:36
  29.5 7.3 %broadcast_select_fusion = bf16[8,2,128,2048]{3,2,1,0:T(8,128)(2,1)} fusion(bf16[8,2,128,2048]{3,2,1,0:T(8,128)(2,1)} %bitcast.42, pred[8,2,128]{2,1,0:T(4,128)(4,1)S(1)} %broadcast_in_dim.40), kind=kLoop, calls=%fused_computation.6 | loop fusion | flops 4194304 | bytes 16779264 | tf_op jit(solution)/shard_map/jit(_where)/select_n | solution.py:36
  36.7 6.4 %all-to-all-start = ((bf16[8,2,128,2048]{3,2,1,0:T(8,128)(2,1)}), bf16[8,2,128,2048]{3,2,1,0:T(8,128)(2,1)}, u32[]{:S(2)}, u32[]{:S(2)}) async-start(bf16[8,2,128,2048]{3,2,1,0:T(8,128)(2,1)} %broadcast_select_fusion), calls=%async_computation | async-start | bytes 16777216 | tf_op jit(solution)/shard_map/all_to_all | solution.py:41
  43.2 0.2 copy.31
  43.3 3.8 mul.81
  47.2 7.2 %mul.82 = f32[2,384,2048]{2,1,0:T(8,128)} reshape(f32[2,384,16,128]{3,2,1,0:T(8,128)} %mul.81) | data formatting | bytes 12582912 | tf_op jit(solution)/shard_map/mul | solution.py:48
  54.4 5.5 %multiply_convert_fusion = bf16[2,384,2048]{2,1,0:T(8,128)(2,1)} fusion(f32[2,384,2048]{2,1,0:T(8,128)} %mul.82, bf16[2,384,2048]{2,1,0:T(8,128)(2,1)S(1)} %copy-done.2), kind=kLoop, calls=%fused_computation.8 | loop fusion | flops 4718592 | bytes 12582912 | tf_op jit(solution)/shard_map/convert_element_type | solution.py:54
  60.0 81.4 %all-gather.2.cloned.1.call-done = bf16[2,768,2048]{2,1,0:T(8,128)(2,1)} async-done(((bf16[2,384,2048]{2,1,0:T(8,128)(2,1)}), bf16[2,768,2048]{2,1,0:T(8,128)(2,1)}) %all-gather.2.cloned.1.call-update) | async-done | bytes 6291472 | tf_op jit(solution)/shard_map/all_gather | solution.py:59
  141.4 82.4 %all-to-all-done = bf16[8,2,128,2048]{3,2,1,0:T(8,128)(2,1)} async-done(((bf16[8,2,128,2048]{3,2,1,0:T(8,128)(2,1)}), bf16[8,2,128,2048]{3,2,1,0:T(8,128)(2,1)}, u32[]{:S(2)}, u32[]{:S(2)}) %all-to-all-start) | async-done | bytes 8388640 | tf_op jit(solution)/shard_map/all_to_all | solution.py:41
  223.7 10.1 %convert_bitcast_fusion = bf16[8,2,128,768]{2,3,0,1:T(8,128)(2,1)S(1)} fusion(bf16[8,2,128,2048]{3,2,1,0:T(8,128)(2,1)} %all-to-all-done, bf16[2,768,2048]{2,1,0:T(8,128)(2,1)} %all-gather.2.cloned.1.call-done), kind=kOutput, calls=%fused_computation.20 | convolution fusion | flops 6444023808 | bytes 17825792 | tf_op jit(solution)/shard_map/secd,efd->secf/dot_general | solution.py:56
  233.8 2.0 copy.38
  235.8 7.1 %all-to-all-start.1 = ((bf16[8,2,128,768]{2,3,1,0:T(8,128)(2,1)}), bf16[8,2,128,768]{2,3,1,0:T(8,128)(2,1)}, u32[]{:S(2)}, u32[]{:S(2)}) async-start(bf16[8,2,128,768]{2,3,1,0:T(8,128)(2,1)} %copy.38), calls=%async_computation.1 | async-start | bytes 6291456 | tf_op jit(solution)/shard_map/all_to_all | solution.py:62
  242.9 0.1 copy.30
  243.0 67.6 %all-to-all-done.1 = bf16[8,2,128,768]{2,3,1,0:T(8,128)(2,1)} async-done(((bf16[8,2,128,768]{2,3,1,0:T(8,128)(2,1)}), bf16[8,2,128,768]{2,3,1,0:T(8,128)(2,1)}, u32[]{:S(2)}, u32[]{:S(2)}) %all-to-all-start.1) | async-done | bytes 3145760 | tf_op jit(solution)/shard_map/all_to_all | solution.py:62
  310.6 3.2 copy.39
  313.7 5.2 gather_fusion.1
  319.0 3.9 fusion.13
  322.8 9.4 %gather_fusion.2 = bf16[2048,768]{1,0:T(8,128)(2,1)} fusion(bf16[1024,768]{1,0:T(8,128)(2,1)S(1)} %get-tuple-element.13, s32[2048]{0:T(1024)S(1)} %get-tuple-element.16), kind=kCustom, calls=%fused_computation.2 | custom fusion | bytes 6299648 | tf_op jit(solution)/shard_map/gather | solution.py:37
  332.2 3.3 broadcast_select_fusion.1
  335.5 3.5 copy.40
  339.0 75.9 %all_to_all.15 = bf16[8,2,128,768]{2,3,1,0:T(8,128)(2,1)S(1)} all-to-all(bf16[8,2,128,768]{2,3,1,0:T(8,128)(2,1)S(1)} %copy.40), channel_id=1, replica_groups=mesh['expert'=8,'fsdp'=2,'replica'=2] {'expert'}, dimensions={0} | all-to-all | bytes 6291456 | tf_op jit(solution)/shard_map/all_to_all | solution.py:42
  414.9 11.7 %convolution_bitcast_fusion = f32[2,768,2048]{2,1,0:T(8,128)} fusion(bf16[8,2,128,768]{2,3,1,0:T(8,128)(2,1)S(1)} %all_to_all.15, bf16[8,2,128,2048]{3,2,1,0:T(8,128)(2,1)} %all-to-all-done), kind=kOutput, calls=%fused_computation.9 | convolution fusion | flops 6442450944 | bytes 24117248 | tf_op jit(solution)/shard_map/secf,secd->efd/dot_general | solution.py:69
  426.7 0.7 copy.43
  427.3 98.0 %reduce-scatter.2.cloned.1.call-done = f32[2,192,2048]{2,1,0:T(8,128)} async-done(((f32[2,768,2048]{2,1,0:T(8,128)}), f32[2,192,2048]{2,1,0:T(8,128)}) %reduce-scatter.2.cloned.1.call-update) | async-done | bytes 3145744 | tf_op jit(solution)/shard_map/reduce_scatter | solution.py:72
  525.3 7.7 %fusion.12 = (bf16[2,192,2048]{2,1,0:T(8,128)(2,1)}, f32[2,192,2048]{2,1,0:T(8,128)}, bf16[2,192,2048]{2,1,0:T(8,128)(2,1)}) fusion(f32[2,192,2048]{2,1,0:T(8,128)} %reduce-scatter.2.cloned.1.call-done, bf16[2,192,2048]{2,1,0:T(8,128)(2,1)S(1)} %copy-done.3, f32[2,192,2048]{2,1,0:T(8,128)} %param.15, bf16[2,192,2048]{2,1,0:T(8,128)(2,1)} %param.16), kind=kLoop, calls=%fused_computation.23 | loop fusion | flops 14942208 | bytes 15728640 | tf_op jit(solution)/shard_map/convert_element_type | solution.py:82
  (33 shorter events, 0.6 us)
Async XLA Ops:
  7.2 11.3 %copy-start = (bf16[128,2048]{1,0:T(8,128)(2,1)S(1)}, bf16[128,2048]{1,0:T(8,128)(2,1)}, u32[]{:S(2)}) copy-start(bf16[128,2048]{1,0:T(8,128)(2,1)} %param.9) | copy-start | bytes 1572868
  36.7 6.4 %copy-start.4 = (s32[2,384,16]{1,2,0:T(8,128)S(1)}, s32[2,384,16]{1,2,0:T(8,128)}, u32[]{:S(2)}) copy-start(s32[2,384,16]{1,2,0:T(8,128)} %param.14) | copy-start | bytes 147460
  36.7 187.0 %all-to-all-start = ((bf16[8,2,128,2048]{3,2,1,0:T(8,128)(2,1)}), bf16[8,2,128,2048]{3,2,1,0:T(8,128)(2,1)}, u32[]{:S(2)}, u32[]{:S(2)}) async-start(bf16[8,2,128,2048]{3,2,1,0:T(8,128)(2,1)} %broadcast_select_fusion), calls=%async_computation | async-start | bytes 16777216 | tf_op jit(solution)/shard_map/all_to_all | solution.py:41
  43.1 98.2 %all-gather.2.cloned.1.call-start = ((), (), s32[]{:S(2)}) async-start(), calls=%async_computation.4 | async-start | bytes 9437184 | tf_op jit(solution)/shard_map/all_gather | solution.py:59
  47.2 7.3 %copy-start.2 = (bf16[2,384,2048]{2,1,0:T(8,128)(2,1)S(1)}, bf16[2,384,2048]{2,1,0:T(8,128)(2,1)}, u32[]{:S(2)}) copy-start(bf16[2,384,2048]{2,1,0:T(8,128)(2,1)} %param.13) | copy-start | bytes 9437188
  235.8 7.1 %copy-start.5 = (f32[128,8]{0,1:T(8,128)S(1)}, f32[128,8]{0,1:T(8,128)}, u32[]{:S(2)}) copy-start(f32[128,8]{0,1:T(8,128)} %param.11) | copy-start | bytes 12292
  235.8 74.8 %all-to-all-start.1 = ((bf16[8,2,128,768]{2,3,1,0:T(8,128)(2,1)}), bf16[8,2,128,768]{2,3,1,0:T(8,128)(2,1)}, u32[]{:S(2)}, u32[]{:S(2)}) async-start(bf16[8,2,128,768]{2,3,1,0:T(8,128)(2,1)} %copy.38), calls=%async_computation.1 | async-start | bytes 6291456 | tf_op jit(solution)/shard_map/all_to_all | solution.py:62
  242.9 282.4 %reduce-scatter.2.cloned.1.call-start = ((), (), s32[]{:S(2)}) async-start(), calls=%async_computation.5 | async-start | bytes 15728640 | tf_op jit(solution)/shard_map/reduce_scatter | solution.py:72
  426.6 98.7 %copy-start.3 = (bf16[2,192,2048]{2,1,0:T(8,128)(2,1)S(1)}, bf16[2,192,2048]{2,1,0:T(8,128)(2,1)}, u32[]{:S(2)}) copy-start(bf16[2,192,2048]{2,1,0:T(8,128)(2,1)} %param.17) | copy-start | bytes 4718596
  525.3 7.7 %copy-start.1 = (bf16[128,2048]{1,0:T(8,128)(2,1)S(1)}, bf16[128,2048]{1,0:T(8,128)(2,1)}, u32[]{:S(2)}) copy-start(bf16[128,2048]{1,0:T(8,128)(2,1)} %param.9) | copy-start | bytes 1572868
Sparse Core Ops, SparseCore 0:
  60.1 81.2 all-gather.1
  426.8 98.4 reduce-scatter.1
where the time goes:
time: 542 us; the launch traced here: 540 us
  waiting for transfers between devices  329 us (61%)
  blocking collectives  75.9 us (14%)
  local copies, waits for them, and re-layouts  52 us (10%)
  other arithmetic  33.1 us (6%)
  matrix products  21.8 us (4%)
  between operations  14.2 us (3%)
  starting transfers between devices  13.5 us (2%)
    reduce_scatter x1, waiting for transfers between devices, body(): lax.psum_scatter(partial_grad, ('fsdp', 'replica'), scatter_dimension=1,...  98 us
    all_to_all x1, waiting for transfers between devices, body(): lax.all_to_all(dy_send, 'expert', split_axis=0, concat_axis=0, tiled=True)  82.4 us
    all_gather x1, waiting for transfers between devices, body(): lax.all_gather(weight_local, 'fsdp', axis=1, tiled=True)  81.4 us
    all_to_all x1, blocking collectives, body(): lax.all_to_all(weighted_send, 'expert', split_axis=0, concat_axis=0, tile...  75.9 us
    all_to_all x1, waiting for transfers between devices, body(): lax.all_to_all(back_rows, 'expert', split_axis=0, concat_axis=0, tiled=True)  67.6 us
    dot_general x1, matrix products, body(): jnp.einsum('secf,secd->efd', recv_weighted, recv_dy, preferred_element_ty...  11.7 us
    mul x2, local copies, waits for them, and re-layouts, body(): weight_q.astype(jnp.float32)  11.1 us
    gather x1, local copies, waits for them, and re-layouts, body(): out_grad[clamped // top_count]  11 us
  transfers between devices with their start and end apart: 4, of which 4 were waited for; matrix products, arithmetic and copies ran while one was open for 3% of the time, Pallas kernels for 0%

commit v1 on v0

--- a/solution.py
+++ b/solution.py
@@ -1,10 +1,11 @@
 import jax
 import jax.numpy as jnp
 from jax import lax
+from jax.experimental import pallas as pl
+from jax.experimental.pallas import tpu as pltpu
 from jax.sharding import PartitionSpec as P
 
-
-def body(
+def slots_body(
     out_grad, hidden_saved, gate_probs, expert_ids, weight_q, weight_exp, master, moment1, moment2
 ):
     tokens_here, top_count = expert_ids.shape
@@ -83,6 +84,300 @@
     )
 
 
+VMEM = 100 * 2**20 // 2
+TOKEN_BLOCK = 16
+
+
+def pick(index, options):
+    result = options[0]
+    for number, option in enumerate(options[1:], 1):
+        result = jnp.where(index == number, option, result)
+    return result
+
+
+def route_match(ids, column_keys):
+    tokens, top = ids.shape
+    shape = (tokens, top, top)
+    token = lax.broadcasted_iota(jnp.int32, shape, 0)
+    diagonal = lax.broadcasted_iota(jnp.int32, shape, 1) == lax.broadcasted_iota(
+        jnp.int32, shape, 2
+    )
+    keys = jnp.where(diagonal, ids[:, None, :] * tokens + token, 0).astype(jnp.float32)
+    keys = jnp.sum(keys.reshape(tokens * top, top), axis=1, keepdims=True)
+    return jnp.where(keys == column_keys, 1.0, 0.0).astype(jnp.bfloat16)
+
+
+def route_column(values):
+    tokens, top = values.shape
+    shape = (tokens, top, top)
+    diagonal = lax.broadcasted_iota(jnp.int32, shape, 1) == lax.broadcasted_iota(
+        jnp.int32, shape, 2
+    )
+    spread = jnp.where(diagonal, jnp.broadcast_to(values[:, None, :], shape), 0.0)
+    return jnp.sum(spread.reshape(tokens * top, top), axis=1, keepdims=True)
+
+
+def route_square(column, tokens, top):
+    shape = (tokens, top, top)
+    diagonal = lax.broadcasted_iota(jnp.int32, shape, 1) == lax.broadcasted_iota(
+        jnp.int32, shape, 2
+    )
+    spread = jnp.broadcast_to(column, (tokens * top, top)).reshape(shape)
+    return jnp.sum(jnp.where(diagonal, spread, 0.0), axis=1)
+
+
+def spread_kernel(groups, here, parts, place, keys, ids, gate, hidden, *outs):
+    fsdp, replica = parts
+    tokens, top, width = hidden.shape
+    unit = width // (fsdp * replica)
+    match = route_match(ids[...], keys[...])
+    values = hidden[...].astype(jnp.float32).reshape(tokens * top, width)
+    weighted = (route_column(gate[...]) * values).astype(jnp.bfloat16)
+
+    def block(f, r):
+        at = (f * replica + r) * unit
+        return weighted[:, at : at + unit]
+
+    shares = [
+        pick(
+            place[1],
+            [
+                jnp.concatenate([block((f + o) % fsdp, r) for o in range(fsdp)], axis=1)
+                for f in range(fsdp)
+            ],
+        )
+        for r in range(replica)
+    ]
+    for c in range(replica):
+        share = pick(place[2], [shares[(r + c) % replica] for r in range(replica)])
+        rows = lax.dot_general(
+            match, share, (((0,), (0,)), ((), ())), preferred_element_type=jnp.float32
+        ).astype(jnp.bfloat16)
+        for g in range(groups):
+            for e in range(here):
+                at = (g * here + e) * tokens
+                outs[g * replica + c][:, e * fsdp * unit : (e + 1) * fsdp * unit] = rows[
+                    at : at + tokens
+                ]
+
+
+def collect_kernel(groups, here, parts, place, keys, ids, gate, hidden, *refs):
+    fsdp, replica = parts
+    backs, (hidden_grad, gate_grad) = refs[:-2], refs[-2:]
+    tokens, top, width = hidden.shape
+    unit = width // (fsdp * replica)
+    match = route_match(ids[...], keys[...])
+    found = []
+    for c in range(replica):
+        rows = jnp.concatenate(
+            [
+                backs[g * replica + c][:, e * fsdp * unit : (e + 1) * fsdp * unit]
+                for g in range(groups)
+                for e in range(here)
+            ],
+            axis=0,
+        )
+        found.append(jnp.dot(match, rows, preferred_element_type=jnp.float32))
+    shares = [
+        pick(place[2], [found[(h - r) % replica] for r in range(replica)])
+        for h in range(replica)
+    ]
+    back = jnp.concatenate(
+        [
+            pick(
+                place[1],
+                [
+                    shares[h][:, (f - m) % fsdp * unit : ((f - m) % fsdp + 1) * unit]
+                    for m in range(fsdp)
+                ],
+            )
+            for f in range(fsdp)
+            for h in range(replica)
+        ],
+        axis=1,
+    )
+    values = hidden[...].astype(jnp.float32).reshape(tokens * top, width)
+    scaled = route_column(gate[...]) * back
+    hidden_grad[...] = scaled.reshape(tokens, top, width).astype(jnp.bfloat16)
+    gate_grad[...] = route_square(jnp.sum(values * back, axis=1, keepdims=True), tokens, top)
+
+
+def scale_kernel(place, values, exponents, out):
+    blocks = exponents.shape[2]
+    width = values.shape[2] // blocks
+    scales = jnp.exp2(exponents[0].astype(jnp.float32))
+    for b in range(blocks):
+        at = slice(b * width, (b + 1) * width)
+        out[0, :, at] = (values[0, :, at].astype(jnp.float32) * scales[:, b : b + 1]).astype(
+            jnp.bfloat16
+        )
+
+
+def dense_body(
+    out_grad, hidden_saved, gate_probs, expert_ids, weight_q, weight_exp, master, moment1, moment2
+):
+    tokens, top = expert_ids.shape
+    here, rows_here, model_width = weight_q.shape
+    width = hidden_saved.shape[2]
+    groups = lax.axis_size("expert")
+    fsdp, replica = lax.axis_size("fsdp"), lax.axis_size("replica")
+    me, mf, mr = lax.axis_index("expert"), lax.axis_index("fsdp"), lax.axis_index("replica")
+    inner = 2 if groups % 2 == 0 else 1
+    outer = groups // inner
+    unit = width // (fsdp * replica)
+    block = min(TOKEN_BLOCK, tokens)
+    offsets = [(s, j) for s in range(outer) for j in range(inner)]
+
+    def moved(e, s, j):
+        return (e // inner + s) % outer * inner + (e % inner + j) % inner
+
+    def send(x, s, j, c):
+        if (s, j, c) == (0, 0, 0):
+            return x
+        pairs = [
+            (e * replica + r, moved(e, s, j) * replica + (r + c) % replica)
+            for e in range(groups)
+            for r in range(replica)
+        ]
+        return lax.ppermute(x, ("expert", "replica"), pairs)
+
+    place = jnp.stack([me, mf, mr]).astype(jnp.int32)
+    weight_part = pl.pallas_call(
+        scale_kernel,
+        out_shape=jax.ShapeDtypeStruct((here, unit, model_width), jnp.bfloat16),
+        grid_spec=pltpu.PrefetchScalarGridSpec(
+            num_scalar_prefetch=1,
+            grid=(here,),
+            in_specs=[
+                pl.BlockSpec((1, unit, model_width), lambda e, p: (e, p[2], 0)),
+                pl.BlockSpec((1, unit, weight_exp.shape[2]), lambda e, p: (e, p[2], 0)),
+            ],
+            out_specs=pl.BlockSpec((1, unit, model_width), lambda e, p: (e, 0, 0)),
+        ),
+        compiler_params=pltpu.CompilerParams(vmem_limit_bytes=VMEM),
+        name="scale",
+    )(place, weight_q, weight_exp)
+
+    ups = outer // 2
+    line = {0: out_grad}
+    for s in range(1, ups + 1):
+        line[s] = send(line[s - 1], 1, 0, 0)
+    for s in range(outer - 1, ups, -1):
+        line[s] = send(line[(s + 1) % outer], outer - 1, 0, 0)
+    dy = {}
+    for s in range(outer):
+        for j in range(inner):
+            held = send(line[s], 0, j, 0)
+            for c in range(replica):
+                dy[s, j, c] = send(held, 0, 0, c)
+
+    weight_parts = [weight_part] + [
+        lax.ppermute(weight_part, "fsdp", [(f, (f - o) % fsdp) for f in range(fsdp)])
+        for o in range(1, fsdp)
+    ]
+    weight_rows = jnp.stack(weight_parts, axis=1).reshape(here * fsdp * unit, model_width)
+
+    def keys(sign):
+        group = [
+            ((me // inner + sign * s) % outer) * inner + (me % inner + sign * j) % inner
+            for s, j in offsets
+        ]
+        expert = (jnp.stack(group)[:, None] * here + jnp.arange(here)[None, :]).reshape(-1)
+        return (
+            (expert[:, None] * block + jnp.arange(block)[None, :])
+            .reshape(1, -1)
+            .astype(jnp.float32)
+        )
+
+    column_keys = keys(1)
+    pieces = len(offsets) * replica
+    piece = (here * fsdp * unit,)
+    row_spec = pl.BlockSpec((block,) + piece, lambda i, p: (i, 0))
+    token_specs = [
+        pl.BlockSpec(column_keys.shape, lambda i, p: (0, 0)),
+        pl.BlockSpec((block, top), lambda i, p: (i, 0)),
+        pl.BlockSpec((block, top), lambda i, p: (i, 0)),
+        pl.BlockSpec((block, top, width), lambda i, p: (i, 0, 0)),
+    ]
+    spread = pl.pallas_call(
+        lambda *refs: spread_kernel(groups, here, (fsdp, replica), *refs),
+        out_shape=[jax.ShapeDtypeStruct((tokens,) + piece, jnp.bfloat16)] * pieces,
+        grid_spec=pltpu.PrefetchScalarGridSpec(
+            num_scalar_prefetch=1,
+            grid=(tokens // block,),
+            in_specs=token_specs,
+            out_specs=[row_spec] * pieces,
+        ),
+        compiler_params=pltpu.CompilerParams(vmem_limit_bytes=VMEM),
+        name="spread",
+    )(place, column_keys, expert_ids, gate_probs, hidden_saved)
+    spread, _ = lax.optimization_barrier((spread, line[ups]))
+    order = [(s, j, c) for s, j in offsets for c in range(replica)]
+    hid = {o: send(x, *o) for o, x in zip(order, spread)}
+
+    back = [
+        lax.dot_general(
+            dy[o], weight_rows, (((1,), (1,)), ((), ())), preferred_element_type=jnp.float32
+        ).astype(jnp.bfloat16)
+        for o in order
+    ]
+    back, hid = lax.optimization_barrier((back, hid))
+    returned = [
+        send(x, (-s) % outer, (-j) % inner, (-c) % replica) for (s, j, c), x in zip(order, back)
+    ]
+
+    hid_all = jnp.concatenate([hid[o] for o in order], axis=0)
+    dy_all = jnp.concatenate([dy[o] for o in order], axis=0)
+    partial_grad = lax.dot_general(
+        hid_all, dy_all, (((0,), (0,)), ((), ())), preferred_element_type=jnp.float32
+    ).reshape(here, fsdp, unit, model_width)
+    gradient = partial_grad[:, 0]
+    for o in range(1, fsdp):
+        gradient = gradient + lax.ppermute(
+            partial_grad[:, o].astype(jnp.bfloat16),
+            "fsdp",
+            [(f, (f + o) % fsdp) for f in range(fsdp)],
+        ).astype(jnp.float32)
+    first = 0.9 * moment1.astype(jnp.float32) + 0.1 * gradient
+    second = 0.95 * moment2.astype(jnp.float32) + 0.05 * gradient * gradient
+    update = first / (1.0 - 0.9**20) / (jnp.sqrt(second / (1.0 - 0.95**20)) + 1e-08) + 0.1 * master
+    master_new = master - 0.001 * update
+
+    hidden_grad, gate_grad = pl.pallas_call(
+        lambda *refs: collect_kernel(groups, here, (fsdp, replica), *refs),
+        out_shape=[
+            jax.ShapeDtypeStruct(hidden_saved.shape, jnp.bfloat16),
+            jax.ShapeDtypeStruct(gate_probs.shape, jnp.float32),
+        ],
+        grid_spec=pltpu.PrefetchScalarGridSpec(
+            num_scalar_prefetch=1,
+            grid=(tokens // block,),
+            in_specs=token_specs + [row_spec] * pieces,
+            out_specs=[
+                pl.BlockSpec((block, top, width), lambda i, p: (i, 0, 0)),
+                pl.BlockSpec((block, top), lambda i, p: (i, 0)),
+            ],
+        ),
+        compiler_params=pltpu.CompilerParams(vmem_limit_bytes=VMEM),
+        name="collect",
+    )(place, column_keys, expert_ids, gate_probs, hidden_saved, *returned)
+    return (
+        hidden_grad,
+        gate_grad,
+        master_new,
+        first.astype(jnp.bfloat16),
+        second.astype(jnp.bfloat16),
+    )
+
+
+def body(*args):
+    tokens, top = args[3].shape
+    experts = lax.axis_size("expert") * args[4].shape[0]
+    if min(tokens, 2 * tokens * top // experts) == tokens:
+        return dense_body(*args)
+    return slots_body(*args)
+
+
 def solution(mesh):
     in_specs = (
         P(("expert", "fsdp", "replica"), None),

time: 542 us -> 271 us (0.50)
  waiting for transfers between devices: 329 us -> 122 us
  blocking collectives: 75.9 us -> 0 us
  starting transfers between devices: 13.5 us -> 74.7 us
  local copies, waits for them, and re-layouts: 52 us -> 17.9 us
  other arithmetic: 33.1 us -> 8.32 us
  Pallas kernels: 0 us -> 17.6 us
  between operations: 14.2 us -> 1.08 us
    all_to_all x2 -> x0, waiting for transfers between devices: 150 us -> none  [the longest x1 82.4 us: body(): lax.all_to_all(dy_send, 'expert', split_axis=0, concat_axis=0, tiled=True)]
    ppermute x0 -> x47, waiting for transfers between devices: none -> 122 us  [the longest x45 113 us: send(): return lax.ppermute(x, ('expert', 'replica'), pairs)]
    reduce_scatter x1 -> x0, waiting for transfers between devices: 98 us -> none  [body(): lax.psum_scatter(partial_grad, ('fsdp', 'replica'), scatter_dimension=1,...]
    all_gather x1 -> x0, waiting for transfers between devices: 81.4 us -> none  [body(): lax.all_gather(weight_local, 'fsdp', axis=1, tiled=True)]
    all_to_all x1 -> x0, blocking collectives: 75.9 us -> none  [body(): lax.all_to_all(weighted_send, 'expert', split_axis=0, concat_axis=0, tile...]
    ppermute x0 -> x47, starting transfers between devices: none -> 74.7 us  [the longest x45 71.7 us: send(): return lax.ppermute(x, ('expert', 'replica'), pairs)]
    gather x3 -> x0, local copies, waits for them, and re-layouts: 25.6 us -> none  [the longest x1 11 us: body(): out_grad[clamped // top_count]]
    pallas_call x0 -> x3, Pallas kernels: none -> 17.6 us  [the longest x1 8.22 us: dense_body(): pl.pallas_call(lambda *refs: collect_kernel(groups, here, (fsdp, replica)...]
  transfers between devices with their start and end apart: 4 -> 47, of which waited for: 4 -> 23; matrix products, arithmetic and copies ran while one was open for 3% -> 13% of each run, Pallas kernels for 0% -> 7%
where the time goes in v1:
time: 271 us; the launch traced here: 268 us
  waiting for transfers between devices  122 us (45%)
  starting transfers between devices  74.7 us (28%)
  matrix products  26.7 us (10%)
  local copies, waits for them, and re-layouts  17.9 us (7%)
  Pallas kernels  17.6 us (6%)
  other arithmetic  8.32 us (3%)
    ppermute x45, waiting for transfers between devices, send(): return lax.ppermute(x, ('expert', 'replica'), pairs)  113 us
    ppermute x45, starting transfers between devices, send(): return lax.ppermute(x, ('expert', 'replica'), pairs)  71.7 us
    dot_general x16, matrix products, dense_body(): lax.dot_general(dy[o], weight_rows, (((1,), (1,)), ((), ())), preferred_e...  19.9 us
    unnamed x44, local copies, waits for them, and re-layouts  15.6 us
    ppermute x1, waiting for transfers between devices, dense_body(): lax.ppermute(weight_part, 'fsdp', [(f, (f - o) % fsdp) for f in range(fsd...  8.22 us
    pallas_call x1, Pallas kernels, dense_body(): pl.pallas_call(lambda *refs: collect_kernel(groups, here, (fsdp, replica)...  8.22 us
    convert_element_type x1, other arithmetic, dense_body(): second.astype(jnp.bfloat16)  7.8 us
    dot_general x1, matrix products, dense_body(): lax.dot_general(hid_all, dy_all, (((0,), (0,)), ((), ())), preferred_elem...  6.83 us
  transfers between devices with their start and end apart: 47, of which 23 were waited for; matrix products, arithmetic and copies ran while one was open for 13% of the time, Pallas kernels for 7%

profile of v1, /device:TPU:8, one launch (start us, length us, event | category | flops | bytes accessed | tf_op | source)
XLA Modules:
  0.0 267.9 jit_solution(14396902732481006282)
XLA Ops:
  6.5 9.2 %collective-permute-done.4 = bf16[128,2048]{1,0:T(8,128)(2,1)S(1)} collective-permute-done((bf16[128,2048]{1,0:T(8,128)(2,1)}, bf16[128,2048]{1,0:T(8,128)(2,1)S(1)}, u32[]{:S(2)}, u32[]{:S(2)}) %collective-permute-start.4) | collective-permute-done | bytes 524320 | tf_op jit(solution)/shard_map/ppermute | solution.py:242
  19.9 2.7 %scale.1 = bf16[2,192,2048]{2,1,0:T(8,128)(2,1)S(1)} custom-call(s32[3]{0:T(128)S(1)} %pad_add_fusion.place.refs_0_, bf16[2,384,2048]{2,1,0:T(8,128)(2,1)} %values.1, s32[2,384,16]{2,1,0:T(8,128)S(1)} %copy.38.exponents), custom_call_target="tpu_custom_call" | custom-call | tf_op jit(solution)/shard_map/scale/pallas_call | solution.py:245
  22.7 6.6 %spread.1 = (bf16[128,768]{1,0:T(8,128)(2,1)S(1)}, bf16[128,768]{1,0:T(8,128)(2,1)S(1)}, bf16[128,768]{1,0:T(8,128)(2,1)S(1)}, bf16[128,768]{1,0:T(8,128)(2,1)S(...) custom-call(s32[3]{0:T(128)S(1)} %pad_add_fusion.place.refs_0_, ...), custom_call_target="tpu_custom_call" | custom-call | tf_op jit(solution)/shard_map/spread/pallas_call | solution.py:302
  29.3 11.7 %collective-permute-start.8 = (bf16[128,2048]{1,0:T(8,128)(2,1)S(1)}, bf16[128,2048]{1,0:T(8,128)(2,1)S(1)}, u32[]{:S(2)}, u32[]{:S(2)}) collective-permute-start(bf16[128,2048]{1,0:T(8,128)(2,1)S(1)} %collective-permute-done.4), channel_id=1, source_target_pairs={{0,8},{1,9},{4,12},{5,13},{8,16},{9,17},{12,20},{13,21},{16,24},{1... | collective-permute-start | bytes 1572872 | tf_op jit(solution)/shard_map/ppermute | solution.py:242
  47.7 5.2 %collective-permute-done.8 = bf16[128,2048]{1,0:T(8,128)(2,1)S(1)} collective-permute-done((bf16[128,2048]{1,0:T(8,128)(2,1)S(1)}, bf16[128,2048]{1,0:T(8,128)(2,1)S(1)}, u32[]{:S(2)}, u32[]{:S(2)}) %collective-permute-start.8) | collective-permute-done | bytes 524320 | tf_op jit(solution)/shard_map/ppermute | solution.py:242
  58.1 11.3 %collective-permute-done.10 = bf16[128,2048]{1,0:T(8,128)(2,1)S(1)} collective-permute-done((bf16[128,2048]{1,0:T(8,128)(2,1)S(1)}, bf16[128,2048]{1,0:T(8,128)(2,1)S(1)}, u32[]{:S(2)}, u32[]{:S(2)}) %collective-permute-start.10) | collective-permute-done | bytes 524320 | tf_op jit(solution)/shard_map/ppermute | solution.py:242
  71.3 8.2 %collective-permute-done = bf16[2,192,2048]{2,1,0:T(8,128)(2,1)S(1)} collective-permute-done((bf16[2,192,2048]{2,1,0:T(8,128)(2,1)S(1)}, bf16[2,192,2048]{2,1,0:T(8,128)(2,1)S(1)}, u32[]{:S(2)}, u32[]{:S(2)}) %collective-permute-start) | collective-permute-done | bytes 1572896 | tf_op jit(solution)/shard_map/ppermute | solution.py:275
  100.7 3.9 %collective-permute-start.22 = (bf16[128,768]{1,0:T(8,128)(2,1)S(1)}, bf16[128,768]{1,0:T(8,128)(2,1)S(1)}, u32[]{:S(2)}, u32[]{:S(2)}) collective-permute-start(bf16[128,768]{1,0:T(8,128)(2,1)S(1)} %get-tuple-element.94), channel_id=1, source_target_pairs={{0,13},{1,12},{4,9},{5,8},{8,21},{9,20},{12,17},{13,16},{16,29},{1... | collective-permute-start | bytes 589832 | tf_op jit(solution)/shard_map/ppermute | solution.py:242
  110.4 3.3 %collective-permute-done.21 = bf16[128,768]{1,0:T(8,128)(2,1)S(1)} collective-permute-done((bf16[128,768]{1,0:T(8,128)(2,1)S(1)}, bf16[128,768]{1,0:T(8,128)(2,1)S(1)}, u32[]{:S(2)}, u32[]{:S(2)}) %collective-permute-start.21) | collective-permute-done | bytes 196640 | tf_op jit(solution)/shard_map/ppermute | solution.py:242
  117.0 14.6 %collective-permute-done.22 = bf16[128,768]{1,0:T(8,128)(2,1)S(1)} collective-permute-done((bf16[128,768]{1,0:T(8,128)(2,1)S(1)}, bf16[128,768]{1,0:T(8,128)(2,1)S(1)}, u32[]{:S(2)}, u32[]{:S(2)}) %collective-permute-start.22) | collective-permute-done | bytes 196640 | tf_op jit(solution)/shard_map/ppermute | solution.py:242
  131.6 4.4 %collective-permute-done.23 = bf16[128,768]{1,0:T(8,128)(2,1)S(1)} collective-permute-done((bf16[128,768]{1,0:T(8,128)(2,1)S(1)}, bf16[128,768]{1,0:T(8,128)(2,1)S(1)}, u32[]{:S(2)}, u32[]{:S(2)}) %collective-permute-start.23) | collective-permute-done | bytes 196640 | tf_op jit(solution)/shard_map/ppermute | solution.py:242
  135.9 3.6 %collective-permute-start.27 = (bf16[128,768]{1,0:T(8,128)(2,1)S(1)}, bf16[128,768]{1,0:T(8,128)(2,1)S(1)}, u32[]{:S(2)}, u32[]{:S(2)}) collective-permute-start(bf16[128,768]{1,0:T(8,128)(2,1)S(1)} %get-tuple-element.99), channel_id=1, source_target_pairs={{0,24},{1,25},{4,28},{5,29},{8,0},{9,1},{12,4},{13,5},{16,8},{17,9... | collective-permute-start | bytes 589832 | tf_op jit(solution)/shard_map/ppermute | solution.py:242
  139.5 7.0 %collective-permute-done.24 = bf16[128,768]{1,0:T(8,128)(2,1)S(1)} collective-permute-done((bf16[128,768]{1,0:T(8,128)(2,1)S(1)}, bf16[128,768]{1,0:T(8,128)(2,1)S(1)}, u32[]{:S(2)}, u32[]{:S(2)}) %collective-permute-start.24) | collective-permute-done | bytes 196640 | tf_op jit(solution)/shard_map/ppermute | solution.py:242
  146.5 4.3 %collective-permute-done.25 = bf16[128,768]{1,0:T(8,128)(2,1)S(1)} collective-permute-done((bf16[128,768]{1,0:T(8,128)(2,1)S(1)}, bf16[128,768]{1,0:T(8,128)(2,1)S(1)}, u32[]{:S(2)}, u32[]{:S(2)}) %collective-permute-start.25) | collective-permute-done | bytes 196640 | tf_op jit(solution)/shard_map/ppermute | solution.py:242
  150.8 4.3 %collective-permute-start.30 = (bf16[128,768]{1,0:T(8,128)(2,1)S(1)}, bf16[128,768]{1,0:T(8,128)(2,1)S(1)}, u32[]{:S(2)}, u32[]{:S(2)}) collective-permute-start(bf16[128,768]{1,0:T(8,128)(2,1)S(1)} %get-tuple-element.102), channel_id=1, source_target_pairs={{0,29},{1,28},{4,25},{5,24},{8,5},{9,4},{12,1},{13,0},{16,13},{17,... | collective-permute-start | bytes 589832 | tf_op jit(solution)/shard_map/ppermute | solution.py:242
  156.3 4.6 %collective-permute-done.26 = bf16[128,768]{1,0:T(8,128)(2,1)S(1)} collective-permute-done((bf16[128,768]{1,0:T(8,128)(2,1)S(1)}, bf16[128,768]{1,0:T(8,128)(2,1)S(1)}, u32[]{:S(2)}, u32[]{:S(2)}) %collective-permute-start.26) | collective-permute-done | bytes 196640 | tf_op jit(solution)/shard_map/ppermute | solution.py:242
  163.3 4.0 %collective-permute-done.30 = bf16[128,768]{1,0:T(8,128)(2,1)S(1)} collective-permute-done((bf16[128,768]{1,0:T(8,128)(2,1)S(1)}, bf16[128,768]{1,0:T(8,128)(2,1)S(1)}, u32[]{:S(2)}, u32[]{:S(2)}) %collective-permute-start.30) | collective-permute-done | bytes 196640 | tf_op jit(solution)/shard_map/ppermute | solution.py:242
  168.0 6.8 %fusion.21 = f32[768,2048]{1,0:T(8,128)S(1)} fusion(bf16[2048,768]{1,0:T(8,128)(2,1)S(1)} %constant_dynamic-update-slice_fusion, bf16[2048,2048]{1,0:T(8,128)(2,1)S(1)} %constant_dynamic-update-slice_fusion.16), kind=kOutput, calls=%fused_computation.79 | convolution fusion | flops 6442450944 | bytes 17825792 | tf_op jit(solution)/shard_map/dot_general | solution.py:331
  181.1 2.5 collective-permute-start.35
  189.0 2.6 collective-permute-start.37
  191.6 3.7 %collective-permute-start.39 = (bf16[128,768]{1,0:T(8,128)(2,1)S(1)}, bf16[128,768]{1,0:T(8,128)(2,1)S(1)}, u32[]{:S(2)}, u32[]{:S(2)}) collective-permute-start(bf16[128,768]{1,0:T(8,128)(2,1)S(1)} %fusion.12), channel_id=1, source_target_pairs={{0,17},{1,16},{4,21},{5,20},{8,25},{9,24},{12,29},{13,28},{16,1},{... | collective-permute-start | bytes 589832 | tf_op jit(solution)/shard_map/ppermute | solution.py:242
  196.9 4.2 %collective-permute-start.40 = (bf16[128,768]{1,0:T(8,128)(2,1)S(1)}, bf16[128,768]{1,0:T(8,128)(2,1)S(1)}, u32[]{:S(2)}, u32[]{:S(2)}) collective-permute-start(bf16[128,768]{1,0:T(8,128)(2,1)S(1)} %fusion.13), channel_id=1, source_target_pairs={{0,20},{1,21},{4,16},{5,17},{8,28},{9,29},{12,24},{13,25},{16,4},{... | collective-permute-start | bytes 589832 | tf_op jit(solution)/shard_map/ppermute | solution.py:242
  201.1 3.6 %collective-permute-start.41 = (bf16[128,768]{1,0:T(8,128)(2,1)S(1)}, bf16[128,768]{1,0:T(8,128)(2,1)S(1)}, u32[]{:S(2)}, u32[]{:S(2)}) collective-permute-start(bf16[128,768]{1,0:T(8,128)(2,1)S(1)} %fusion.14), channel_id=1, source_target_pairs={{0,21},{1,20},{4,17},{5,16},{8,29},{9,28},{12,25},{13,24},{16,5},{... | collective-permute-start | bytes 589832 | tf_op jit(solution)/shard_map/ppermute | solution.py:242
  204.7 17.1 %collective-permute-done.38.refs_13_ = bf16[128,768]{1,0:T(8,128)(2,1)S(1)} collective-permute-done((bf16[128,768]{1,0:T(8,128)(2,1)S(1)}, bf16[128,768]{1,0:T(8,128)(2,1)S(1)}, u32[]{:S(2)}, u32[]{:S(2)}) %collective-permute-start.38) | collective-permute-done | bytes 196640 | tf_op jit(solution)/shard_map/ppermute | solution.py:242
  221.8 4.2 %collective-permute-done.39.refs_14_ = bf16[128,768]{1,0:T(8,128)(2,1)S(1)} collective-permute-done((bf16[128,768]{1,0:T(8,128)(2,1)S(1)}, bf16[128,768]{1,0:T(8,128)(2,1)S(1)}, u32[]{:S(2)}, u32[]{:S(2)}) %collective-permute-start.39) | collective-permute-done | bytes 196640 | tf_op jit(solution)/shard_map/ppermute | solution.py:242
  226.0 4.2 %collective-permute-done.40.refs_15_ = bf16[128,768]{1,0:T(8,128)(2,1)S(1)} collective-permute-done((bf16[128,768]{1,0:T(8,128)(2,1)S(1)}, bf16[128,768]{1,0:T(8,128)(2,1)S(1)}, u32[]{:S(2)}, u32[]{:S(2)}) %collective-permute-start.40) | collective-permute-done | bytes 196640 | tf_op jit(solution)/shard_map/ppermute | solution.py:242
  230.2 8.3 %collective-permute-start.44 = (bf16[128,768]{1,0:T(8,128)(2,1)S(1)}, bf16[128,768]{1,0:T(8,128)(2,1)S(1)}, u32[]{:S(2)}, u32[]{:S(2)}) collective-permute-start(bf16[128,768]{1,0:T(8,128)(2,1)S(1)} %fusion.17), channel_id=1, source_target_pairs={{0,12},{1,13},{4,8},{5,9},{8,20},{9,21},{12,16},{13,17},{16,28},{1... | collective-permute-start | bytes 589832 | tf_op jit(solution)/shard_map/ppermute | solution.py:242
  238.5 2.6 collective-permute-start.45
  242.9 4.2 %collective-permute-done.44.refs_19_ = bf16[128,768]{1,0:T(8,128)(2,1)S(1)} collective-permute-done((bf16[128,768]{1,0:T(8,128)(2,1)S(1)}, bf16[128,768]{1,0:T(8,128)(2,1)S(1)}, u32[]{:S(2)}, u32[]{:S(2)}) %collective-permute-start.44) | collective-permute-done | bytes 196640 | tf_op jit(solution)/shard_map/ppermute | solution.py:242
  247.1 4.1 %collective-permute-done.45.refs_20_ = bf16[128,768]{1,0:T(8,128)(2,1)S(1)} collective-permute-done((bf16[128,768]{1,0:T(8,128)(2,1)S(1)}, bf16[128,768]{1,0:T(8,128)(2,1)S(1)}, u32[]{:S(2)}, u32[]{:S(2)}) %collective-permute-start.45) | collective-permute-done | bytes 196640 | tf_op jit(solution)/shard_map/ppermute | solution.py:242
  251.2 8.2 %collect.1 = (bf16[128,8,768]{2,1,0:T(8,128)(2,1)}, f32[128,8]{1,0:T(8,128)S(1)}) custom-call(s32[3]{0:T(128)S(1)} %pad_add_fusion.place.refs_0_, f32[1,256]{1,0:T(1,128)S(1)} %convert_element_type.121.refs_1_, s32[128,8]{1,0:T(8,128)S(1)} %copy.58.refs_2_, f32[128,8]{1,0:T(8,128)S(1)} %copy.59.refs_3_, bf16[128,8,768]{2,1,0:T(8,128)(2,1)} %refs_4_.3, ...), custom_call_target="tpu_custom_call" | custom-call | tf_op jit(solution)/shard_map/collect/pallas_call | solution.py:346
  260.1 7.8 %fusion.20 = (bf16[2,192,2048]{2,1,0:T(8,128)(2,1)}, f32[2,192,2048]{2,1,0:T(8,128)}, bf16[2,192,2048]{2,1,0:T(8,128)(2,1)}) fusion(bf16[2,192,2048]{2,1,0:T(8,128)(2,1)} %collective-permute-done.46, bf16[2,192,2048]{2,1,0:T(8,128)(2,1)} %param.17, f32[2,192,2048]{2,1,0:T(8,128)S(1)} %copy-done.1, bf16[2,192,2048]{2,1,0:T(8,128)(2,1)} %param.16, ...), kind=kLoop, calls=%fused_computation.42 | loop fusion | flops 16515072 | bytes 17301504 | tf_op jit(solution)/shard_map/convert_element_type | solution.py:369
  (140 shorter events, 73.6 us)
Async XLA Ops:
  0.6 15.1 %collective-permute-start.4 = (bf16[128,2048]{1,0:T(8,128)(2,1)}, bf16[128,2048]{1,0:T(8,128)(2,1)S(1)}, u32[]{:S(2)}, u32[]{:S(2)}) collective-permute-start(bf16[128,2048]{1,0:T(8,128)(2,1)} %param.9), channel_id=1, source_target_pairs={{0,8},{1,9},{4,12},{5,13},{8,16},{9,17},{12,20},{13,21},{16,24},{1... | collective-permute-start | bytes 1572872 | tf_op jit(solution)/shard_map/ppermute | solution.py:242
  2.3 15.0 %collective-permute-start.2 = (bf16[128,2048]{1,0:T(8,128)(2,1)}, bf16[128,2048]{1,0:T(8,128)(2,1)S(1)}, u32[]{:S(2)}, u32[]{:S(2)}) collective-permute-start(bf16[128,2048]{1,0:T(8,128)(2,1)} %param.9), channel_id=1, source_target_pairs={{0,4},{1,5},{4,0},{5,1},{8,12},{9,13},{12,8},{13,9},{16,20},{17,21... | collective-permute-start | bytes 1572872 | tf_op jit(solution)/shard_map/ppermute | solution.py:242
  3.8 37.2 %collective-permute-start.1 = (bf16[128,2048]{1,0:T(8,128)(2,1)}, bf16[128,2048]{1,0:T(8,128)(2,1)S(1)}, u32[]{:S(2)}, u32[]{:S(2)}) collective-permute-start(bf16[128,2048]{1,0:T(8,128)(2,1)} %param.9), channel_id=1, source_target_pairs={{0,1},{1,0},{4,5},{5,4},{8,9},{9,8},{12,13},{13,12},{16,17},{17,16... | collective-permute-start | bytes 1572872 | tf_op jit(solution)/shard_map/ppermute | solution.py:242
  3.8 39.1 %collective-permute-start.12 = (bf16[128,2048]{1,0:T(8,128)(2,1)}, bf16[128,2048]{1,0:T(8,128)(2,1)S(1)}, u32[]{:S(2)}, u32[]{:S(2)}) collective-permute-start(bf16[128,2048]{1,0:T(8,128)(2,1)} %param.9), channel_id=1, source_target_pairs={{0,24},{1,25},{4,28},{5,29},{8,0},{9,1},{12,4},{13,5},{16,8},{17,9... | collective-permute-start | bytes 1572872 | tf_op jit(solution)/shard_map/ppermute | solution.py:242
  15.7 28.7 %collective-permute-start.6 = (bf16[128,2048]{1,0:T(8,128)(2,1)S(1)}, bf16[128,2048]{1,0:T(8,128)(2,1)S(1)}, u32[]{:S(2)}, u32[]{:S(2)}) collective-permute-start(bf16[128,2048]{1,0:T(8,128)(2,1)S(1)} %collective-permute-done.4), channel_id=1, source_target_pairs={{0,4},{1,5},{4,0},{5,1},{8,12},{9,13},{12,8},{13,9},{16,20},{17,21... | collective-permute-start | bytes 1572872 | tf_op jit(solution)/shard_map/ppermute | solution.py:242
  17.2 27.7 %collective-permute-start.3 = (bf16[128,2048]{1,0:T(8,128)(2,1)S(1)}, bf16[128,2048]{1,0:T(8,128)(2,1)}, u32[]{:S(2)}, u32[]{:S(2)}) collective-permute-start(bf16[128,2048]{1,0:T(8,128)(2,1)S(1)} %collective-permute-done.2), channel_id=1, source_target_pairs={{0,1},{1,0},{4,5},{5,4},{8,9},{9,8},{12,13},{13,12},{16,17},{17,16... | collective-permute-start | bytes 1572872 | tf_op jit(solution)/shard_map/ppermute | solution.py:242
  29.3 23.6 %collective-permute-start.8 = (bf16[128,2048]{1,0:T(8,128)(2,1)S(1)}, bf16[128,2048]{1,0:T(8,128)(2,1)S(1)}, u32[]{:S(2)}, u32[]{:S(2)}) collective-permute-start(bf16[128,2048]{1,0:T(8,128)(2,1)S(1)} %collective-permute-done.4), channel_id=1, source_target_pairs={{0,8},{1,9},{4,12},{5,13},{8,16},{9,17},{12,20},{13,21},{16,24},{1... | collective-permute-start | bytes 1572872 | tf_op jit(solution)/shard_map/ppermute | solution.py:242
  42.9 36.6 %collective-permute-start = (bf16[2,192,2048]{2,1,0:T(8,128)(2,1)S(1)}, bf16[2,192,2048]{2,1,0:T(8,128)(2,1)S(1)}, u32[]{:S(2)}, u32[]{:S(2)}) collective-permute-start(bf16[2,192,2048]{2,1,0:T(8,128)(2,1)S(1)} %scale.1), channel_id=1, source_target_pairs={{0,2},{2,0},{1,3},{3,1},{4,6},{6,4},{5,7},{7,5},{8,10},{10,8},{9,1... | collective-permute-start | bytes 4718600 | tf_op jit(solution)/shard_map/ppermute | solution.py:275
  44.4 26.4 %collective-permute-start.14 = (bf16[128,2048]{1,0:T(8,128)(2,1)S(1)}, bf16[128,2048]{1,0:T(8,128)(2,1)S(1)}, u32[]{:S(2)}, u32[]{:S(2)}) collective-permute-start(bf16[128,2048]{1,0:T(8,128)(2,1)S(1)} %collective-permute-done.12), channel_id=1, source_target_pairs={{0,4},{1,5},{4,0},{5,1},{8,12},{9,13},{12,8},{13,9},{16,20},{17,21... | collective-permute-start | bytes 1572872 | tf_op jit(solution)/shard_map/ppermute | solution.py:242
  52.9 44.5 %collective-permute-start.13 = (bf16[128,2048]{1,0:T(8,128)(2,1)S(1)}, bf16[128,2048]{1,0:T(8,128)(2,1)S(1)}, u32[]{:S(2)}, u32[]{:S(2)}) collective-permute-start(bf16[128,2048]{1,0:T(8,128)(2,1)S(1)} %collective-permute-done.12), channel_id=1, source_target_pairs={{0,1},{1,0},{4,5},{5,4},{8,9},{9,8},{12,13},{13,12},{16,17},{17,16... | collective-permute-start | bytes 1572872 | tf_op jit(solution)/shard_map/ppermute | solution.py:242
  55.1 14.4 %collective-permute-start.10 = (bf16[128,2048]{1,0:T(8,128)(2,1)S(1)}, bf16[128,2048]{1,0:T(8,128)(2,1)S(1)}, u32[]{:S(2)}, u32[]{:S(2)}) collective-permute-start(bf16[128,2048]{1,0:T(8,128)(2,1)S(1)} %collective-permute-done.8), channel_id=1, source_target_pairs={{0,4},{1,5},{4,0},{5,1},{8,12},{9,13},{12,8},{13,9},{16,20},{17,21... | collective-permute-start | bytes 1572872 | tf_op jit(solution)/shard_map/ppermute | solution.py:242
  57.3 41.9 %collective-permute-start.16 = (bf16[128,768]{1,0:T(8,128)(2,1)S(1)}, bf16[128,768]{1,0:T(8,128)(2,1)S(1)}, u32[]{:S(2)}, u32[]{:S(2)}) collective-permute-start(bf16[128,768]{1,0:T(8,128)(2,1)S(1)} %get-tuple-element.88), channel_id=1, source_target_pairs={{0,1},{1,0},{4,5},{5,4},{8,9},{9,8},{12,13},{13,12},{16,17},{17,16... | collective-permute-start | bytes 589832 | tf_op jit(solution)/shard_map/ppermute | solution.py:242
  69.5 29.8 %collective-permute-start.17 = (bf16[128,768]{1,0:T(8,128)(2,1)S(1)}, bf16[128,768]{1,0:T(8,128)(2,1)S(1)}, u32[]{:S(2)}, u32[]{:S(2)}) collective-permute-start(bf16[128,768]{1,0:T(8,128)(2,1)S(1)} %get-tuple-element.89), channel_id=1, source_target_pairs={{0,4},{1,5},{4,0},{5,1},{8,12},{9,13},{12,8},{13,9},{16,20},{17,21... | collective-permute-start | bytes 589832 | tf_op jit(solution)/shard_map/ppermute | solution.py:242
  70.8 29.9 %collective-permute-start.18 = (bf16[128,768]{1,0:T(8,128)(2,1)S(1)}, bf16[128,768]{1,0:T(8,128)(2,1)S(1)}, u32[]{:S(2)}, u32[]{:S(2)}) collective-permute-start(bf16[128,768]{1,0:T(8,128)(2,1)S(1)} %get-tuple-element.90), channel_id=1, source_target_pairs={{0,5},{1,4},{4,1},{5,0},{8,13},{9,12},{12,9},{13,8},{16,21},{17,20... | collective-permute-start | bytes 589832 | tf_op jit(solution)/shard_map/ppermute | solution.py:242
  79.5 19.9 %collective-permute-start.15 = (bf16[128,2048]{1,0:T(8,128)(2,1)S(1)}, bf16[128,2048]{1,0:T(8,128)(2,1)S(1)}, u32[]{:S(2)}, u32[]{:S(2)}) collective-permute-start(bf16[128,2048]{1,0:T(8,128)(2,1)S(1)} %collective-permute-done.14), channel_id=1, source_target_pairs={{0,1},{1,0},{4,5},{5,4},{8,9},{9,8},{12,13},{13,12},{16,17},{17,16... | collective-permute-start | bytes 1572872 | tf_op jit(solution)/shard_map/ppermute | solution.py:242
  99.4 51.4 %collective-permute-start.11 = (bf16[128,2048]{1,0:T(8,128)(2,1)S(1)}, bf16[128,2048]{1,0:T(8,128)(2,1)S(1)}, u32[]{:S(2)}, u32[]{:S(2)}) collective-permute-start(bf16[128,2048]{1,0:T(8,128)(2,1)S(1)} %collective-permute-done.10), channel_id=1, source_target_pairs={{0,1},{1,0},{4,5},{5,4},{8,9},{9,8},{12,13},{13,12},{16,17},{17,16... | collective-permute-start | bytes 1572872 | tf_op jit(solution)/shard_map/ppermute | solution.py:242
  100.7 30.8 %collective-permute-start.22 = (bf16[128,768]{1,0:T(8,128)(2,1)S(1)}, bf16[128,768]{1,0:T(8,128)(2,1)S(1)}, u32[]{:S(2)}, u32[]{:S(2)}) collective-permute-start(bf16[128,768]{1,0:T(8,128)(2,1)S(1)} %get-tuple-element.94), channel_id=1, source_target_pairs={{0,13},{1,12},{4,9},{5,8},{8,21},{9,20},{12,17},{13,16},{16,29},{1... | collective-permute-start | bytes 589832 | tf_op jit(solution)/shard_map/ppermute | solution.py:242
  105.3 30.7 %collective-permute-start.23 = (bf16[128,768]{1,0:T(8,128)(2,1)S(1)}, bf16[128,768]{1,0:T(8,128)(2,1)S(1)}, u32[]{:S(2)}, u32[]{:S(2)}) collective-permute-start(bf16[128,768]{1,0:T(8,128)(2,1)S(1)} %get-tuple-element.95), channel_id=1, source_target_pairs={{0,16},{1,17},{4,20},{5,21},{8,24},{9,25},{12,28},{13,29},{16,0},{... | collective-permute-start | bytes 589832 | tf_op jit(solution)/shard_map/ppermute | solution.py:242
  108.7 37.8 %collective-permute-start.24 = (bf16[128,768]{1,0:T(8,128)(2,1)S(1)}, bf16[128,768]{1,0:T(8,128)(2,1)S(1)}, u32[]{:S(2)}, u32[]{:S(2)}) collective-permute-start(bf16[128,768]{1,0:T(8,128)(2,1)S(1)} %get-tuple-element.96), channel_id=1, source_target_pairs={{0,17},{1,16},{4,21},{5,20},{8,25},{9,24},{12,29},{13,28},{16,1},{... | collective-permute-start | bytes 589832 | tf_op jit(solution)/shard_map/ppermute | solution.py:242
  113.6 37.1 %collective-permute-start.25 = (bf16[128,768]{1,0:T(8,128)(2,1)S(1)}, bf16[128,768]{1,0:T(8,128)(2,1)S(1)}, u32[]{:S(2)}, u32[]{:S(2)}) collective-permute-start(bf16[128,768]{1,0:T(8,128)(2,1)S(1)} %get-tuple-element.97), channel_id=1, source_target_pairs={{0,20},{1,21},{4,16},{5,17},{8,28},{9,29},{12,24},{13,25},{16,4},{... | collective-permute-start | bytes 589832 | tf_op jit(solution)/shard_map/ppermute | solution.py:242
  131.6 29.3 %collective-permute-start.26 = (bf16[128,768]{1,0:T(8,128)(2,1)S(1)}, bf16[128,768]{1,0:T(8,128)(2,1)S(1)}, u32[]{:S(2)}, u32[]{:S(2)}) collective-permute-start(bf16[128,768]{1,0:T(8,128)(2,1)S(1)} %get-tuple-element.98), channel_id=1, source_target_pairs={{0,21},{1,20},{4,17},{5,16},{8,29},{9,28},{12,25},{13,24},{16,5},{... | collective-permute-start | bytes 589832 | tf_op jit(solution)/shard_map/ppermute | solution.py:242
  135.9 25.0 %collective-permute-start.27 = (bf16[128,768]{1,0:T(8,128)(2,1)S(1)}, bf16[128,768]{1,0:T(8,128)(2,1)S(1)}, u32[]{:S(2)}, u32[]{:S(2)}) collective-permute-start(bf16[128,768]{1,0:T(8,128)(2,1)S(1)} %get-tuple-element.99), channel_id=1, source_target_pairs={{0,24},{1,25},{4,28},{5,29},{8,0},{9,1},{12,4},{13,5},{16,8},{17,9... | collective-permute-start | bytes 589832 | tf_op jit(solution)/shard_map/ppermute | solution.py:242
  146.5 14.4 %collective-permute-start.28 = (bf16[128,768]{1,0:T(8,128)(2,1)S(1)}, bf16[128,768]{1,0:T(8,128)(2,1)S(1)}, u32[]{:S(2)}, u32[]{:S(2)}) collective-permute-start(bf16[128,768]{1,0:T(8,128)(2,1)S(1)} %get-tuple-element.100), channel_id=1, source_target_pairs={{0,25},{1,24},{4,29},{5,28},{8,1},{9,0},{12,5},{13,4},{16,9},{17,8... | collective-permute-start | bytes 589832 | tf_op jit(solution)/shard_map/ppermute | solution.py:242
  150.8 16.6 %collective-permute-start.30 = (bf16[128,768]{1,0:T(8,128)(2,1)S(1)}, bf16[128,768]{1,0:T(8,128)(2,1)S(1)}, u32[]{:S(2)}, u32[]{:S(2)}) collective-permute-start(bf16[128,768]{1,0:T(8,128)(2,1)S(1)} %get-tuple-element.102), channel_id=1, source_target_pairs={{0,29},{1,28},{4,25},{5,24},{8,5},{9,4},{12,1},{13,0},{16,13},{17,... | collective-permute-start | bytes 589832 | tf_op jit(solution)/shard_map/ppermute | solution.py:242
  176.4 83.7 %collective-permute-start.46 = (bf16[2,192,2048]{2,1,0:T(8,128)(2,1)}, bf16[2,192,2048]{2,1,0:T(8,128)(2,1)}, u32[]{:S(2)}, u32[]{:S(2)}) collective-permute-start(bf16[2,192,2048]{2,1,0:T(8,128)(2,1)} %fusion.2), channel_id=1, source_target_pairs={{0,2},{2,0},{1,3},{3,1},{4,6},{6,4},{5,7},{7,5},{8,10},{10,8},{9,1... | collective-permute-start | bytes 4718600 | tf_op jit(solution)/shard_map/ppermute | solution.py:336
  191.6 30.2 %collective-permute-start.38 = (bf16[128,768]{1,0:T(8,128)(2,1)S(1)}, bf16[128,768]{1,0:T(8,128)(2,1)S(1)}, u32[]{:S(2)}, u32[]{:S(2)}) collective-permute-start(bf16[128,768]{1,0:T(8,128)(2,1)S(1)} %fusion.11), channel_id=1, source_target_pairs={{0,16},{1,17},{4,20},{5,21},{8,24},{9,25},{12,28},{13,29},{16,0},{... | collective-permute-start | bytes 589832 | tf_op jit(solution)/shard_map/ppermute | solution.py:242
  191.6 34.4 %collective-permute-start.39 = (bf16[128,768]{1,0:T(8,128)(2,1)S(1)}, bf16[128,768]{1,0:T(8,128)(2,1)S(1)}, u32[]{:S(2)}, u32[]{:S(2)}) collective-permute-start(bf16[128,768]{1,0:T(8,128)(2,1)S(1)} %fusion.12), channel_id=1, source_target_pairs={{0,17},{1,16},{4,21},{5,20},{8,25},{9,24},{12,29},{13,28},{16,1},{... | collective-permute-start | bytes 589832 | tf_op jit(solution)/shard_map/ppermute | solution.py:242
  196.9 33.4 %collective-permute-start.40 = (bf16[128,768]{1,0:T(8,128)(2,1)S(1)}, bf16[128,768]{1,0:T(8,128)(2,1)S(1)}, u32[]{:S(2)}, u32[]{:S(2)}) collective-permute-start(bf16[128,768]{1,0:T(8,128)(2,1)S(1)} %fusion.13), channel_id=1, source_target_pairs={{0,20},{1,21},{4,16},{5,17},{8,28},{9,29},{12,24},{13,25},{16,4},{... | collective-permute-start | bytes 589832 | tf_op jit(solution)/shard_map/ppermute | solution.py:242
  201.1 37.5 %collective-permute-start.41 = (bf16[128,768]{1,0:T(8,128)(2,1)S(1)}, bf16[128,768]{1,0:T(8,128)(2,1)S(1)}, u32[]{:S(2)}, u32[]{:S(2)}) collective-permute-start(bf16[128,768]{1,0:T(8,128)(2,1)S(1)} %fusion.14), channel_id=1, source_target_pairs={{0,21},{1,20},{4,17},{5,16},{8,29},{9,28},{12,25},{13,24},{16,5},{... | collective-permute-start | bytes 589832 | tf_op jit(solution)/shard_map/ppermute | solution.py:242
  221.8 19.4 %collective-permute-start.42 = (bf16[128,768]{1,0:T(8,128)(2,1)S(1)}, bf16[128,768]{1,0:T(8,128)(2,1)S(1)}, u32[]{:S(2)}, u32[]{:S(2)}) collective-permute-start(bf16[128,768]{1,0:T(8,128)(2,1)S(1)} %fusion.15), channel_id=1, source_target_pairs={{0,8},{1,9},{4,12},{5,13},{8,16},{9,17},{12,20},{13,21},{16,24},{1... | collective-permute-start | bytes 589832 | tf_op jit(solution)/shard_map/ppermute | solution.py:242
  226.0 16.9 %collective-permute-start.43 = (bf16[128,768]{1,0:T(8,128)(2,1)S(1)}, bf16[128,768]{1,0:T(8,128)(2,1)S(1)}, u32[]{:S(2)}, u32[]{:S(2)}) collective-permute-start(bf16[128,768]{1,0:T(8,128)(2,1)S(1)} %fusion.16), channel_id=1, source_target_pairs={{0,9},{1,8},{4,13},{5,12},{8,17},{9,16},{12,21},{13,20},{16,25},{1... | collective-permute-start | bytes 589832 | tf_op jit(solution)/shard_map/ppermute | solution.py:242
  230.2 16.9 %collective-permute-start.44 = (bf16[128,768]{1,0:T(8,128)(2,1)S(1)}, bf16[128,768]{1,0:T(8,128)(2,1)S(1)}, u32[]{:S(2)}, u32[]{:S(2)}) collective-permute-start(bf16[128,768]{1,0:T(8,128)(2,1)S(1)} %fusion.17), channel_id=1, source_target_pairs={{0,12},{1,13},{4,8},{5,9},{8,20},{9,21},{12,16},{13,17},{16,28},{1... | collective-permute-start | bytes 589832 | tf_op jit(solution)/shard_map/ppermute | solution.py:242
  (20 other events, 409.4 us)

commit v2 on v1

--- a/solution.py
+++ b/solution.py
@@ -95,7 +95,7 @@
     return result
 
 
-def route_match(ids, column_keys):
+def route_match(ids, experts):
     tokens, top = ids.shape
     shape = (tokens, top, top)
     token = lax.broadcasted_iota(jnp.int32, shape, 0)
@@ -103,8 +103,9 @@
         jnp.int32, shape, 2
     )
     keys = jnp.where(diagonal, ids[:, None, :] * tokens + token, 0).astype(jnp.float32)
-    keys = jnp.sum(keys.reshape(tokens * top, top), axis=1, keepdims=True)
-    return jnp.where(keys == column_keys, 1.0, 0.0).astype(jnp.bfloat16)
+    keys = jnp.sum(keys.reshape(tokens * top, top), axis=1, keepdims=True).astype(jnp.int32)
+    columns = lax.broadcasted_iota(jnp.int32, (tokens * top, experts * tokens), 1)
+    return jnp.where(keys == columns, 1.0, 0.0).astype(jnp.bfloat16)
 
 
 def route_column(values):
@@ -126,11 +127,12 @@
     return jnp.sum(jnp.where(diagonal, spread, 0.0), axis=1)
 
 
-def spread_kernel(groups, here, parts, place, keys, ids, gate, hidden, *outs):
+def spread_kernel(here, parts, place, ids, gate, hidden, out):
     fsdp, replica = parts
     tokens, top, width = hidden.shape
+    groups = out.shape[1]
     unit = width // (fsdp * replica)
-    match = route_match(ids[...], keys[...])
+    match = route_match(ids[...], groups * here)
     values = hidden[...].astype(jnp.float32).reshape(tokens * top, width)
     weighted = (route_column(gate[...]) * values).astype(jnp.bfloat16)
 
@@ -138,61 +140,45 @@
         at = (f * replica + r) * unit
         return weighted[:, at : at + unit]
 
-    shares = [
-        pick(
+    for r in range(replica):
+        share = pick(
             place[1],
             [
                 jnp.concatenate([block((f + o) % fsdp, r) for o in range(fsdp)], axis=1)
                 for f in range(fsdp)
             ],
         )
-        for r in range(replica)
-    ]
-    for c in range(replica):
-        share = pick(place[2], [shares[(r + c) % replica] for r in range(replica)])
         rows = lax.dot_general(
             match, share, (((0,), (0,)), ((), ())), preferred_element_type=jnp.float32
         ).astype(jnp.bfloat16)
         for g in range(groups):
             for e in range(here):
                 at = (g * here + e) * tokens
-                outs[g * replica + c][:, e * fsdp * unit : (e + 1) * fsdp * unit] = rows[
-                    at : at + tokens
-                ]
-
-
-def collect_kernel(groups, here, parts, place, keys, ids, gate, hidden, *refs):
+                out[r, g, :, e * fsdp * unit : (e + 1) * fsdp * unit] = rows[at : at + tokens]
+
+
+def collect_kernel(here, parts, ids, gate, hidden, backs, hidden_grad, gate_grad):
     fsdp, replica = parts
-    backs, (hidden_grad, gate_grad) = refs[:-2], refs[-2:]
     tokens, top, width = hidden.shape
+    groups = backs.shape[1]
     unit = width // (fsdp * replica)
-    match = route_match(ids[...], keys[...])
-    found = []
-    for c in range(replica):
+    match = route_match(ids[...], groups * here)
+    shares = []
+    for r in range(replica):
         rows = jnp.concatenate(
             [
-                backs[g * replica + c][:, e * fsdp * unit : (e + 1) * fsdp * unit]
+                backs[r, g, :, e * fsdp * unit : (e + 1) * fsdp * unit]
                 for g in range(groups)
                 for e in range(here)
             ],
             axis=0,
         )
-        found.append(jnp.dot(match, rows, preferred_element_type=jnp.float32))
-    shares = [
-        pick(place[2], [found[(h - r) % replica] for r in range(replica)])
-        for h in range(replica)
-    ]
+        shares.append(jnp.dot(match, rows, preferred_element_type=jnp.float32))
     back = jnp.concatenate(
         [
-            pick(
-                place[1],
-                [
-                    shares[h][:, (f - m) % fsdp * unit : ((f - m) % fsdp + 1) * unit]
-                    for m in range(fsdp)
-                ],
-            )
+            shares[r][:, f * unit : (f + 1) * unit]
             for f in range(fsdp)
-            for h in range(replica)
+            for r in range(replica)
         ],
         axis=1,
     )
@@ -211,6 +197,49 @@
         out[0, :, at] = (values[0, :, at].astype(jnp.float32) * scales[:, b : b + 1]).astype(
             jnp.bfloat16
         )
+
+
+def back_kernel(parts, place, dy, *refs):
+    fsdp = parts[0]
+    weights, out, rows = refs[:fsdp], refs[-2], refs[-1]
+    here, unit, _ = weights[0].shape
+
+    @pl.when(pl.program_id(0) == 0)
+    def _():
+        for e in range(here):
+            for o in range(fsdp):
+                at = (e * fsdp + lax.rem(place[1] + o, fsdp)) * unit
+                rows[pl.ds(pl.multiple_of(at, unit), unit), :] = weights[o][e]
+
+    back = lax.dot_general(
+        dy[...], rows[...], (((1,), (1,)), ((), ())), preferred_element_type=jnp.float32
+    )
+    out[...] = back.astype(jnp.bfloat16).reshape(out.shape)
+
+
+def gradient_kernel(parts, place, *refs):
+    fsdp, replica = parts
+    hids, dys, outs, turned = (
+        refs[:replica],
+        refs[replica : 2 * replica],
+        refs[2 * replica : -1],
+        refs[-1],
+    )
+    here, unit, _ = outs[0].shape
+
+    @pl.when(pl.program_id(0) == 0)
+    def _():
+        for c in range(replica):
+            turned[c] = hids[c][...].reshape(turned.shape[2], turned.shape[1]).T
+
+    total = sum(
+        jnp.dot(turned[c], dys[c][...], preferred_element_type=jnp.float32)
+        for c in range(replica)
+    )
+    for e in range(here):
+        for o in range(fsdp):
+            at = (e * fsdp + o) * unit
+            outs[o][e] = total[at : at + unit].astype(outs[o].dtype)
 
 
 def dense_body(
@@ -226,20 +255,18 @@
     outer = groups // inner
     unit = width // (fsdp * replica)
     block = min(TOKEN_BLOCK, tokens)
-    offsets = [(s, j) for s in range(outer) for j in range(inner)]
+    lanes = here * fsdp * unit
 
     def moved(e, s, j):
         return (e // inner + s) % outer * inner + (e % inner + j) % inner
 
-    def send(x, s, j, c):
-        if (s, j, c) == (0, 0, 0):
-            return x
-        pairs = [
-            (e * replica + r, moved(e, s, j) * replica + (r + c) % replica)
-            for e in range(groups)
-            for r in range(replica)
-        ]
-        return lax.ppermute(x, ("expert", "replica"), pairs)
+    def send(x, s, j):
+        return lax.ppermute(x, "expert", [(e, moved(e, s, j)) for e in range(groups)])
+
+    def exchange(x):
+        x = x.reshape(replica * groups, tokens, lanes)
+        x = lax.all_to_all(x, ("replica", "expert"), split_axis=0, concat_axis=0, tiled=True)
+        return x.reshape(replica, groups, tokens, lanes)
 
     place = jnp.stack([me, mf, mr]).astype(jnp.int32)
     weight_part = pl.pallas_call(
@@ -258,116 +285,151 @@
         name="scale",
     )(place, weight_q, weight_exp)
 
+    token_specs = [
+        pl.BlockSpec((block, top), lambda i, p: (i, 0)),
+        pl.BlockSpec((block, top), lambda i, p: (i, 0)),
+        pl.BlockSpec((block, top, width), lambda i, p: (i, 0, 0)),
+    ]
+    row_spec = pl.BlockSpec((replica, groups, block, lanes), lambda i, p: (0, 0, i, 0))
+    spread = pl.pallas_call(
+        lambda *refs: spread_kernel(here, (fsdp, replica), *refs),
+        out_shape=jax.ShapeDtypeStruct((replica, groups, tokens, lanes), jnp.bfloat16),
+        grid_spec=pltpu.PrefetchScalarGridSpec(
+            num_scalar_prefetch=1,
+            grid=(tokens // block,),
+            in_specs=token_specs,
+            out_specs=row_spec,
+        ),
+        compiler_params=pltpu.CompilerParams(vmem_limit_bytes=VMEM),
+        name="spread",
+    )(place, expert_ids, gate_probs, hidden_saved)
+
     ups = outer // 2
     line = {0: out_grad}
     for s in range(1, ups + 1):
-        line[s] = send(line[s - 1], 1, 0, 0)
+        line[s] = send(line[s - 1], 1, 0)
+        if s == 1:
+            line[1], spread, weight_part = lax.optimization_barrier((line[1], spread, weight_part))
     for s in range(outer - 1, ups, -1):
-        line[s] = send(line[(s + 1) % outer], outer - 1, 0, 0)
-    dy = {}
-    for s in range(outer):
-        for j in range(inner):
-            held = send(line[s], 0, j, 0)
-            for c in range(replica):
-                dy[s, j, c] = send(held, 0, 0, c)
-
+        line[s] = send(line[(s + 1) % outer], outer - 1, 0)
+    hid = exchange(spread)
     weight_parts = [weight_part] + [
         lax.ppermute(weight_part, "fsdp", [(f, (f - o) % fsdp) for f in range(fsdp)])
         for o in range(1, fsdp)
     ]
-    weight_rows = jnp.stack(weight_parts, axis=1).reshape(here * fsdp * unit, model_width)
-
-    def keys(sign):
-        group = [
-            ((me // inner + sign * s) % outer) * inner + (me % inner + sign * j) % inner
-            for s, j in offsets
+    line[ups], weight_parts = lax.optimization_barrier((line[ups], weight_parts))
+    own = jnp.zeros((groups, tokens, model_width), jnp.bfloat16)
+    for s in range(outer):
+        for j in range(inner):
+            piece = send(line[s], 0, j) if j else line[s]
+            source = lax.rem(lax.div(me, inner) + (outer - s), outer) * inner + lax.rem(
+                me + (inner - j), inner
+            )
+            own = lax.dynamic_update_index_in_dim(own, piece, source, 0)
+    own = own.reshape(groups * tokens, model_width)
+    dy = [own] + [
+        lax.ppermute(own, "replica", [(r, (r - c) % replica) for r in range(replica)])
+        for c in range(1, replica)
+    ]
+
+    together = 2 if groups % 2 == 0 else 1
+    part_spec = pl.BlockSpec((here, unit, model_width), lambda i, p: (0, 0, 0))
+    back = []
+    for c in range(replica):
+        back = [
+            pl.pallas_call(
+                lambda *refs: back_kernel((fsdp, replica), *refs),
+                out_shape=jax.ShapeDtypeStruct((replica, groups, tokens, lanes), jnp.bfloat16),
+                grid_spec=pltpu.PrefetchScalarGridSpec(
+                    num_scalar_prefetch=1,
+                    grid=(groups // together,),
+                    in_specs=[
+                        pl.BlockSpec((together * tokens, model_width), lambda i, p: (i, 0))
+                    ]
+                    + [part_spec] * fsdp
+                    + [pl.BlockSpec(memory_space=pl.ANY)] * len(back),
+                    out_specs=pl.BlockSpec(
+                        (1, together, tokens, lanes),
+                        lambda i, p, c=c: (lax.rem(p[2] + c, replica), i, 0, 0),
+                    ),
+                    scratch_shapes=[pltpu.VMEM((lanes, model_width), jnp.bfloat16)],
+                ),
+                compiler_params=pltpu.CompilerParams(vmem_limit_bytes=VMEM),
+                cost_estimate=pl.CostEstimate(
+                    flops=2 * groups * tokens * lanes * model_width,
+                    bytes_accessed=2 * groups * tokens * (lanes + model_width),
+                    transcendentals=0,
+                ),
+                input_output_aliases={2 + fsdp: 0} if back else {},
+                name="back",
+            )(place, dy[c], *weight_parts, *back)
         ]
-        expert = (jnp.stack(group)[:, None] * here + jnp.arange(here)[None, :]).reshape(-1)
-        return (
-            (expert[:, None] * block + jnp.arange(block)[None, :])
-            .reshape(1, -1)
-            .astype(jnp.float32)
-        )
-
-    column_keys = keys(1)
-    pieces = len(offsets) * replica
-    piece = (here * fsdp * unit,)
-    row_spec = pl.BlockSpec((block,) + piece, lambda i, p: (i, 0))
-    token_specs = [
-        pl.BlockSpec(column_keys.shape, lambda i, p: (0, 0)),
-        pl.BlockSpec((block, top), lambda i, p: (i, 0)),
-        pl.BlockSpec((block, top), lambda i, p: (i, 0)),
-        pl.BlockSpec((block, top, width), lambda i, p: (i, 0, 0)),
-    ]
-    spread = pl.pallas_call(
-        lambda *refs: spread_kernel(groups, here, (fsdp, replica), *refs),
-        out_shape=[jax.ShapeDtypeStruct((tokens,) + piece, jnp.bfloat16)] * pieces,
+    back, hid = lax.optimization_barrier((back[0], hid))
+    returned = exchange(back)
+
+    columns = min(512, model_width)
+    grad_spec = pl.BlockSpec((here, unit, columns), lambda i, p: (0, 0, i))
+    grads = pl.pallas_call(
+        lambda *refs: gradient_kernel((fsdp, replica), *refs),
+        out_shape=[
+            jax.ShapeDtypeStruct((here, unit, model_width), jnp.bfloat16 if o else jnp.float32)
+            for o in range(fsdp)
+        ],
         grid_spec=pltpu.PrefetchScalarGridSpec(
             num_scalar_prefetch=1,
-            grid=(tokens // block,),
-            in_specs=token_specs,
-            out_specs=[row_spec] * pieces,
+            grid=(model_width // columns,),
+            in_specs=[
+                pl.BlockSpec(
+                    (1, groups, tokens, lanes),
+                    lambda i, p, c=c: (lax.rem(p[2] + c, replica), 0, 0, 0),
+                )
+                for c in range(replica)
+            ]
+            + [pl.BlockSpec((groups * tokens, columns), lambda i, p: (0, i))] * replica,
+            out_specs=[grad_spec] * fsdp,
+            scratch_shapes=[pltpu.VMEM((replica, lanes, groups * tokens), jnp.bfloat16)],
         ),
         compiler_params=pltpu.CompilerParams(vmem_limit_bytes=VMEM),
-        name="spread",
-    )(place, column_keys, expert_ids, gate_probs, hidden_saved)
-    spread, _ = lax.optimization_barrier((spread, line[ups]))
-    order = [(s, j, c) for s, j in offsets for c in range(replica)]
-    hid = {o: send(x, *o) for o, x in zip(order, spread)}
-
-    back = [
-        lax.dot_general(
-            dy[o], weight_rows, (((1,), (1,)), ((), ())), preferred_element_type=jnp.float32
-        ).astype(jnp.bfloat16)
-        for o in order
-    ]
-    back, hid = lax.optimization_barrier((back, hid))
-    returned = [
-        send(x, (-s) % outer, (-j) % inner, (-c) % replica) for (s, j, c), x in zip(order, back)
-    ]
-
-    hid_all = jnp.concatenate([hid[o] for o in order], axis=0)
-    dy_all = jnp.concatenate([dy[o] for o in order], axis=0)
-    partial_grad = lax.dot_general(
-        hid_all, dy_all, (((0,), (0,)), ((), ())), preferred_element_type=jnp.float32
-    ).reshape(here, fsdp, unit, model_width)
-    gradient = partial_grad[:, 0]
+        cost_estimate=pl.CostEstimate(
+            flops=2 * replica * groups * tokens * lanes * model_width,
+            bytes_accessed=2 * replica * groups * tokens * (lanes + model_width),
+            transcendentals=0,
+        ),
+        name="gradient",
+    )(place, *[hid] * replica, *dy)
+    gradient = grads[0]
     for o in range(1, fsdp):
         gradient = gradient + lax.ppermute(
-            partial_grad[:, o].astype(jnp.bfloat16),
-            "fsdp",
-            [(f, (f + o) % fsdp) for f in range(fsdp)],
+            grads[o], "fsdp", [(f, (f + o) % fsdp) for f in range(fsdp)]
         ).astype(jnp.float32)
     first = 0.9 * moment1.astype(jnp.float32) + 0.1 * gradient
     second = 0.95 * moment2.astype(jnp.float32) + 0.05 * gradient * gradient
     update = first / (1.0 - 0.9**20) / (jnp.sqrt(second / (1.0 - 0.95**20)) + 1e-08) + 0.1 * master
     master_new = master - 0.001 * update
 
+    new = (master_new, first.astype(jnp.bfloat16), second.astype(jnp.bfloat16))
+    returned, new = lax.optimization_barrier((returned, new))
     hidden_grad, gate_grad = pl.pallas_call(
-        lambda *refs: collect_kernel(groups, here, (fsdp, replica), *refs),
+        lambda *refs: collect_kernel(here, (fsdp, replica), *refs),
         out_shape=[
             jax.ShapeDtypeStruct(hidden_saved.shape, jnp.bfloat16),
             jax.ShapeDtypeStruct(gate_probs.shape, jnp.float32),
         ],
-        grid_spec=pltpu.PrefetchScalarGridSpec(
-            num_scalar_prefetch=1,
-            grid=(tokens // block,),
-            in_specs=token_specs + [row_spec] * pieces,
-            out_specs=[
-                pl.BlockSpec((block, top, width), lambda i, p: (i, 0, 0)),
-                pl.BlockSpec((block, top), lambda i, p: (i, 0)),
-            ],
-        ),
+        grid=(tokens // block,),
+        in_specs=[
+            pl.BlockSpec((block, top), lambda i: (i, 0)),
+            pl.BlockSpec((block, top), lambda i: (i, 0)),
+            pl.BlockSpec((block, top, width), lambda i: (i, 0, 0)),
+            pl.BlockSpec((replica, groups, block, lanes), lambda i: (0, 0, i, 0)),
+        ],
+        out_specs=[
+            pl.BlockSpec((block, top, width), lambda i: (i, 0, 0)),
+            pl.BlockSpec((block, top), lambda i: (i, 0)),
+        ],
         compiler_params=pltpu.CompilerParams(vmem_limit_bytes=VMEM),
         name="collect",
-    )(place, column_keys, expert_ids, gate_probs, hidden_saved, *returned)
-    return (
-        hidden_grad,
-        gate_grad,
-        master_new,
-        first.astype(jnp.bfloat16),
-        second.astype(jnp.bfloat16),
-    )
+    )(expert_ids, gate_probs, hidden_saved, returned)
+    return (hidden_grad, gate_grad) + new
 
 
 def body(*args):

time: 271 us -> 200 us (0.74)
  starting transfers between devices: 74.7 us -> 27.1 us
  matrix products: 26.7 us -> 0 us
  Pallas kernels: 17.6 us -> 43.9 us
  waiting for transfers between devices: 122 us -> 97.9 us
  local copies, waits for them, and re-layouts: 17.9 us -> 22 us
    ppermute x46 -> x9, starting transfers between devices: 73.2 us -> 9.58 us  [the longest x7 9.04 us: send(): lax.ppermute(x, 'expert', [(e, moved(e, s, j)) for e in range(groups)])]
    ppermute x46 -> x9, waiting for transfers between devices: 113 us -> 76.7 us  [the longest x7 40.8 us: send(): lax.ppermute(x, 'expert', [(e, moved(e, s, j)) for e in range(groups)])]
    dot_general x17 -> x0, matrix products: 26.7 us -> none  [the longest x16 19.9 us: dense_body(): lax.dot_general(dy[o], weight_rows, (((1,), (1,)), ((), ())), preferred_e...]
    pallas_call x2 -> x5, Pallas kernels: 14.8 us -> 41.1 us  [the longest x2 15.6 us: dense_body(): pl.pallas_call(lambda *refs: back_kernel((fsdp, replica), *refs), out_sha...]
    all_to_all x0 -> x2, starting transfers between devices: none -> 16 us  [exchange(): lax.all_to_all(x, ('replica', 'expert'), split_axis=0, concat_axis=0, til...]
    all_to_all x0 -> x2, waiting for transfers between devices: none -> 15.3 us  [exchange(): lax.all_to_all(x, ('replica', 'expert'), split_axis=0, concat_axis=0, til...]
    dynamic_update_slice x0 -> x8, local copies, waits for them, and re-layouts: none -> 13 us  [dense_body(): own = lax.dynamic_update_index_in_dim(own, piece, source, 0)]
    unnamed x44 -> x22, local copies, waits for them, and re-layouts: 15.6 us -> 6.42 us
  transfers between devices with their start and end apart: 47 -> 12, of which waited for: 23 -> 6; matrix products, arithmetic and copies ran while one was open for 13% -> 13% of each run, Pallas kernels for 7% -> 18%
where the time goes in v2:
time: 200 us; the launch traced here: 199 us
  waiting for transfers between devices  97.9 us (49%)
  Pallas kernels  43.9 us (22%)
  starting transfers between devices  27.1 us (14%)
  local copies, waits for them, and re-layouts  22 us (11%)
  other arithmetic  6.97 us (3%)
    ppermute x7, waiting for transfers between devices, send(): lax.ppermute(x, 'expert', [(e, moved(e, s, j)) for e in range(groups)])  40.8 us
    ppermute x1, waiting for transfers between devices, dense_body(): lax.ppermute(grads[o], 'fsdp', [(f, (f + o) % fsdp) for f in range(fsdp)])  35.9 us
    all_to_all x2, starting transfers between devices, exchange(): lax.all_to_all(x, ('replica', 'expert'), split_axis=0, concat_axis=0, til...  16 us
    pallas_call x2, Pallas kernels, dense_body(): pl.pallas_call(lambda *refs: back_kernel((fsdp, replica), *refs), out_sha...  15.6 us
    all_to_all x2, waiting for transfers between devices, exchange(): lax.all_to_all(x, ('replica', 'expert'), split_axis=0, concat_axis=0, til...  15.3 us
    dynamic_update_slice x8, local copies, waits for them, and re-layouts, dense_body(): own = lax.dynamic_update_index_in_dim(own, piece, source, 0)  13 us
    pallas_call x1, Pallas kernels, dense_body(): pl.pallas_call(lambda *refs: gradient_kernel((fsdp, replica), *refs), out...  12.4 us
    ppermute x7, starting transfers between devices, send(): lax.ppermute(x, 'expert', [(e, moved(e, s, j)) for e in range(groups)])  9.04 us
  transfers between devices with their start and end apart: 12, of which 6 were waited for; matrix products, arithmetic and copies ran while one was open for 13% of the time, Pallas kernels for 18%

profile of v2, /device:TPU:8, one launch (start us, length us, event | category | flops | bytes accessed | tf_op | source)
XLA Modules:
  0.0 198.6 jit_solution(13499094359407983508)
XLA Ops:
  0.6 1.6 collective-permute-start.1
  2.3 1.4 copy.19.refs_2_.refs_1_
  3.7 1.4 copy.18.refs_1_.refs_0_
  5.1 1.0 copy.17.exponents
  6.2 2.7 %scale.1.refs_2_ = bf16[2,192,2048]{2,1,0:T(8,128)(2,1)S(1)} custom-call(s32[3]{0:T(128)S(1)} %pad_add_fusion.refs_0_.place, bf16[2,384,2048]{2,1,0:T(8,128)(2,1)} %values.1, s32[2,384,16]{2,1,0:T(8,128)S(1)} %copy.17.exponents), custom_call_target="tpu_custom_call" | custom-call | tf_op jit(solution)/shard_map/scale/pallas_call | solution.py:272
  8.9 5.7 %spread.1 = bf16[2,8,128,768]{3,2,1,0:T(8,128)(2,1)} custom-call(s32[3]{0:T(128)S(1)} %pad_add_fusion.refs_0_.place, s32[128,8]{1,0:T(8,128)S(1)} %copy-done.3, f32[128,8]{1,0:T(8,128)S(1)} %copy-done.1, bf16[128,8,768]{2,1,0:T(8,128)(2,1)S(1)} %copy-done), custom_call_target="tpu_custom_call" | custom-call | tf_op jit(solution)/shard_map/spread/pallas_call | solution.py:294
  14.7 1.5 collective-permute-start.4
  16.2 2.3 %collective-permute-start.6 = (bf16[128,2048]{1,0:T(8,128)(2,1)}, bf16[128,2048]{1,0:T(8,128)(2,1)}, u32[]{:S(2)}, u32[]{:S(2)}) collective-permute-start(bf16[128,2048]{1,0:T(8,128)(2,1)} %param.9), channel_id=1, source_target_pairs={{0,24},{4,28},{8,0},{12,4},{16,8},{20,12},{24,16},{28,20},{1,25},{... | collective-permute-start | bytes 1572872 | tf_op jit(solution)/shard_map/ppermute | solution.py:264
  18.5 1.5 collective-permute-start
  20.0 2.5 %broadcast_in_dim.28 = bf16[8,128,2048]{2,1,0:T(8,128)(2,1)} broadcast(bf16[]{:T(256)} %constant.59.clone.1), dimensions={} | broadcast | bytes 4194306 | tf_op jit(solution)/shard_map/broadcast_in_dim | solution.py:321
  22.5 1.9 bitcast_dynamic-update-slice_fusion.7
  24.9 7.8 %all-to-all-start = ((bf16[16,128,768]{2,1,0:T(8,128)(2,1)}), bf16[16,128,768]{2,1,0:T(8,128)(2,1)}, u32[]{:S(2)}, u32[]{:S(2)}) async-start(bf16[16,128,768]{2,1,0:T(8,128)(2,1)} %bitcast.24), calls=%async_computation | async-start | bytes 6291456 | tf_op jit(solution)/shard_map/all_to_all | solution.py:268
  32.7 1.5 collective-permute-start.7
  34.3 1.9 bitcast_dynamic-update-slice_fusion.6
  36.2 1.9 bitcast_dynamic-update-slice_fusion.5
  38.1 6.6 %collective-permute-done.3 = bf16[128,2048]{1,0:T(8,128)(2,1)} collective-permute-done((bf16[128,2048]{1,0:T(8,128)(2,1)}, bf16[128,2048]{1,0:T(8,128)(2,1)}, u32[]{:S(2)}, u32[]{:S(2)}) %collective-permute-start.3) | collective-permute-done | bytes 524320 | tf_op jit(solution)/shard_map/ppermute | solution.py:264
  44.6 5.9 %collective-permute-done.4.refs_3_ = bf16[2,192,2048]{2,1,0:T(8,128)(2,1)} collective-permute-done((bf16[2,192,2048]{2,1,0:T(8,128)(2,1)S(1)}, bf16[2,192,2048]{2,1,0:T(8,128)(2,1)}, u32[]{:S(2)}, u32[]{:S(2)}) %collective-permute-start.4) | collective-permute-done | bytes 1572896 | tf_op jit(solution)/shard_map/ppermute | solution.py:317
  50.6 1.5 collective-permute-start.5
  52.1 1.9 bitcast_dynamic-update-slice_fusion.4
  54.0 1.9 bitcast_dynamic-update-slice_fusion.3
  55.9 34.1 %collective-permute-done.5 = bf16[128,2048]{1,0:T(8,128)(2,1)S(1)} collective-permute-done((bf16[128,2048]{1,0:T(8,128)(2,1)}, bf16[128,2048]{1,0:T(8,128)(2,1)S(1)}, u32[]{:S(2)}, u32[]{:S(2)}) %collective-permute-start.5) | collective-permute-done | bytes 524320 | tf_op jit(solution)/shard_map/ppermute | solution.py:264
  90.0 0.9 bitcast_dynamic-update-slice_fusion.2
  90.9 1.9 bitcast_dynamic-update-slice_fusion.1
  93.6 7.8 %back.2.refs_4_ = bf16[2,8,128,768]{3,2,1,0:T(8,128)(2,1)} custom-call(s32[3]{0:T(128)S(1)} %pad_add_fusion.refs_0_.place, bf16[1024,2048]{1,0:T(8,128)(2,1)} %bitcast.11.refs_1_.refs_3_, bf16[2,192,2048]{2,1,0:T(8,128)(2,1)S(1)} %scale.1.refs_2_, bf16[2,192,2048]{2,1,0:T(8,128)(2,1)} %collective-permute-done.4.refs_3_), custom_call_target="tpu_custom_call" | custom-call | flops 3221225472 | bytes 5767168 | tf_op jit(solution)/shard_map/back/pallas_call | solution.py:340
  101.4 1.9 copy-done.5
  103.3 7.8 %back.3 = bf16[2,8,128,768]{3,2,1,0:T(8,128)(2,1)} custom-call(s32[3]{0:T(128)S(1)} %pad_add_fusion.refs_0_.place, bf16[1024,2048]{1,0:T(8,128)(2,1)} %copy-done.5, bf16[2,192,2048]{2,1,0:T(8,128)(2,1)S(1)} %scale.1.refs_2_, bf16[2,192,2048]{2,1,0:T(8,128)(2,1)} %collective-permute-done.4.refs_3_, ...), custom_call_target="tpu_custom_call", output_to_operand_aliasing={{}: (4, {})} | custom-call | flops 3221225472 | bytes 5767168 | tf_op jit(solution)/shard_map/back/pallas_call | solution.py:340
  111.1 8.2 %all-to-all-start.1 = ((bf16[16,128,768]{2,1,0:T(8,128)(2,1)}), bf16[16,128,768]{2,1,0:T(8,128)(2,1)}, u32[]{:S(2)}, u32[]{:S(2)}) async-start(bf16[16,128,768]{2,1,0:T(8,128)(2,1)} %bitcast.25), calls=%async_computation.1 | async-start | bytes 6291456 | tf_op jit(solution)/shard_map/all_to_all | solution.py:268
  119.3 12.4 %gradient.1 = (f32[2,192,2048]{2,1,0:T(8,128)}, bf16[2,192,2048]{2,1,0:T(8,128)(2,1)S(1)}) custom-call(s32[3]{0:T(128)S(1)} %pad_add_fusion.refs_0_.place, bf16[2,8,128,768]{3,2,1,0:T(8,128)(2,1)} %bitcast.13.refs_1_.refs_2_, bf16[2,8,128,768]{3,2,1,0:T(8,128)(2,1)} %bitcast.13.refs_1_.refs_2_, bf16[1024,2048]{1,0:T(8,128)(2,1)} %bitcast.11.refs_1_.refs_3_, ...), custom_call_target="tpu_custom_call" | custom-call | flops 6442450944 | bytes 11534336 | tf_op jit(solution)/shard_map/gradient/pallas_call | solution.py:372
  132.3 35.9 %collective-permute-done.9 = bf16[2,192,2048]{2,1,0:T(8,128)(2,1)S(1)} collective-permute-done((bf16[2,192,2048]{2,1,0:T(8,128)(2,1)S(1)}, bf16[2,192,2048]{2,1,0:T(8,128)(2,1)S(1)}, u32[]{:S(2)}, u32[]{:S(2)}) %collective-permute-start.9) | collective-permute-done | bytes 1572896 | tf_op jit(solution)/shard_map/ppermute | solution.py:402
  168.3 6.9 %fusion.2 = (bf16[2,192,2048]{2,1,0:T(8,128)(2,1)}, f32[2,192,2048]{2,1,0:T(8,128)}, bf16[2,192,2048]{2,1,0:T(8,128)(2,1)}) fusion(f32[2,192,2048]{2,1,0:T(8,128)} %get-tuple-element.29, bf16[2,192,2048]{2,1,0:T(8,128)(2,1)S(1)} %collective-permute-done.9, bf16[2,192,2048]{2,1,0:T(8,128)(2,1)S(1)} %copy-done.7, f32[2,192,2048]{2,1,0:T(8,128)S(1)} %copy-done.6, ...), kind=kLoop, calls=%fused_computation.6 | loop fusion | flops 16515072 | bytes 17301504 | tf_op jit(solution)/shard_map/convert_element_type | solution.py:410
  175.2 15.3 %all-to-all-done.1 = bf16[16,128,768]{2,1,0:T(8,128)(2,1)} async-done(((bf16[16,128,768]{2,1,0:T(8,128)(2,1)}), bf16[16,128,768]{2,1,0:T(8,128)(2,1)}, u32[]{:S(2)}, u32[]{:S(2)}) %all-to-all-start.1) | async-done | bytes 3145760 | tf_op jit(solution)/shard_map/all_to_all | solution.py:268
  190.5 7.4 %collect.1 = (bf16[128,8,768]{2,1,0:T(8,128)(2,1)}, f32[128,8]{1,0:T(8,128)S(1)}) custom-call(s32[128,8]{1,0:T(8,128)S(1)} %copy-done.4, f32[128,8]{1,0:T(8,128)S(1)} %copy-done.2, bf16[128,8,768]{2,1,0:T(8,128)(2,1)S(1)} %copy-done, bf16[2,8,128,768]{3,2,1,0:T(8,128)(2,1)} %bitcast.15.refs_3_), custom_call_target="tpu_custom_call" | custom-call | tf_op jit(solution)/shard_map/collect/pallas_call | solution.py:412
  (31 shorter events, 2.8 us)
Async XLA Ops:
  0.6 8.3 %copy-start = (bf16[128,8,768]{2,1,0:T(8,128)(2,1)S(1)}, bf16[128,8,768]{2,1,0:T(8,128)(2,1)}, u32[]{:S(2)}) copy-start(bf16[128,8,768]{2,1,0:T(8,128)(2,1)} %refs_2_.2) | copy-start | bytes 4718596
  0.6 14.0 %collective-permute-start.1 = (bf16[128,2048]{1,0:T(8,128)(2,1)}, bf16[128,2048]{1,0:T(8,128)(2,1)}, u32[]{:S(2)}, u32[]{:S(2)}) collective-permute-start(bf16[128,2048]{1,0:T(8,128)(2,1)} %param.9), channel_id=1, source_target_pairs={{0,8},{4,12},{8,16},{12,20},{16,24},{20,28},{24,0},{28,4},{1,9},{5... | collective-permute-start | bytes 1572872 | tf_op jit(solution)/shard_map/ppermute | solution.py:264
  6.1 2.8 %copy-start.1 = (f32[128,8]{1,0:T(8,128)S(1)}, f32[128,8]{1,0:T(8,128)}, u32[]{:S(2)}) copy-start(f32[128,8]{1,0:T(8,128)} %copy.19.refs_2_.refs_1_) | copy-start | bytes 12292
  6.1 2.8 %copy-start.3 = (s32[128,8]{1,0:T(8,128)S(1)}, s32[128,8]{1,0:T(8,128)}, u32[]{:S(2)}) copy-start(s32[128,8]{1,0:T(8,128)} %copy.18.refs_1_.refs_0_) | copy-start | bytes 12292
  14.7 35.9 %collective-permute-start.4 = (bf16[2,192,2048]{2,1,0:T(8,128)(2,1)S(1)}, bf16[2,192,2048]{2,1,0:T(8,128)(2,1)}, u32[]{:S(2)}, u32[]{:S(2)}) collective-permute-start(bf16[2,192,2048]{2,1,0:T(8,128)(2,1)S(1)} %scale.1.refs_2_), channel_id=1, source_target_pairs={{0,2},{2,0},{1,3},{3,1},{4,6},{6,4},{5,7},{7,5},{8,10},{10,8},{9,1... | collective-permute-start | bytes 4718600 | tf_op jit(solution)/shard_map/ppermute | solution.py:317
  16.2 16.6 %collective-permute-start.6 = (bf16[128,2048]{1,0:T(8,128)(2,1)}, bf16[128,2048]{1,0:T(8,128)(2,1)}, u32[]{:S(2)}, u32[]{:S(2)}) collective-permute-start(bf16[128,2048]{1,0:T(8,128)(2,1)} %param.9), channel_id=1, source_target_pairs={{0,24},{4,28},{8,0},{12,4},{16,8},{20,12},{24,16},{28,20},{1,25},{... | collective-permute-start | bytes 1572872 | tf_op jit(solution)/shard_map/ppermute | solution.py:264
  18.5 15.8 %collective-permute-start = (bf16[128,2048]{1,0:T(8,128)(2,1)}, bf16[128,2048]{1,0:T(8,128)(2,1)}, u32[]{:S(2)}, u32[]{:S(2)}) collective-permute-start(bf16[128,2048]{1,0:T(8,128)(2,1)} %param.9), channel_id=1, source_target_pairs={{0,4},{4,0},{8,12},{12,8},{16,20},{20,16},{24,28},{28,24},{1,5},{5... | collective-permute-start | bytes 1572872 | tf_op jit(solution)/shard_map/ppermute | solution.py:264
  24.4 20.2 %collective-permute-start.3 = (bf16[128,2048]{1,0:T(8,128)(2,1)}, bf16[128,2048]{1,0:T(8,128)(2,1)}, u32[]{:S(2)}, u32[]{:S(2)}) collective-permute-start(bf16[128,2048]{1,0:T(8,128)(2,1)} %collective-permute-done.1), channel_id=1, source_target_pairs={{0,8},{4,12},{8,16},{12,20},{16,24},{20,28},{24,0},{28,4},{1,9},{5... | collective-permute-start | bytes 1572872 | tf_op jit(solution)/shard_map/ppermute | solution.py:264
  24.4 27.7 %collective-permute-start.2 = (bf16[128,2048]{1,0:T(8,128)(2,1)}, bf16[128,2048]{1,0:T(8,128)(2,1)}, u32[]{:S(2)}, u32[]{:S(2)}) collective-permute-start(bf16[128,2048]{1,0:T(8,128)(2,1)} %collective-permute-done.1), channel_id=1, source_target_pairs={{0,4},{4,0},{8,12},{12,8},{16,20},{20,16},{24,28},{28,24},{1,5},{5... | collective-permute-start | bytes 1572872 | tf_op jit(solution)/shard_map/ppermute | solution.py:264
  24.9 86.2 %all-to-all-start = ((bf16[16,128,768]{2,1,0:T(8,128)(2,1)}), bf16[16,128,768]{2,1,0:T(8,128)(2,1)}, u32[]{:S(2)}, u32[]{:S(2)}) async-start(bf16[16,128,768]{2,1,0:T(8,128)(2,1)} %bitcast.24), calls=%async_computation | async-start | bytes 6291456 | tf_op jit(solution)/shard_map/all_to_all | solution.py:268
  32.7 60.0 %collective-permute-start.7 = (bf16[128,2048]{1,0:T(8,128)(2,1)}, bf16[128,2048]{1,0:T(8,128)(2,1)S(1)}, u32[]{:S(2)}, u32[]{:S(2)}) collective-permute-start(bf16[128,2048]{1,0:T(8,128)(2,1)} %collective-permute-done.6), channel_id=1, source_target_pairs={{0,4},{4,0},{8,12},{12,8},{16,20},{20,16},{24,28},{28,24},{1,5},{5... | collective-permute-start | bytes 1572872 | tf_op jit(solution)/shard_map/ppermute | solution.py:264
  50.6 39.4 %collective-permute-start.5 = (bf16[128,2048]{1,0:T(8,128)(2,1)}, bf16[128,2048]{1,0:T(8,128)(2,1)S(1)}, u32[]{:S(2)}, u32[]{:S(2)}) collective-permute-start(bf16[128,2048]{1,0:T(8,128)(2,1)} %collective-permute-done.3), channel_id=1, source_target_pairs={{0,4},{4,0},{8,12},{12,8},{16,20},{20,16},{24,28},{28,24},{1,5},{5... | collective-permute-start | bytes 1572872 | tf_op jit(solution)/shard_map/ppermute | solution.py:264
  93.6 7.8 %collective-permute-start.8 = (bf16[1024,2048]{1,0:T(8,128)(2,1)}, bf16[1024,2048]{1,0:T(8,128)(2,1)S(1)}, u32[]{:S(2)}, u32[]{:S(2)}) collective-permute-start(bf16[1024,2048]{1,0:T(8,128)(2,1)} %bitcast.11.refs_1_.refs_3_), channel_id=1, source_target_pairs={{0,1},{1,0},{2,3},{3,2},{4,5},{5,4},{6,7},{7,6},{8,9},{9,8},{10,11... | collective-permute-start | bytes 12582920 | tf_op jit(solution)/shard_map/ppermute | solution.py:331
  101.4 1.9 copy-start.5
  111.1 79.4 %all-to-all-start.1 = ((bf16[16,128,768]{2,1,0:T(8,128)(2,1)}), bf16[16,128,768]{2,1,0:T(8,128)(2,1)}, u32[]{:S(2)}, u32[]{:S(2)}) async-start(bf16[16,128,768]{2,1,0:T(8,128)(2,1)} %bitcast.25), calls=%async_computation.1 | async-start | bytes 6291456 | tf_op jit(solution)/shard_map/all_to_all | solution.py:268
  119.3 48.9 %copy-start.6 = (f32[2,192,2048]{2,1,0:T(8,128)S(1)}, f32[2,192,2048]{2,1,0:T(8,128)}, u32[]{:S(2)}) copy-start(f32[2,192,2048]{2,1,0:T(8,128)} %param.15) | copy-start | bytes 9437188
  119.3 48.9 %copy-start.7 = (bf16[2,192,2048]{2,1,0:T(8,128)(2,1)S(1)}, bf16[2,192,2048]{2,1,0:T(8,128)(2,1)}, u32[]{:S(2)}) copy-start(bf16[2,192,2048]{2,1,0:T(8,128)(2,1)} %param.17) | copy-start | bytes 4718596
  119.3 48.9 %copy-start.8 = (bf16[2,192,2048]{2,1,0:T(8,128)(2,1)S(1)}, bf16[2,192,2048]{2,1,0:T(8,128)(2,1)}, u32[]{:S(2)}) copy-start(bf16[2,192,2048]{2,1,0:T(8,128)(2,1)} %param.16) | copy-start | bytes 4718596
  131.8 36.4 %collective-permute-start.9 = (bf16[2,192,2048]{2,1,0:T(8,128)(2,1)S(1)}, bf16[2,192,2048]{2,1,0:T(8,128)(2,1)S(1)}, u32[]{:S(2)}, u32[]{:S(2)}) collective-permute-start(bf16[2,192,2048]{2,1,0:T(8,128)(2,1)S(1)} %get-tuple-element.30), channel_id=1, source_target_pairs={{0,2},{2,0},{1,3},{3,1},{4,6},{6,4},{5,7},{7,5},{8,10},{10,8},{9,1... | collective-permute-start | bytes 4718600 | tf_op jit(solution)/shard_map/ppermute | solution.py:402
  168.2 22.2 %copy-start.2 = (f32[128,8]{1,0:T(8,128)S(1)}, f32[128,8]{1,0:T(8,128)}, u32[]{:S(2)}) copy-start(f32[128,8]{1,0:T(8,128)} %copy.19.refs_2_.refs_1_) | copy-start | bytes 12292
  168.2 22.2 %copy-start.4 = (s32[128,8]{1,0:T(8,128)S(1)}, s32[128,8]{1,0:T(8,128)}, u32[]{:S(2)}) copy-start(s32[128,8]{1,0:T(8,128)} %copy.18.refs_1_.refs_0_) | copy-start | bytes 12292

commit v3 on v2

--- a/solution.py
+++ b/solution.py
@@ -86,6 +86,7 @@
 
 VMEM = 100 * 2**20 // 2
 TOKEN_BLOCK = 16
+PARTS = 4
 
 
 def pick(index, options):
@@ -95,106 +96,128 @@
     return result
 
 
-def route_match(ids, experts):
-    tokens, top = ids.shape
-    shape = (tokens, top, top)
-    token = lax.broadcasted_iota(jnp.int32, shape, 0)
-    diagonal = lax.broadcasted_iota(jnp.int32, shape, 1) == lax.broadcasted_iota(
-        jnp.int32, shape, 2
-    )
-    keys = jnp.where(diagonal, ids[:, None, :] * tokens + token, 0).astype(jnp.float32)
-    keys = jnp.sum(keys.reshape(tokens * top, top), axis=1, keepdims=True).astype(jnp.int32)
-    columns = lax.broadcasted_iota(jnp.int32, (tokens * top, experts * tokens), 1)
-    return jnp.where(keys == columns, 1.0, 0.0).astype(jnp.bfloat16)
+def diagonal(shape):
+    return lax.broadcasted_iota(jnp.int32, shape, 1) == lax.broadcasted_iota(jnp.int32, shape, 2)
 
 
 def route_column(values):
     tokens, top = values.shape
     shape = (tokens, top, top)
-    diagonal = lax.broadcasted_iota(jnp.int32, shape, 1) == lax.broadcasted_iota(
-        jnp.int32, shape, 2
-    )
-    spread = jnp.where(diagonal, jnp.broadcast_to(values[:, None, :], shape), 0.0)
+    spread = jnp.where(diagonal(shape), jnp.broadcast_to(values[:, None, :], shape), 0.0)
     return jnp.sum(spread.reshape(tokens * top, top), axis=1, keepdims=True)
 
 
 def route_square(column, tokens, top):
     shape = (tokens, top, top)
-    diagonal = lax.broadcasted_iota(jnp.int32, shape, 1) == lax.broadcasted_iota(
-        jnp.int32, shape, 2
-    )
     spread = jnp.broadcast_to(column, (tokens * top, top)).reshape(shape)
-    return jnp.sum(jnp.where(diagonal, spread, 0.0), axis=1)
-
-
-def spread_kernel(here, parts, place, ids, gate, hidden, out):
+    return jnp.sum(jnp.where(diagonal(shape), spread, 0.0), axis=1)
+
+
+def route_match(ids, experts):
+    tokens, top = ids.shape
+    token = lax.broadcasted_iota(jnp.int32, (tokens, top), 0).astype(jnp.float32)
+    keys = route_column(ids * tokens + token).astype(jnp.int32)
+    columns = lax.broadcasted_iota(jnp.int32, (tokens * top, experts * tokens), 1)
+    return jnp.where(keys == columns, 1.0, 0.0).astype(jnp.bfloat16)
+
+
+def turn_routes(ids, gate, turned):
+    @pl.when(pl.program_id(0) == 0)
+    def _():
+        turned[0] = ids[...].astype(jnp.float32).T
+        turned[1] = gate[...].T
+
+
+def rows_of_part(step, part, tokens):
+    start = pl.program_id(0) * step + part * tokens
+    return pl.ds(pl.multiple_of(start, tokens), tokens)
+
+
+def spread_kernel(here, parts, place, ids, gate, hidden, out, turned):
     fsdp, replica = parts
-    tokens, top, width = hidden.shape
+    step, top, width = hidden.shape
+    tokens = min(TOKEN_BLOCK, step)
     groups = out.shape[1]
     unit = width // (fsdp * replica)
-    match = route_match(ids[...], groups * here)
-    values = hidden[...].astype(jnp.float32).reshape(tokens * top, width)
-    weighted = (route_column(gate[...]) * values).astype(jnp.bfloat16)
-
-    def block(f, r):
-        at = (f * replica + r) * unit
-        return weighted[:, at : at + unit]
-
-    for r in range(replica):
-        share = pick(
-            place[1],
-            [
-                jnp.concatenate([block((f + o) % fsdp, r) for o in range(fsdp)], axis=1)
+    turn_routes(ids, gate, turned)
+    for part in range(step // tokens):
+        inside = slice(part * tokens, (part + 1) * tokens)
+        at = rows_of_part(step, part, tokens)
+        match = route_match(turned[0, at], groups * here)
+        values = hidden[inside].astype(jnp.float32).reshape(tokens * top, width)
+        weighted = (route_column(turned[1, at]) * values).astype(jnp.bfloat16)
+        for r in range(replica):
+            blocks = [
+                weighted[:, (f * replica + r) * unit : (f * replica + r + 1) * unit]
                 for f in range(fsdp)
-            ],
-        )
-        rows = lax.dot_general(
-            match, share, (((0,), (0,)), ((), ())), preferred_element_type=jnp.float32
-        ).astype(jnp.bfloat16)
-        for g in range(groups):
-            for e in range(here):
-                at = (g * here + e) * tokens
-                out[r, g, :, e * fsdp * unit : (e + 1) * fsdp * unit] = rows[at : at + tokens]
-
-
-def collect_kernel(here, parts, ids, gate, hidden, backs, hidden_grad, gate_grad):
+            ]
+            share = pick(
+                place[1],
+                [jnp.concatenate(blocks[f:] + blocks[:f], axis=1) for f in range(fsdp)],
+            )
+            rows = lax.dot_general(
+                match, share, (((0,), (0,)), ((), ())), preferred_element_type=jnp.float32
+            ).astype(jnp.bfloat16)
+            for g in range(groups):
+                for e in range(here):
+                    row = (g * here + e) * tokens
+                    out[r, g, inside, e * fsdp * unit : (e + 1) * fsdp * unit] = rows[
+                        row : row + tokens
+                    ]
+
+
+def collect_kernel(
+    here, parts, ids, gate, hidden, backs, hidden_grad, gate_grad, turned, gate_turned
+):
     fsdp, replica = parts
-    tokens, top, width = hidden.shape
+    step, top, width = hidden.shape
+    tokens = min(TOKEN_BLOCK, step)
     groups = backs.shape[1]
     unit = width // (fsdp * replica)
-    match = route_match(ids[...], groups * here)
-    shares = []
-    for r in range(replica):
-        rows = jnp.concatenate(
+    turn_routes(ids, gate, turned)
+    for part in range(step // tokens):
+        inside = slice(part * tokens, (part + 1) * tokens)
+        at = rows_of_part(step, part, tokens)
+        match = route_match(turned[0, at], groups * here)
+        shares = []
+        for r in range(replica):
+            rows = jnp.concatenate(
+                [
+                    backs[r, g, inside, e * fsdp * unit : (e + 1) * fsdp * unit]
+                    for g in range(groups)
+                    for e in range(here)
+                ],
+                axis=0,
+            )
+            shares.append(jnp.dot(match, rows, preferred_element_type=jnp.float32))
+        back = jnp.concatenate(
             [
-                backs[r, g, :, e * fsdp * unit : (e + 1) * fsdp * unit]
-                for g in range(groups)
-                for e in range(here)
+                shares[r][:, f * unit : (f + 1) * unit]
+                for f in range(fsdp)
+                for r in range(replica)
             ],
-            axis=0,
+            axis=1,
         )
-        shares.append(jnp.dot(match, rows, preferred_element_type=jnp.float32))
-    back = jnp.concatenate(
-        [
-            shares[r][:, f * unit : (f + 1) * unit]
-            for f in range(fsdp)
-            for r in range(replica)
-        ],
-        axis=1,
-    )
-    values = hidden[...].astype(jnp.float32).reshape(tokens * top, width)
-    scaled = route_column(gate[...]) * back
-    hidden_grad[...] = scaled.reshape(tokens, top, width).astype(jnp.bfloat16)
-    gate_grad[...] = route_square(jnp.sum(values * back, axis=1, keepdims=True), tokens, top)
-
-
-def scale_kernel(place, values, exponents, out):
-    blocks = exponents.shape[2]
-    width = values.shape[2] // blocks
-    scales = jnp.exp2(exponents[0].astype(jnp.float32))
+        values = hidden[inside].astype(jnp.float32).reshape(tokens * top, width)
+        scaled = route_column(turned[1, at]) * back
+        hidden_grad[inside] = scaled.reshape(tokens, top, width).astype(jnp.bfloat16)
+        column = jnp.sum(values * back, axis=1, keepdims=True)
+        gate_turned[at] = route_square(column, tokens, top)
+
+    @pl.when(pl.program_id(0) == pl.num_programs(0) - 1)
+    def _():
+        gate_grad[...] = gate_turned[...].T
+
+
+def scale_kernel(place, values, exponents, out, scales):
+    _, unit, model_width = values.shape
+    blocks = exponents.shape[1]
+    width = model_width // blocks
+    scales[...] = jnp.exp2(exponents[0].astype(jnp.float32)).T
+    rows = scales[pl.ds(pl.multiple_of(place[2] * unit, unit), unit), :]
     for b in range(blocks):
         at = slice(b * width, (b + 1) * width)
-        out[0, :, at] = (values[0, :, at].astype(jnp.float32) * scales[:, b : b + 1]).astype(
+        out[0, :, at] = (values[0, :, at].astype(jnp.float32) * rows[:, b : b + 1]).astype(
             jnp.bfloat16
         )
 
@@ -254,7 +277,7 @@
     inner = 2 if groups % 2 == 0 else 1
     outer = groups // inner
     unit = width // (fsdp * replica)
-    block = min(TOKEN_BLOCK, tokens)
+    block = min(TOKEN_BLOCK * PARTS, tokens)
     lanes = here * fsdp * unit
 
     def moved(e, s, j):
@@ -277,19 +300,21 @@
             grid=(here,),
             in_specs=[
                 pl.BlockSpec((1, unit, model_width), lambda e, p: (e, p[2], 0)),
-                pl.BlockSpec((1, unit, weight_exp.shape[2]), lambda e, p: (e, p[2], 0)),
+                pl.BlockSpec((1, weight_exp.shape[2], rows_here), lambda e, p: (e, 0, 0)),
             ],
             out_specs=pl.BlockSpec((1, unit, model_width), lambda e, p: (e, 0, 0)),
+            scratch_shapes=[pltpu.VMEM((rows_here, weight_exp.shape[2]), jnp.float32)],
         ),
         compiler_params=pltpu.CompilerParams(vmem_limit_bytes=VMEM),
         name="scale",
-    )(place, weight_q, weight_exp)
+    )(place, weight_q, weight_exp.swapaxes(1, 2))
 
     token_specs = [
-        pl.BlockSpec((block, top), lambda i, p: (i, 0)),
-        pl.BlockSpec((block, top), lambda i, p: (i, 0)),
+        pl.BlockSpec((top, tokens), lambda i, p: (0, 0)),
+        pl.BlockSpec((top, tokens), lambda i, p: (0, 0)),
         pl.BlockSpec((block, top, width), lambda i, p: (i, 0, 0)),
     ]
+    turned = pltpu.VMEM((2, tokens, top), jnp.float32)
     row_spec = pl.BlockSpec((replica, groups, block, lanes), lambda i, p: (0, 0, i, 0))
     spread = pl.pallas_call(
         lambda *refs: spread_kernel(here, (fsdp, replica), *refs),
@@ -299,40 +324,50 @@
             grid=(tokens // block,),
             in_specs=token_specs,
             out_specs=row_spec,
+            scratch_shapes=[turned],
         ),
         compiler_params=pltpu.CompilerParams(vmem_limit_bytes=VMEM),
         name="spread",
-    )(place, expert_ids, gate_probs, hidden_saved)
+    )(place, expert_ids.T, gate_probs.T, hidden_saved)
 
     ups = outer // 2
     line = {0: out_grad}
-    for s in range(1, ups + 1):
+    pair = {}
+    if outer > 1:
+        line[1] = send(out_grad, 1, 0)
+    if outer > 2:
+        line[outer - 1] = send(out_grad, outer - 1, 0)
+    if inner > 1:
+        pair[0] = send(out_grad, 0, 1)
+    line, pair, spread = lax.optimization_barrier((line, pair, spread))
+    hid = exchange(spread)
+    for s in range(2, ups + 1):
         line[s] = send(line[s - 1], 1, 0)
-        if s == 1:
-            line[1], spread, weight_part = lax.optimization_barrier((line[1], spread, weight_part))
-    for s in range(outer - 1, ups, -1):
-        line[s] = send(line[(s + 1) % outer], outer - 1, 0)
-    hid = exchange(spread)
+    for s in range(outer - 2, ups, -1):
+        line[s] = send(line[s + 1], outer - 1, 0)
     weight_parts = [weight_part] + [
         lax.ppermute(weight_part, "fsdp", [(f, (f - o) % fsdp) for f in range(fsdp)])
         for o in range(1, fsdp)
     ]
-    line[ups], weight_parts = lax.optimization_barrier((line[ups], weight_parts))
     own = jnp.zeros((groups, tokens, model_width), jnp.bfloat16)
     for s in range(outer):
         for j in range(inner):
-            piece = send(line[s], 0, j) if j else line[s]
+            piece = line[s]
+            if j:
+                piece = pair[s] if s in pair else send(line[s], 0, j)
             source = lax.rem(lax.div(me, inner) + (outer - s), outer) * inner + lax.rem(
                 me + (inner - j), inner
             )
             own = lax.dynamic_update_index_in_dim(own, piece, source, 0)
-    own = own.reshape(groups * tokens, model_width)
+    own, weight_parts = lax.optimization_barrier(
+        (own.reshape(groups * tokens, model_width), weight_parts)
+    )
     dy = [own] + [
         lax.ppermute(own, "replica", [(r, (r - c) % replica) for r in range(replica)])
         for c in range(1, replica)
     ]
 
-    together = 2 if groups % 2 == 0 else 1
+    together = max(g for g in (1, 2, 4) if groups % g == 0)
     part_spec = pl.BlockSpec((here, unit, model_width), lambda i, p: (0, 0, 0))
     back = []
     for c in range(replica):
@@ -413,23 +448,24 @@
         lambda *refs: collect_kernel(here, (fsdp, replica), *refs),
         out_shape=[
             jax.ShapeDtypeStruct(hidden_saved.shape, jnp.bfloat16),
-            jax.ShapeDtypeStruct(gate_probs.shape, jnp.float32),
+            jax.ShapeDtypeStruct((top, tokens), jnp.float32),
         ],
         grid=(tokens // block,),
         in_specs=[
-            pl.BlockSpec((block, top), lambda i: (i, 0)),
-            pl.BlockSpec((block, top), lambda i: (i, 0)),
+            pl.BlockSpec((top, tokens), lambda i: (0, 0)),
+            pl.BlockSpec((top, tokens), lambda i: (0, 0)),
             pl.BlockSpec((block, top, width), lambda i: (i, 0, 0)),
             pl.BlockSpec((replica, groups, block, lanes), lambda i: (0, 0, i, 0)),
         ],
         out_specs=[
             pl.BlockSpec((block, top, width), lambda i: (i, 0, 0)),
-            pl.BlockSpec((block, top), lambda i: (i, 0)),
+            pl.BlockSpec((top, tokens), lambda i: (0, 0)),
         ],
+        scratch_shapes=[turned, pltpu.VMEM((tokens, top), jnp.float32)],
         compiler_params=pltpu.CompilerParams(vmem_limit_bytes=VMEM),
         name="collect",
-    )(expert_ids, gate_probs, hidden_saved, returned)
-    return (hidden_grad, gate_grad) + new
+    )(expert_ids.T, gate_probs.T, hidden_saved, returned)
+    return (hidden_grad, gate_grad.T) + new
 
 
 def body(*args):

time: 200 us -> 194 us (0.970)
  waiting for transfers between devices: 97.9 us -> 111 us
  local copies, waits for them, and re-layouts: 22 us -> 10.8 us
  Pallas kernels: 43.9 us -> 39.1 us
  starting transfers between devices: 27.1 us -> 24.6 us
    ppermute x7, waiting for transfers between devices: 40.8 us -> 59.2 us  [send(): lax.ppermute(x, 'expert', [(e, moved(e, s, j)) for e in range(groups)])]
    dynamic_update_slice x8, local copies, waits for them, and re-layouts: 13 us -> 5.58 us  [dense_body(): own = lax.dynamic_update_index_in_dim(own, piece, source, 0)]
    ppermute x1, waiting for transfers between devices: 5.92 us -> 0.01 us  [dense_body(): lax.ppermute(weight_part, 'fsdp', [(f, (f - o) % fsdp) for f in range(fsd...]
    all_to_all x2, starting transfers between devices: 16 us -> 13.3 us  [exchange(): lax.all_to_all(x, ('replica', 'expert'), split_axis=0, concat_axis=0, til...]
    pallas_call x1, Pallas kernels: 7.44 us -> 4.83 us  [dense_body(): pl.pallas_call(lambda *refs: collect_kernel(here, (fsdp, replica), *refs)...]
    broadcast_in_dim x1, local copies, waits for them, and re-layouts: 2.53 us -> 0.51 us  [dense_body(): own = jnp.zeros((groups, tokens, model_width), jnp.bfloat16)]
    unnamed x22 -> x20, local copies, waits for them, and re-layouts: 6.42 us -> 4.7 us
  transfers between devices with their start and end apart: 12 -> 12, of which waited for: 6 -> 7; matrix products, arithmetic and copies ran while one was open for 13% -> 7% of each run, Pallas kernels for 18% -> 18%
where the time goes in v3:
time: 194 us; the launch traced here: 193 us
  waiting for transfers between devices  111 us (57%)
  Pallas kernels  39.1 us (20%)
  starting transfers between devices  24.6 us (13%)
  local copies, waits for them, and re-layouts  10.8 us (6%)
  other arithmetic  6.94 us (4%)
    ppermute x7, waiting for transfers between devices, send(): lax.ppermute(x, 'expert', [(e, moved(e, s, j)) for e in range(groups)])  59.2 us
    ppermute x1, waiting for transfers between devices, dense_body(): lax.ppermute(grads[o], 'fsdp', [(f, (f + o) % fsdp) for f in range(fsdp)])  35 us
    all_to_all x2, waiting for transfers between devices, exchange(): lax.all_to_all(x, ('replica', 'expert'), split_axis=0, concat_axis=0, til...  16.8 us
    pallas_call x2, Pallas kernels, dense_body(): pl.pallas_call(lambda *refs: back_kernel((fsdp, replica), *refs), out_sha...  14.8 us
    all_to_all x2, starting transfers between devices, exchange(): lax.all_to_all(x, ('replica', 'expert'), split_axis=0, concat_axis=0, til...  13.3 us
    pallas_call x1, Pallas kernels, dense_body(): pl.pallas_call(lambda *refs: gradient_kernel((fsdp, replica), *refs), out...  12.4 us
    ppermute x7, starting transfers between devices, send(): lax.ppermute(x, 'expert', [(e, moved(e, s, j)) for e in range(groups)])  8.17 us
    convert_element_type x1, other arithmetic, dense_body(): new = (master_new, first.astype(jnp.bfloat16), second.astype(jnp.bfloat16))  6.86 us
  transfers between devices with their start and end apart: 12, of which 7 were waited for; matrix products, arithmetic and copies ran while one was open for 7% of the time, Pallas kernels for 18%

profile of v3, /device:TPU:8, one launch (start us, length us, event | category | flops | bytes accessed | tf_op | source)
XLA Modules:
  0.0 193.3 jit_solution(17468550271397128101)
XLA Ops:
  0.7 2.0 %collective-permute-start = (bf16[128,2048]{1,0:T(8,128)(2,1)}, bf16[128,2048]{1,0:T(8,128)(2,1)}, u32[]{:S(2)}, u32[]{:S(2)}) collective-permute-start(bf16[128,2048]{1,0:T(8,128)(2,1)} %param.9), channel_id=1, source_target_pairs={{0,8},{4,12},{8,16},{12,20},{16,24},{20,28},{24,0},{28,4},{1,9},{5... | collective-permute-start | bytes 1572872 | tf_op jit(solution)/shard_map/ppermute | solution.py:287
  2.7 1.5 collective-permute-start.2
  4.3 0.8 copy-done.1
  5.1 3.1 %scale.1.refs_2_ = bf16[2,192,2048]{2,1,0:T(8,128)(2,1)S(1)} custom-call(s32[3]{0:T(128)S(1)} %pad_add_fusion.refs_0_.place, bf16[2,384,2048]{2,1,0:T(8,128)(2,1)} %values.1, s32[2,16,384]{2,1,0:T(8,128)S(1)} %bitcast.28), custom_call_target="tpu_custom_call" | custom-call | tf_op jit(solution)/shard_map/scale/pallas_call | solution.py:295
  8.2 1.6 collective-permute-start.7
  9.8 3.9 %spread.1 = bf16[2,8,128,768]{3,2,1,0:T(8,128)(2,1)} custom-call(s32[3]{0:T(128)S(1)} %pad_add_fusion.refs_0_.place, s32[8,128]{1,0:T(8,128)S(1)} %bitcast.29, f32[8,128]{1,0:T(8,128)S(1)} %bitcast.31, bf16[128,8,768]{2,1,0:T(8,128)(2,1)S(1)} %copy-done), custom_call_target="tpu_custom_call" | custom-call | tf_op jit(solution)/shard_map/spread/pallas_call | solution.py:319
  13.7 1.1 collective-permute-done.1
  14.8 13.2 %collective-permute-done = bf16[128,2048]{1,0:T(8,128)(2,1)} collective-permute-done((bf16[128,2048]{1,0:T(8,128)(2,1)}, bf16[128,2048]{1,0:T(8,128)(2,1)}, u32[]{:S(2)}, u32[]{:S(2)}) %collective-permute-start) | collective-permute-done | bytes 524320 | tf_op jit(solution)/shard_map/ppermute | solution.py:287
  28.0 1.5 collective-permute-start.3
  29.5 6.3 %all-to-all-start = ((bf16[16,128,768]{2,1,0:T(8,128)(2,1)}), bf16[16,128,768]{2,1,0:T(8,128)(2,1)}, u32[]{:S(2)}, u32[]{:S(2)}) async-start(bf16[16,128,768]{2,1,0:T(8,128)(2,1)} %bitcast.33), calls=%async_computation | async-start | bytes 6291456 | tf_op jit(solution)/shard_map/all_to_all | solution.py:291
  35.8 1.5 collective-permute-start.6
  37.3 0.5 broadcast_in_dim.28
  37.9 1.1 bitcast_dynamic-update-slice_fusion.6
  39.0 1.1 bitcast_dynamic-update-slice_fusion.5
  40.1 7.0 %collective-permute-done.4 = bf16[128,2048]{1,0:T(8,128)(2,1)} collective-permute-done((bf16[128,2048]{1,0:T(8,128)(2,1)}, bf16[128,2048]{1,0:T(8,128)(2,1)}, u32[]{:S(2)}, u32[]{:S(2)}) %collective-permute-start.4) | collective-permute-done | bytes 524320 | tf_op jit(solution)/shard_map/ppermute | solution.py:287
  47.1 1.5 collective-permute-start.5
  48.6 1.1 bitcast_dynamic-update-slice_fusion.4
  49.7 1.1 bitcast_dynamic-update-slice_fusion.3
  50.8 38.0 %collective-permute-done.5 = bf16[128,2048]{1,0:T(8,128)(2,1)S(1)} collective-permute-done((bf16[128,2048]{1,0:T(8,128)(2,1)}, bf16[128,2048]{1,0:T(8,128)(2,1)S(1)}, u32[]{:S(2)}, u32[]{:S(2)}) %collective-permute-start.5) | collective-permute-done | bytes 524320 | tf_op jit(solution)/shard_map/ppermute | solution.py:287
  88.8 1.1 bitcast_dynamic-update-slice_fusion.1
  90.1 1.8 copy-done.4
  91.9 7.4 %back.2.refs_4_ = bf16[2,8,128,768]{3,2,1,0:T(8,128)(2,1)} custom-call(s32[3]{0:T(128)S(1)} %pad_add_fusion.refs_0_.place, bf16[1024,2048]{1,0:T(8,128)(2,1)} %bitcast.36, bf16[2,192,2048]{2,1,0:T(8,128)(2,1)S(1)} %scale.1.refs_2_, bf16[2,192,2048]{2,1,0:T(8,128)(2,1)} %collective-permute-done.7.refs_3_), custom_call_target="tpu_custom_call" | custom-call | flops 3221225472 | bytes 5767168 | tf_op jit(solution)/shard_map/back/pallas_call | solution.py:375
  99.4 2.0 %copy-done.5 = bf16[1024,2048]{1,0:T(8,128)(2,1)} copy-done((bf16[1024,2048]{1,0:T(8,128)(2,1)}, bf16[1024,2048]{1,0:T(8,128)(2,1)S(1)}, u32[]{:S(2)}) %copy-start.5) | copy-done | bytes 4194328
  101.4 7.4 %back.3 = bf16[2,8,128,768]{3,2,1,0:T(8,128)(2,1)} custom-call(s32[3]{0:T(128)S(1)} %pad_add_fusion.refs_0_.place, bf16[1024,2048]{1,0:T(8,128)(2,1)} %copy-done.5, bf16[2,192,2048]{2,1,0:T(8,128)(2,1)S(1)} %scale.1.refs_2_, bf16[2,192,2048]{2,1,0:T(8,128)(2,1)} %collective-permute-done.7.refs_3_, ...), custom_call_target="tpu_custom_call", output_to_operand_aliasing={{}: (4, {})} | custom-call | flops 3221225472 | bytes 5767168 | tf_op jit(solution)/shard_map/back/pallas_call | solution.py:375
  108.8 1.5 all-to-all-done
  110.2 7.1 %all-to-all-start.1 = ((bf16[16,128,768]{2,1,0:T(8,128)(2,1)}), bf16[16,128,768]{2,1,0:T(8,128)(2,1)}, u32[]{:S(2)}, u32[]{:S(2)}) async-start(bf16[16,128,768]{2,1,0:T(8,128)(2,1)} %bitcast.34), calls=%async_computation.1 | async-start | bytes 6291456 | tf_op jit(solution)/shard_map/all_to_all | solution.py:291
  117.3 12.4 %gradient.1 = (f32[2,192,2048]{2,1,0:T(8,128)}, bf16[2,192,2048]{2,1,0:T(8,128)(2,1)S(1)}) custom-call(s32[3]{0:T(128)S(1)} %pad_add_fusion.refs_0_.place, bf16[2,8,128,768]{3,2,1,0:T(8,128)(2,1)} %bitcast.16.refs_1_.refs_2_, bf16[2,8,128,768]{3,2,1,0:T(8,128)(2,1)} %bitcast.16.refs_1_.refs_2_, bf16[1024,2048]{1,0:T(8,128)(2,1)} %bitcast.37, ...), custom_call_target="tpu_custom_call" | custom-call | flops 6442450944 | bytes 11534336 | tf_op jit(solution)/shard_map/gradient/pallas_call | solution.py:407
  129.8 1.5 collective-permute-start.9
  131.3 35.0 %collective-permute-done.9 = bf16[2,192,2048]{2,1,0:T(8,128)(2,1)S(1)} collective-permute-done((bf16[2,192,2048]{2,1,0:T(8,128)(2,1)S(1)}, bf16[2,192,2048]{2,1,0:T(8,128)(2,1)S(1)}, u32[]{:S(2)}, u32[]{:S(2)}) %collective-permute-start.9) | collective-permute-done | bytes 1572896 | tf_op jit(solution)/shard_map/ppermute | solution.py:437
  166.2 6.9 %fusion.2 = (bf16[2,192,2048]{2,1,0:T(8,128)(2,1)}, f32[2,192,2048]{2,1,0:T(8,128)}, bf16[2,192,2048]{2,1,0:T(8,128)(2,1)}) fusion(f32[2,192,2048]{2,1,0:T(8,128)} %get-tuple-element.33, bf16[2,192,2048]{2,1,0:T(8,128)(2,1)S(1)} %collective-permute-done.9, bf16[2,192,2048]{2,1,0:T(8,128)(2,1)S(1)} %copy-done.7, f32[2,192,2048]{2,1,0:T(8,128)S(1)} %copy-done.6, ...), kind=kLoop, calls=%fused_computation.6 | loop fusion | flops 16515072 | bytes 17301504 | tf_op jit(solution)/shard_map/convert_element_type | solution.py:445
  173.1 15.4 %all-to-all-done.1 = bf16[16,128,768]{2,1,0:T(8,128)(2,1)} async-done(((bf16[16,128,768]{2,1,0:T(8,128)(2,1)}), bf16[16,128,768]{2,1,0:T(8,128)(2,1)}, u32[]{:S(2)}, u32[]{:S(2)}) %all-to-all-start.1) | async-done | bytes 3145760 | tf_op jit(solution)/shard_map/all_to_all | solution.py:291
  188.5 4.8 %collect.1 = (bf16[128,8,768]{2,1,0:T(8,128)(2,1)}, f32[8,128]{1,0:T(8,128)}) custom-call(s32[8,128]{1,0:T(8,128)S(1)} %bitcast.30, f32[8,128]{1,0:T(8,128)S(1)} %bitcast.32, bf16[128,8,768]{2,1,0:T(8,128)(2,1)S(1)} %copy-done, bf16[2,8,128,768]{3,2,1,0:T(8,128)(2,1)} %bitcast.18.refs_3_), custom_call_target="tpu_custom_call" | custom-call | tf_op jit(solution)/shard_map/collect/pallas_call | solution.py:447
  (29 shorter events, 0.4 us)
Async XLA Ops:
  0.6 9.2 %copy-start = (bf16[128,8,768]{2,1,0:T(8,128)(2,1)S(1)}, bf16[128,8,768]{2,1,0:T(8,128)(2,1)}, u32[]{:S(2)}) copy-start(bf16[128,8,768]{2,1,0:T(8,128)(2,1)} %refs_2_.1) | copy-start | bytes 4718596
  0.6 14.2 %collective-permute-start.1 = (bf16[128,2048]{1,0:T(8,128)(2,1)}, bf16[128,2048]{1,0:T(8,128)(2,1)}, u32[]{:S(2)}, u32[]{:S(2)}) collective-permute-start(bf16[128,2048]{1,0:T(8,128)(2,1)} %param.9), channel_id=1, source_target_pairs={{0,24},{4,28},{8,0},{12,4},{16,8},{20,12},{24,16},{28,20},{1,25},{... | collective-permute-start | bytes 1572872 | tf_op jit(solution)/shard_map/ppermute | solution.py:287
  0.7 27.3 %collective-permute-start = (bf16[128,2048]{1,0:T(8,128)(2,1)}, bf16[128,2048]{1,0:T(8,128)(2,1)}, u32[]{:S(2)}, u32[]{:S(2)}) collective-permute-start(bf16[128,2048]{1,0:T(8,128)(2,1)} %param.9), channel_id=1, source_target_pairs={{0,8},{4,12},{8,16},{12,20},{16,24},{20,28},{24,0},{28,4},{1,9},{5... | collective-permute-start | bytes 1572872 | tf_op jit(solution)/shard_map/ppermute | solution.py:287
  2.7 25.3 %collective-permute-start.2 = (bf16[128,2048]{1,0:T(8,128)(2,1)}, bf16[128,2048]{1,0:T(8,128)(2,1)}, u32[]{:S(2)}, u32[]{:S(2)}) collective-permute-start(bf16[128,2048]{1,0:T(8,128)(2,1)} %param.9), channel_id=1, source_target_pairs={{0,4},{4,0},{8,12},{12,8},{16,20},{20,16},{24,28},{28,24},{1,5},{5... | collective-permute-start | bytes 1572872 | tf_op jit(solution)/shard_map/ppermute | solution.py:287
  4.3 0.8 copy-start.1
  5.1 4.7 %copy-start.2 = (s32[128,8]{0,1:T(8,128)S(1)}, s32[128,8]{0,1:T(8,128)}, u32[]{:S(2)}) copy-start(s32[128,8]{0,1:T(8,128)} %param.12) | copy-start | bytes 12292
  5.1 4.7 %copy-start.3 = (f32[128,8]{0,1:T(8,128)S(1)}, f32[128,8]{0,1:T(8,128)}, u32[]{:S(2)}) copy-start(f32[128,8]{0,1:T(8,128)} %param.11) | copy-start | bytes 12292
  8.2 81.8 %collective-permute-start.7 = (bf16[2,192,2048]{2,1,0:T(8,128)(2,1)S(1)}, bf16[2,192,2048]{2,1,0:T(8,128)(2,1)}, u32[]{:S(2)}, u32[]{:S(2)}) collective-permute-start(bf16[2,192,2048]{2,1,0:T(8,128)(2,1)S(1)} %scale.1.refs_2_), channel_id=1, source_target_pairs={{0,2},{2,0},{1,3},{3,1},{4,6},{6,4},{5,7},{7,5},{8,10},{10,8},{9,1... | collective-permute-start | bytes 4718600 | tf_op jit(solution)/shard_map/ppermute | solution.py:349
  28.0 19.1 %collective-permute-start.4 = (bf16[128,2048]{1,0:T(8,128)(2,1)}, bf16[128,2048]{1,0:T(8,128)(2,1)}, u32[]{:S(2)}, u32[]{:S(2)}) collective-permute-start(bf16[128,2048]{1,0:T(8,128)(2,1)} %collective-permute-done), channel_id=1, source_target_pairs={{0,8},{4,12},{8,16},{12,20},{16,24},{20,28},{24,0},{28,4},{1,9},{5... | collective-permute-start | bytes 1572872 | tf_op jit(solution)/shard_map/ppermute | solution.py:287
  28.0 20.6 %collective-permute-start.3 = (bf16[128,2048]{1,0:T(8,128)(2,1)}, bf16[128,2048]{1,0:T(8,128)(2,1)}, u32[]{:S(2)}, u32[]{:S(2)}) collective-permute-start(bf16[128,2048]{1,0:T(8,128)(2,1)} %collective-permute-done), channel_id=1, source_target_pairs={{0,4},{4,0},{8,12},{12,8},{16,20},{20,16},{24,28},{28,24},{1,5},{5... | collective-permute-start | bytes 1572872 | tf_op jit(solution)/shard_map/ppermute | solution.py:287
  29.5 80.7 %all-to-all-start = ((bf16[16,128,768]{2,1,0:T(8,128)(2,1)}), bf16[16,128,768]{2,1,0:T(8,128)(2,1)}, u32[]{:S(2)}, u32[]{:S(2)}) async-start(bf16[16,128,768]{2,1,0:T(8,128)(2,1)} %bitcast.33), calls=%async_computation | async-start | bytes 6291456 | tf_op jit(solution)/shard_map/all_to_all | solution.py:291
  35.8 2.1 %copy-start.9 = (bf16[128,2048]{1,0:T(8,128)(2,1)S(1)}, bf16[128,2048]{1,0:T(8,128)(2,1)}, u32[]{:S(2)}) copy-start(bf16[128,2048]{1,0:T(8,128)(2,1)} %param.9) | copy-start | bytes 1572868
  35.8 54.2 %collective-permute-start.6 = (bf16[128,2048]{1,0:T(8,128)(2,1)}, bf16[128,2048]{1,0:T(8,128)(2,1)S(1)}, u32[]{:S(2)}, u32[]{:S(2)}) collective-permute-start(bf16[128,2048]{1,0:T(8,128)(2,1)} %collective-permute-done.1), channel_id=1, source_target_pairs={{0,4},{4,0},{8,12},{12,8},{16,20},{20,16},{24,28},{28,24},{1,5},{5... | collective-permute-start | bytes 1572872 | tf_op jit(solution)/shard_map/ppermute | solution.py:287
  47.1 41.7 %collective-permute-start.5 = (bf16[128,2048]{1,0:T(8,128)(2,1)}, bf16[128,2048]{1,0:T(8,128)(2,1)S(1)}, u32[]{:S(2)}, u32[]{:S(2)}) collective-permute-start(bf16[128,2048]{1,0:T(8,128)(2,1)} %collective-permute-done.4), channel_id=1, source_target_pairs={{0,4},{4,0},{8,12},{12,8},{16,20},{20,16},{24,28},{28,24},{1,5},{5... | collective-permute-start | bytes 1572872 | tf_op jit(solution)/shard_map/ppermute | solution.py:287
  90.0 1.9 %copy-start.4 = (bf16[8,128,2048]{2,1,0:T(8,128)(2,1)}, bf16[8,128,2048]{2,1,0:T(8,128)(2,1)S(1)}, u32[]{:S(2)}) copy-start(bf16[8,128,2048]{2,1,0:T(8,128)(2,1)S(1)} %bitcast_dynamic-update-slice_fusion) | copy-start | bytes 12582916
  90.0 9.3 %collective-permute-start.8 = (bf16[1024,2048]{1,0:T(8,128)(2,1)S(1)}, bf16[1024,2048]{1,0:T(8,128)(2,1)S(1)}, u32[]{:S(2)}, u32[]{:S(2)}) collective-permute-start(bf16[1024,2048]{1,0:T(8,128)(2,1)S(1)} %bitcast.35), channel_id=1, source_target_pairs={{0,1},{1,0},{2,3},{3,2},{4,5},{5,4},{6,7},{7,6},{8,9},{9,8},{10,11... | collective-permute-start | bytes 12582920 | tf_op jit(solution)/shard_map/ppermute | solution.py:366
  99.4 2.0 %copy-start.5 = (bf16[1024,2048]{1,0:T(8,128)(2,1)}, bf16[1024,2048]{1,0:T(8,128)(2,1)S(1)}, u32[]{:S(2)}) copy-start(bf16[1024,2048]{1,0:T(8,128)(2,1)S(1)} %collective-permute-done.8.refs_1_.refs_4_) | copy-start | bytes 12582916
  110.2 78.2 %all-to-all-start.1 = ((bf16[16,128,768]{2,1,0:T(8,128)(2,1)}), bf16[16,128,768]{2,1,0:T(8,128)(2,1)}, u32[]{:S(2)}, u32[]{:S(2)}) async-start(bf16[16,128,768]{2,1,0:T(8,128)(2,1)} %bitcast.34), calls=%async_computation.1 | async-start | bytes 6291456 | tf_op jit(solution)/shard_map/all_to_all | solution.py:291
  117.3 48.9 %copy-start.6 = (f32[2,192,2048]{2,1,0:T(8,128)S(1)}, f32[2,192,2048]{2,1,0:T(8,128)}, u32[]{:S(2)}) copy-start(f32[2,192,2048]{2,1,0:T(8,128)} %param.15) | copy-start | bytes 9437188
  117.3 48.9 %copy-start.7 = (bf16[2,192,2048]{2,1,0:T(8,128)(2,1)S(1)}, bf16[2,192,2048]{2,1,0:T(8,128)(2,1)}, u32[]{:S(2)}) copy-start(bf16[2,192,2048]{2,1,0:T(8,128)(2,1)} %param.17) | copy-start | bytes 4718596
  117.3 48.9 %copy-start.8 = (bf16[2,192,2048]{2,1,0:T(8,128)(2,1)S(1)}, bf16[2,192,2048]{2,1,0:T(8,128)(2,1)}, u32[]{:S(2)}) copy-start(bf16[2,192,2048]{2,1,0:T(8,128)(2,1)} %param.16) | copy-start | bytes 4718596
  129.8 36.4 %collective-permute-start.9 = (bf16[2,192,2048]{2,1,0:T(8,128)(2,1)S(1)}, bf16[2,192,2048]{2,1,0:T(8,128)(2,1)S(1)}, u32[]{:S(2)}, u32[]{:S(2)}) collective-permute-start(bf16[2,192,2048]{2,1,0:T(8,128)(2,1)S(1)} %get-tuple-element.34), channel_id=1, source_target_pairs={{0,2},{2,0},{1,3},{3,1},{4,6},{6,4},{5,7},{7,5},{8,10},{10,8},{9,1... | collective-permute-start | bytes 4718600 | tf_op jit(solution)/shard_map/ppermute | solution.py:437

commit v4 on v3

--- a/solution.py
+++ b/solution.py
@@ -271,27 +271,39 @@
     tokens, top = expert_ids.shape
     here, rows_here, model_width = weight_q.shape
     width = hidden_saved.shape[2]
-    groups = lax.axis_size("expert")
+    halves, line, pair = lax.axis_size("half"), lax.axis_size("line"), lax.axis_size("pair")
+    groups = halves * line * pair
     fsdp, replica = lax.axis_size("fsdp"), lax.axis_size("replica")
-    me, mf, mr = lax.axis_index("expert"), lax.axis_index("fsdp"), lax.axis_index("replica")
-    inner = 2 if groups % 2 == 0 else 1
-    outer = groups // inner
+    place_of = {name: lax.axis_index(name) for name in ("half", "line", "pair")}
+    mf, mr = lax.axis_index("fsdp"), lax.axis_index("replica")
     unit = width // (fsdp * replica)
     block = min(TOKEN_BLOCK * PARTS, tokens)
     lanes = here * fsdp * unit
 
-    def moved(e, s, j):
-        return (e // inner + s) % outer * inner + (e % inner + j) % inner
-
-    def send(x, s, j):
-        return lax.ppermute(x, "expert", [(e, moved(e, s, j)) for e in range(groups)])
+    def shift(x, axis, by, across=0):
+        size = lax.axis_size(axis)
+        if not across:
+            return lax.ppermute(x, axis, [(i, (i + by) % size) for i in range(size)])
+        pairs = [
+            (i * pair + j, (i + by) % size * pair + (j + across) % pair)
+            for i in range(size)
+            for j in range(pair)
+        ]
+        return lax.ppermute(x, (axis, "pair"), pairs)
+
+    def source_of(b, i, j):
+        place = 0
+        for name, by in (("half", b), ("line", i), ("pair", j)):
+            size = lax.axis_size(name)
+            place = place * size + lax.rem(place_of[name] + (size - by), size)
+        return place
 
     def exchange(x):
         x = x.reshape(replica * groups, tokens, lanes)
-        x = lax.all_to_all(x, ("replica", "expert"), split_axis=0, concat_axis=0, tiled=True)
+        x = lax.all_to_all(x, ("replica", "half", "line", "pair"), split_axis=0, concat_axis=0, tiled=True)
         return x.reshape(replica, groups, tokens, lanes)
 
-    place = jnp.stack([me, mf, mr]).astype(jnp.int32)
+    place = jnp.stack([mf, mf, mr]).astype(jnp.int32)
     weight_part = pl.pallas_call(
         scale_kernel,
         out_shape=jax.ShapeDtypeStruct((here, unit, model_width), jnp.bfloat16),
@@ -305,7 +317,7 @@
             out_specs=pl.BlockSpec((1, unit, model_width), lambda e, p: (e, 0, 0)),
             scratch_shapes=[pltpu.VMEM((rows_here, weight_exp.shape[2]), jnp.float32)],
         ),
-        compiler_params=pltpu.CompilerParams(vmem_limit_bytes=VMEM),
+        compiler_params=pltpu.CompilerParams(vmem_limit_bytes=20 * 2**20),
         name="scale",
     )(place, weight_q, weight_exp.swapaxes(1, 2))
 
@@ -326,39 +338,33 @@
             out_specs=row_spec,
             scratch_shapes=[turned],
         ),
-        compiler_params=pltpu.CompilerParams(vmem_limit_bytes=VMEM),
+        compiler_params=pltpu.CompilerParams(vmem_limit_bytes=20 * 2**20),
         name="spread",
     )(place, expert_ids.T, gate_probs.T, hidden_saved)
 
-    ups = outer // 2
-    line = {0: out_grad}
-    pair = {}
-    if outer > 1:
-        line[1] = send(out_grad, 1, 0)
-    if outer > 2:
-        line[outer - 1] = send(out_grad, outer - 1, 0)
-    if inner > 1:
-        pair[0] = send(out_grad, 0, 1)
-    line, pair, spread = lax.optimization_barrier((line, pair, spread))
+    dy = {(0, 0, 0): out_grad}
+    for b in range(1, halves):
+        dy[b, 0, 0] = shift(out_grad, "half", b)
+    for i in range(1, line):
+        dy[0, i, 0] = shift(out_grad, "line", i)
+    for j in range(1, pair):
+        dy[0, 0, j] = shift(out_grad, "pair", j)
+    dy, spread = lax.optimization_barrier((dy, spread))
     hid = exchange(spread)
-    for s in range(2, ups + 1):
-        line[s] = send(line[s - 1], 1, 0)
-    for s in range(outer - 2, ups, -1):
-        line[s] = send(line[s + 1], outer - 1, 0)
+    for b in range(1, halves):
+        for i in range(1, line):
+            dy[b, i, 0] = shift(dy[b, 0, 0], "line", i)
     weight_parts = [weight_part] + [
         lax.ppermute(weight_part, "fsdp", [(f, (f - o) % fsdp) for f in range(fsdp)])
         for o in range(1, fsdp)
     ]
     own = jnp.zeros((groups, tokens, model_width), jnp.bfloat16)
-    for s in range(outer):
-        for j in range(inner):
-            piece = line[s]
-            if j:
-                piece = pair[s] if s in pair else send(line[s], 0, j)
-            source = lax.rem(lax.div(me, inner) + (outer - s), outer) * inner + lax.rem(
-                me + (inner - j), inner
-            )
-            own = lax.dynamic_update_index_in_dim(own, piece, source, 0)
+    for b in range(halves):
+        for i in range(line):
+            for j in range(pair):
+                if (b, i, j) not in dy:
+                    dy[b, i, j] = (shift(dy[b, 0, 0], "line", i, j) if i else shift(dy[b, 0, 0], "pair", j)) if b else shift(dy[0, i, 0], "pair", j)
+                own = lax.dynamic_update_index_in_dim(own, dy[b, i, j], source_of(b, i, j), 0)
     own, weight_parts = lax.optimization_barrier(
         (own.reshape(groups * tokens, model_width), weight_parts)
     )
@@ -389,7 +395,7 @@
                     ),
                     scratch_shapes=[pltpu.VMEM((lanes, model_width), jnp.bfloat16)],
                 ),
-                compiler_params=pltpu.CompilerParams(vmem_limit_bytes=VMEM),
+                compiler_params=pltpu.CompilerParams(vmem_limit_bytes=36 * 2**20),
                 cost_estimate=pl.CostEstimate(
                     flops=2 * groups * tokens * lanes * model_width,
                     bytes_accessed=2 * groups * tokens * (lanes + model_width),
@@ -424,7 +430,7 @@
             out_specs=[grad_spec] * fsdp,
             scratch_shapes=[pltpu.VMEM((replica, lanes, groups * tokens), jnp.bfloat16)],
         ),
-        compiler_params=pltpu.CompilerParams(vmem_limit_bytes=VMEM),
+        compiler_params=pltpu.CompilerParams(vmem_limit_bytes=20 * 2**20),
         cost_estimate=pl.CostEstimate(
             flops=2 * replica * groups * tokens * lanes * model_width,
             bytes_accessed=2 * replica * groups * tokens * (lanes + model_width),
@@ -462,37 +468,41 @@
             pl.BlockSpec((top, tokens), lambda i: (0, 0)),
         ],
         scratch_shapes=[turned, pltpu.VMEM((tokens, top), jnp.float32)],
-        compiler_params=pltpu.CompilerParams(vmem_limit_bytes=VMEM),
+        compiler_params=pltpu.CompilerParams(vmem_limit_bytes=20 * 2**20),
         name="collect",
-    )(expert_ids.T, gate_probs.T, hidden_saved, returned)
+    )(
+        expert_ids.T,
+        gate_probs.T,
+        pltpu.with_memory_space_constraint(hidden_saved, pltpu.HBM),
+        returned,
+    )
     return (hidden_grad, gate_grad.T) + new
 
 
-def body(*args):
-    tokens, top = args[3].shape
-    experts = lax.axis_size("expert") * args[4].shape[0]
-    if min(tokens, 2 * tokens * top // experts) == tokens:
-        return dense_body(*args)
-    return slots_body(*args)
-
-
 def solution(mesh):
-    in_specs = (
-        P(("expert", "fsdp", "replica"), None),
-        P(("expert", "fsdp", "replica"), None, None),
-        P(("expert", "fsdp", "replica"), None),
-        P(("expert", "fsdp", "replica"), None),
-        P("expert", "fsdp", None),
-        P("expert", "fsdp", None),
-        P("expert", ("fsdp", "replica"), None),
-        P("expert", ("fsdp", "replica"), None),
-        P("expert", ("fsdp", "replica"), None),
-    )
-    out_specs = (
-        P(("expert", "fsdp", "replica"), None, None),
-        P(("expert", "fsdp", "replica"), None),
-        P("expert", ("fsdp", "replica"), None),
-        P("expert", ("fsdp", "replica"), None),
-        P("expert", ("fsdp", "replica"), None),
-    )
-    return jax.shard_map(body, mesh=mesh, in_specs=in_specs, out_specs=out_specs, check_vma=False)
+    sizes = dict(mesh.shape)
+    devices = mesh.devices.size
+    groups = sizes["expert"]
+
+    def mapped(function, mesh, expert):
+        rows = P(expert + ("fsdp", "replica"))
+        state = P(expert, ("fsdp", "replica"))
+        weights = P(expert, "fsdp")
+        in_specs = (rows,) * 4 + (weights,) * 2 + (state,) * 3
+        out_specs = (rows,) * 2 + (state,) * 3
+        return jax.shard_map(
+            function, mesh=mesh, in_specs=in_specs, out_specs=out_specs, check_vma=False
+        )
+
+    def program(*args):
+        tokens, top = args[3].shape[0] // devices, args[3].shape[1]
+        dense = min(tokens, 2 * tokens * top // args[4].shape[0]) == tokens
+        if not dense or groups % 4 or mesh.axis_names[0] != "expert":
+            return mapped(slots_body, mesh, ("expert",))(*args)
+        halves = jax.sharding.Mesh(
+            mesh.devices.reshape((2, groups // 4, 2) + mesh.devices.shape[1:]),
+            ("half", "line", "pair") + mesh.axis_names[1:],
+        )
+        return mapped(dense_body, halves, ("half", "line", "pair"))(*args)
+
+    return program

time: 194 us -> 189 us (0.974)
  Pallas kernels: 39.1 us -> 34.8 us
  local copies, waits for them, and re-layouts: 10.8 us -> 14.9 us
  waiting for transfers between devices: 111 us -> 109 us
    ppermute x7, waiting for transfers between devices: 59.2 us -> 42.7 us  [the longest x6 42.7 us: shift(): return lax.ppermute(x, axis, [(i, (i + by) % size) for i in range(size)])]
    all_to_all x2, waiting for transfers between devices: 16.8 us -> 30.9 us  [exchange(): lax.all_to_all(x, ('replica', 'half', 'line', 'pair'), split_axis=0, conc...]
    unnamed x20 -> x32, local copies, waits for them, and re-layouts: 4.7 us -> 10.8 us
    all_to_all x2, starting transfers between devices: 13.3 us -> 10.1 us  [exchange(): lax.all_to_all(x, ('replica', 'half', 'line', 'pair'), split_axis=0, conc...]
    pallas_call x2, Pallas kernels: 14.8 us -> 12.6 us  [dense_body(): pl.pallas_call(lambda *refs: back_kernel((fsdp, replica), *refs), out_sha...]
    dynamic_update_slice x8, local copies, waits for them, and re-layouts: 5.58 us -> 3.63 us  [dense_body(): lax.dynamic_update_index_in_dim(own, dy[b, i, j], source_of(b, i, j), 0)]
  transfers between devices with their start and end apart: 12 -> 12, of which waited for: 7 -> 7; matrix products, arithmetic and copies ran while one was open for 7% -> 5% of each run, Pallas kernels for 18% -> 16%
where the time goes in v4:
time: 189 us; the launch traced here: 188 us
  waiting for transfers between devices  109 us (58%)
  Pallas kernels  34.8 us (18%)
  starting transfers between devices  23.4 us (12%)
  local copies, waits for them, and re-layouts  14.9 us (8%)
  other arithmetic  5.62 us (3%)
    ppermute x6, waiting for transfers between devices, shift(): return lax.ppermute(x, axis, [(i, (i + by) % size) for i in range(size)])  42.7 us
    ppermute x1, waiting for transfers between devices, dense_body(): lax.ppermute(grads[o], 'fsdp', [(f, (f + o) % fsdp) for f in range(fsdp)])  34.5 us
    all_to_all x2, waiting for transfers between devices, exchange(): lax.all_to_all(x, ('replica', 'half', 'line', 'pair'), split_axis=0, conc...  30.9 us
    pallas_call x2, Pallas kernels, dense_body(): pl.pallas_call(lambda *refs: back_kernel((fsdp, replica), *refs), out_sha...  12.6 us
    pallas_call x1, Pallas kernels, dense_body(): pl.pallas_call(lambda *refs: gradient_kernel((fsdp, replica), *refs), out...  11.7 us
    unnamed x32, local copies, waits for them, and re-layouts  10.8 us
    all_to_all x2, starting transfers between devices, exchange(): lax.all_to_all(x, ('replica', 'half', 'line', 'pair'), split_axis=0, conc...  10.1 us
    ppermute x6, starting transfers between devices, shift(): return lax.ppermute(x, axis, [(i, (i + by) % size) for i in range(size)])  7.75 us
  transfers between devices with their start and end apart: 12, of which 7 were waited for; matrix products, arithmetic and copies ran while one was open for 5% of the time, Pallas kernels for 16%

profile of v4, /device:TPU:8, one launch (start us, length us, event | category | flops | bytes accessed | tf_op | source)
XLA Modules:
  0.0 188.1 jit_solution(5370741000682813808)
XLA Ops:
  0.7 2.0 %collective-permute-start = (bf16[128,2048]{1,0:T(8,128)(2,1)}, bf16[128,2048]{1,0:T(8,128)(2,1)}, u32[]{:S(2)}, u32[]{:S(2)}) collective-permute-start(bf16[128,2048]{1,0:T(8,128)(2,1)} %param.9), channel_id=1, source_target_pairs={{0,4},{4,0},{1,5},{5,1},{2,6},{6,2},{3,7},{7,3},{8,12},{12,8},{9,1... | collective-permute-start | bytes 1572872 | tf_op jit(solution)/shard_map/ppermute | solution.py:286
  2.7 2.6 %collective-permute-start.2 = (bf16[128,2048]{1,0:T(8,128)(2,1)}, bf16[128,2048]{1,0:T(8,128)(2,1)}, u32[]{:S(2)}, u32[]{:S(2)}) collective-permute-start(bf16[128,2048]{1,0:T(8,128)(2,1)} %param.9), channel_id=1, source_target_pairs={{0,16},{16,0},{1,17},{17,1},{2,18},{18,2},{3,19},{19,3},{4,20},{20... | collective-permute-start | bytes 1572872 | tf_op jit(solution)/shard_map/ppermute | solution.py:286
  5.3 1.9 %copy-done.8 = bf16[2,384,2048]{2,1,0:T(8,128)(2,1)S(1)} copy-done((bf16[2,384,2048]{2,1,0:T(8,128)(2,1)S(1)}, bf16[2,384,2048]{2,1,0:T(8,128)(2,1)}, u32[]{:S(2)}) %copy-start.8) | copy-done | bytes 3145752
  7.2 0.8 copy-done.9
  8.0 2.0 %scale.1.refs_2_ = bf16[2,192,2048]{2,1,0:T(8,128)(2,1)S(1)} custom-call(s32[3]{0:T(128)S(1)} %pad_add_fusion.refs_0_.place, bf16[2,384,2048]{2,1,0:T(8,128)(2,1)S(1)} %copy-done.8, s32[2,16,384]{2,1,0:T(8,128)S(1)} %bitcast.32), custom_call_target="tpu_custom_call" | custom-call | tf_op jit(solution)/shard_map/scale/pallas_call | solution.py:307
  10.0 1.6 collective-permute-start.7
  11.6 3.9 %spread.1 = bf16[2,8,128,768]{3,2,1,0:T(8,128)(2,1)} custom-call(s32[3]{0:T(128)S(1)} %pad_add_fusion.refs_0_.place, s32[8,128]{1,0:T(8,128)S(1)} %bitcast.33, f32[8,128]{1,0:T(8,128)S(1)} %bitcast.35, bf16[128,8,768]{2,1,0:T(8,128)(2,1)S(1)} %copy-done.1), custom_call_target="tpu_custom_call" | custom-call | tf_op jit(solution)/shard_map/spread/pallas_call | solution.py:331
  15.5 6.8 %collective-permute-done.1 = bf16[128,2048]{1,0:T(8,128)(2,1)} collective-permute-done((bf16[128,2048]{1,0:T(8,128)(2,1)}, bf16[128,2048]{1,0:T(8,128)(2,1)}, u32[]{:S(2)}, u32[]{:S(2)}) %collective-permute-start.1) | collective-permute-done | bytes 524320 | tf_op jit(solution)/shard_map/ppermute | solution.py:286
  22.4 5.1 %collective-permute-done.2 = bf16[128,2048]{1,0:T(8,128)(2,1)} collective-permute-done((bf16[128,2048]{1,0:T(8,128)(2,1)}, bf16[128,2048]{1,0:T(8,128)(2,1)}, u32[]{:S(2)}, u32[]{:S(2)}) %collective-permute-start.2) | collective-permute-done | bytes 524320 | tf_op jit(solution)/shard_map/ppermute | solution.py:286
  27.5 2.3 %collective-permute-start.6 = (bf16[128,2048]{1,0:T(8,128)(2,1)}, bf16[128,2048]{1,0:T(8,128)(2,1)S(1)}, u32[]{:S(2)}, u32[]{:S(2)}) collective-permute-start(bf16[128,2048]{1,0:T(8,128)(2,1)} %collective-permute-done.2), channel_id=1, source_target_pairs={{0,12},{4,8},{8,4},{12,0},{1,13},{5,9},{9,5},{13,1},{2,14},{6,10},... | collective-permute-start | bytes 1572872 | tf_op jit(solution)/shard_map/ppermute | solution.py:292
  30.0 1.4 collective-permute-start.4
  31.4 6.3 %all-to-all-start = ((bf16[16,128,768]{2,1,0:T(8,128)(2,1)}), bf16[16,128,768]{2,1,0:T(8,128)(2,1)}, u32[]{:S(2)}, u32[]{:S(2)}) async-start(bf16[16,128,768]{2,1,0:T(8,128)(2,1)} %bitcast.14), calls=%async_computation | async-start | bytes 6291456 | tf_op jit(solution)/shard_map/all_to_all | solution.py:303
  37.7 1.5 collective-permute-start.3
  39.2 0.5 broadcast_in_dim.28
  39.8 1.1 bitcast_dynamic-update-slice_fusion.6
  40.9 1.2 bitcast_dynamic-update-slice_fusion.5
  42.1 30.7 %collective-permute-done.3 = bf16[128,2048]{1,0:T(8,128)(2,1)S(1)} collective-permute-done((bf16[128,2048]{1,0:T(8,128)(2,1)}, bf16[128,2048]{1,0:T(8,128)(2,1)S(1)}, u32[]{:S(2)}, u32[]{:S(2)}) %collective-permute-start.3) | collective-permute-done | bytes 524320 | tf_op jit(solution)/shard_map/ppermute | solution.py:286
  72.9 1.1 bitcast_dynamic-update-slice_fusion.3
  74.3 6.7 %back.2.refs_4_ = bf16[2,8,128,768]{3,2,1,0:T(8,128)(2,1)S(1)} custom-call(s32[3]{0:T(128)S(1)} %pad_add_fusion.refs_0_.place, bf16[1024,2048]{1,0:T(8,128)(2,1)S(1)} %bitcast.30, bf16[2,192,2048]{2,1,0:T(8,128)(2,1)S(1)} %copy-done.3, bf16[2,192,2048]{2,1,0:T(8,128)(2,1)} %collective-permute-done.7.refs_3_), custom_call_target="tpu_custom_call" | custom-call | flops 3221225472 | bytes 5767168 | tf_op jit(solution)/shard_map/back/pallas_call | solution.py:381
  81.5 5.9 %back.3 = bf16[2,8,128,768]{3,2,1,0:T(8,128)(2,1)S(1)} custom-call(s32[3]{0:T(128)S(1)} %pad_add_fusion.refs_0_.place, bf16[1024,2048]{1,0:T(8,128)(2,1)S(1)} %collective-permute-done.8.refs_1_.refs_4_, bf16[2,192,2048]{2,1,0:T(8,128)(2,1)S(1)} %copy-done.3, bf16[2,192,2048]{2,1,0:T(8,128)(2,1)} %collective-permute-done.7.refs_3_, ...), custom_call_target="tpu_custom_call", output_to_operand_aliasing={{}: (4, {})} | custom-call | flops 3221225472 | bytes 5767168 | tf_op jit(solution)/shard_map/back/pallas_call | solution.py:381
  87.4 1.7 copy-done
  89.0 2.0 %copy-done.6 = bf16[1024,2048]{1,0:T(8,128)(2,1)} copy-done((bf16[1024,2048]{1,0:T(8,128)(2,1)}, bf16[1024,2048]{1,0:T(8,128)(2,1)S(1)}, u32[]{:S(2)}) %copy-start.6) | copy-done | bytes 4194328
  91.0 18.1 %all-to-all-done = bf16[16,128,768]{2,1,0:T(8,128)(2,1)} async-done(((bf16[16,128,768]{2,1,0:T(8,128)(2,1)}), bf16[16,128,768]{2,1,0:T(8,128)(2,1)}, u32[]{:S(2)}, u32[]{:S(2)}) %all-to-all-start) | async-done | bytes 3145760 | tf_op jit(solution)/shard_map/all_to_all | solution.py:303
  109.2 3.8 %all-to-all-start.1 = ((bf16[16,128,768]{2,1,0:T(8,128)(2,1)}), bf16[16,128,768]{2,1,0:T(8,128)(2,1)S(1)}, u32[]{:S(2)}, u32[]{:S(2)}) async-start(bf16[16,128,768]{2,1,0:T(8,128)(2,1)} %bitcast.28), calls=%async_computation.1 | async-start | bytes 6291456 | tf_op jit(solution)/shard_map/all_to_all | solution.py:303
  113.0 2.2 %copy-done.5 = bf16[8,128,2048]{2,1,0:T(8,128)(2,1)S(1)} copy-done((bf16[8,128,2048]{2,1,0:T(8,128)(2,1)S(1)}, bf16[8,128,2048]{2,1,0:T(8,128)(2,1)}, u32[]{:S(2)}) %copy-start.5) | copy-done | bytes 4194328
  115.2 2.2 %copy-done.7 = bf16[1024,2048]{1,0:T(8,128)(2,1)S(1)} copy-done((bf16[1024,2048]{1,0:T(8,128)(2,1)S(1)}, bf16[1024,2048]{1,0:T(8,128)(2,1)}, u32[]{:S(2)}) %copy-start.7) | copy-done | bytes 4194328
  117.4 11.7 %gradient.1 = (f32[2,192,2048]{2,1,0:T(8,128)S(1)}, bf16[2,192,2048]{2,1,0:T(8,128)(2,1)S(1)}) custom-call(s32[3]{0:T(128)S(1)} %pad_add_fusion.refs_0_.place, bf16[2,8,128,768]{3,2,1,0:T(8,128)(2,1)} %bitcast.15.refs_1_.refs_2_, bf16[2,8,128,768]{3,2,1,0:T(8,128)(2,1)} %bitcast.15.refs_1_.refs_2_, bf16[1024,2048]{1,0:T(8,128)(2,1)S(1)} %bitcast.31, ...), custom_call_target="tpu_custom_call" | custom-call | flops 6442450944 | bytes 11534336 | tf_op jit(solution)/shard_map/gradient/pallas_call | solution.py:413
  129.1 1.6 collective-permute-start.9
  130.7 34.5 %collective-permute-done.9 = bf16[2,192,2048]{2,1,0:T(8,128)(2,1)S(1)} collective-permute-done((bf16[2,192,2048]{2,1,0:T(8,128)(2,1)S(1)}, bf16[2,192,2048]{2,1,0:T(8,128)(2,1)S(1)}, u32[]{:S(2)}, u32[]{:S(2)}) %collective-permute-start.9) | collective-permute-done | bytes 1572896 | tf_op jit(solution)/shard_map/ppermute | solution.py:443
  165.2 5.5 %fusion.2 = (bf16[2,192,2048]{2,1,0:T(8,128)(2,1)}, f32[2,192,2048]{2,1,0:T(8,128)}, bf16[2,192,2048]{2,1,0:T(8,128)(2,1)}) fusion(f32[2,192,2048]{2,1,0:T(8,128)S(1)} %get-tuple-element.33, bf16[2,192,2048]{2,1,0:T(8,128)(2,1)S(1)} %collective-permute-done.9, bf16[2,192,2048]{2,1,0:T(8,128)(2,1)S(1)} %copy-done.13, f32[2,192,2048]{2,1,0:T(8,128)S(1)} %copy-done.12, ...), kind=kLoop, calls=%fused_computation.6 | loop fusion | flops 16515072 | bytes 17301504 | tf_op jit(solution)/shard_map/convert_element_type | solution.py:451
  170.7 12.8 %all-to-all-done.1 = bf16[16,128,768]{2,1,0:T(8,128)(2,1)S(1)} async-done(((bf16[16,128,768]{2,1,0:T(8,128)(2,1)}), bf16[16,128,768]{2,1,0:T(8,128)(2,1)S(1)}, u32[]{:S(2)}, u32[]{:S(2)}) %all-to-all-start.1) | async-done | bytes 3145760 | tf_op jit(solution)/shard_map/all_to_all | solution.py:303
  183.5 4.6 %collect.1 = (bf16[128,8,768]{2,1,0:T(8,128)(2,1)}, f32[8,128]{1,0:T(8,128)}) custom-call(s32[8,128]{1,0:T(8,128)S(1)} %bitcast.34, f32[8,128]{1,0:T(8,128)S(1)} %bitcast.36, bf16[128,8,768]{2,1,0:T(8,128)(2,1)} %refs_2_.1, bf16[2,8,128,768]{3,2,1,0:T(8,128)(2,1)S(1)} %bitcast.27), custom_call_target="tpu_custom_call" | custom-call | tf_op jit(solution)/shard_map/collect/pallas_call | solution.py:453
  (41 shorter events, 1.2 us)
Async XLA Ops:
  0.6 10.9 %copy-start.1 = (bf16[128,8,768]{2,1,0:T(8,128)(2,1)S(1)}, bf16[128,8,768]{2,1,0:T(8,128)(2,1)}, u32[]{:S(2)}) copy-start(bf16[128,8,768]{2,1,0:T(8,128)(2,1)} %refs_2_.1) | copy-start | bytes 4718596
  0.6 21.7 %collective-permute-start.1 = (bf16[128,2048]{1,0:T(8,128)(2,1)}, bf16[128,2048]{1,0:T(8,128)(2,1)}, u32[]{:S(2)}, u32[]{:S(2)}) collective-permute-start(bf16[128,2048]{1,0:T(8,128)(2,1)} %param.9), channel_id=1, source_target_pairs={{0,8},{8,0},{1,9},{9,1},{2,10},{10,2},{3,11},{11,3},{4,12},{12,4},... | collective-permute-start | bytes 1572872 | tf_op jit(solution)/shard_map/ppermute | solution.py:286
  0.7 21.6 %collective-permute-start = (bf16[128,2048]{1,0:T(8,128)(2,1)}, bf16[128,2048]{1,0:T(8,128)(2,1)}, u32[]{:S(2)}, u32[]{:S(2)}) collective-permute-start(bf16[128,2048]{1,0:T(8,128)(2,1)} %param.9), channel_id=1, source_target_pairs={{0,4},{4,0},{1,5},{5,1},{2,6},{6,2},{3,7},{7,3},{8,12},{12,8},{9,1... | collective-permute-start | bytes 1572872 | tf_op jit(solution)/shard_map/ppermute | solution.py:286
  2.7 24.8 %collective-permute-start.2 = (bf16[128,2048]{1,0:T(8,128)(2,1)}, bf16[128,2048]{1,0:T(8,128)(2,1)}, u32[]{:S(2)}, u32[]{:S(2)}) collective-permute-start(bf16[128,2048]{1,0:T(8,128)(2,1)} %param.9), channel_id=1, source_target_pairs={{0,16},{16,0},{1,17},{17,1},{2,18},{18,2},{3,19},{19,3},{4,20},{20... | collective-permute-start | bytes 1572872 | tf_op jit(solution)/shard_map/ppermute | solution.py:286
  5.3 1.9 %copy-start.8 = (bf16[2,384,2048]{2,1,0:T(8,128)(2,1)S(1)}, bf16[2,384,2048]{2,1,0:T(8,128)(2,1)}, u32[]{:S(2)}) copy-start(bf16[2,384,2048]{2,1,0:T(8,128)(2,1)} %values.1) | copy-start | bytes 9437188
  7.2 0.8 copy-start.9
  8.0 3.5 %copy-start.10 = (s32[128,8]{0,1:T(8,128)S(1)}, s32[128,8]{0,1:T(8,128)}, u32[]{:S(2)}) copy-start(s32[128,8]{0,1:T(8,128)} %param.12) | copy-start | bytes 12292
  8.0 3.5 %copy-start.11 = (f32[128,8]{0,1:T(8,128)S(1)}, f32[128,8]{0,1:T(8,128)}, u32[]{:S(2)}) copy-start(f32[128,8]{0,1:T(8,128)} %param.11) | copy-start | bytes 12292
  10.0 21.4 %copy-start.2 = (bf16[2,192,2048]{2,1,0:T(8,128)(2,1)}, bf16[2,192,2048]{2,1,0:T(8,128)(2,1)S(1)}, u32[]{:S(2)}) copy-start(bf16[2,192,2048]{2,1,0:T(8,128)(2,1)S(1)} %scale.1.refs_2_) | copy-start | bytes 4718596
  10.0 64.2 %collective-permute-start.7 = (bf16[2,192,2048]{2,1,0:T(8,128)(2,1)S(1)}, bf16[2,192,2048]{2,1,0:T(8,128)(2,1)}, u32[]{:S(2)}, u32[]{:S(2)}) collective-permute-start(bf16[2,192,2048]{2,1,0:T(8,128)(2,1)S(1)} %scale.1.refs_2_), channel_id=1, source_target_pairs={{0,2},{2,0},{1,3},{3,1},{4,6},{6,4},{5,7},{7,5},{8,10},{10,8},{9,1... | collective-permute-start | bytes 4718600 | tf_op jit(solution)/shard_map/ppermute | solution.py:358
  27.5 46.7 %collective-permute-start.6 = (bf16[128,2048]{1,0:T(8,128)(2,1)}, bf16[128,2048]{1,0:T(8,128)(2,1)S(1)}, u32[]{:S(2)}, u32[]{:S(2)}) collective-permute-start(bf16[128,2048]{1,0:T(8,128)(2,1)} %collective-permute-done.2), channel_id=1, source_target_pairs={{0,12},{4,8},{8,4},{12,0},{1,13},{5,9},{9,5},{13,1},{2,14},{6,10},... | collective-permute-start | bytes 1572872 | tf_op jit(solution)/shard_map/ppermute | solution.py:292
  29.8 44.3 %collective-permute-start.5 = (bf16[128,2048]{1,0:T(8,128)(2,1)}, bf16[128,2048]{1,0:T(8,128)(2,1)S(1)}, u32[]{:S(2)}, u32[]{:S(2)}) collective-permute-start(bf16[128,2048]{1,0:T(8,128)(2,1)} %collective-permute-done.2), channel_id=1, source_target_pairs={{0,8},{8,0},{1,9},{9,1},{2,10},{10,2},{3,11},{11,3},{4,12},{12,4},... | collective-permute-start | bytes 1572872 | tf_op jit(solution)/shard_map/ppermute | solution.py:286
  30.0 44.0 %collective-permute-start.4 = (bf16[128,2048]{1,0:T(8,128)(2,1)}, bf16[128,2048]{1,0:T(8,128)(2,1)S(1)}, u32[]{:S(2)}, u32[]{:S(2)}) collective-permute-start(bf16[128,2048]{1,0:T(8,128)(2,1)} %collective-permute-done.2), channel_id=1, source_target_pairs={{0,4},{4,0},{1,5},{5,1},{2,6},{6,2},{3,7},{7,3},{8,12},{12,8},{9,1... | collective-permute-start | bytes 1572872 | tf_op jit(solution)/shard_map/ppermute | solution.py:286
  31.4 77.7 %all-to-all-start = ((bf16[16,128,768]{2,1,0:T(8,128)(2,1)}), bf16[16,128,768]{2,1,0:T(8,128)(2,1)}, u32[]{:S(2)}, u32[]{:S(2)}) async-start(bf16[16,128,768]{2,1,0:T(8,128)(2,1)} %bitcast.14), calls=%async_computation | async-start | bytes 6291456 | tf_op jit(solution)/shard_map/all_to_all | solution.py:303
  37.7 2.1 %copy-start.15 = (bf16[128,2048]{1,0:T(8,128)(2,1)S(1)}, bf16[128,2048]{1,0:T(8,128)(2,1)}, u32[]{:S(2)}) copy-start(bf16[128,2048]{1,0:T(8,128)(2,1)} %param.9) | copy-start | bytes 1572868
  37.7 35.2 %collective-permute-start.3 = (bf16[128,2048]{1,0:T(8,128)(2,1)}, bf16[128,2048]{1,0:T(8,128)(2,1)S(1)}, u32[]{:S(2)}, u32[]{:S(2)}) collective-permute-start(bf16[128,2048]{1,0:T(8,128)(2,1)} %collective-permute-done.1), channel_id=1, source_target_pairs={{0,4},{4,0},{1,5},{5,1},{2,6},{6,2},{3,7},{7,3},{8,12},{12,8},{9,1... | collective-permute-start | bytes 1572872 | tf_op jit(solution)/shard_map/ppermute | solution.py:286
  40.9 33.4 %copy-start.3 = (bf16[2,192,2048]{2,1,0:T(8,128)(2,1)S(1)}, bf16[2,192,2048]{2,1,0:T(8,128)(2,1)}, u32[]{:S(2)}) copy-start(bf16[2,192,2048]{2,1,0:T(8,128)(2,1)} %copy-done.2) | copy-start | bytes 4718596
  74.2 6.8 %copy-start.4 = (bf16[8,128,2048]{2,1,0:T(8,128)(2,1)}, bf16[8,128,2048]{2,1,0:T(8,128)(2,1)S(1)}, u32[]{:S(2)}) copy-start(bf16[8,128,2048]{2,1,0:T(8,128)(2,1)S(1)} %bitcast_dynamic-update-slice_fusion) | copy-start | bytes 12582916
  74.2 7.2 %collective-permute-start.8 = (bf16[1024,2048]{1,0:T(8,128)(2,1)S(1)}, bf16[1024,2048]{1,0:T(8,128)(2,1)S(1)}, u32[]{:S(2)}, u32[]{:S(2)}) collective-permute-start(bf16[1024,2048]{1,0:T(8,128)(2,1)S(1)} %bitcast.29), channel_id=1, source_target_pairs={{0,1},{1,0},{2,3},{3,2},{4,5},{5,4},{6,7},{7,6},{8,9},{9,8},{10,11... | collective-permute-start | bytes 12582920 | tf_op jit(solution)/shard_map/ppermute | solution.py:372
  87.4 1.7 copy-start
  89.0 2.0 %copy-start.6 = (bf16[1024,2048]{1,0:T(8,128)(2,1)}, bf16[1024,2048]{1,0:T(8,128)(2,1)S(1)}, u32[]{:S(2)}) copy-start(bf16[1024,2048]{1,0:T(8,128)(2,1)S(1)} %collective-permute-done.8.refs_1_.refs_4_) | copy-start | bytes 12582916
  109.2 74.4 %all-to-all-start.1 = ((bf16[16,128,768]{2,1,0:T(8,128)(2,1)}), bf16[16,128,768]{2,1,0:T(8,128)(2,1)S(1)}, u32[]{:S(2)}, u32[]{:S(2)}) async-start(bf16[16,128,768]{2,1,0:T(8,128)(2,1)} %bitcast.28), calls=%async_computation.1 | async-start | bytes 6291456 | tf_op jit(solution)/shard_map/all_to_all | solution.py:303
  113.0 2.2 %copy-start.5 = (bf16[8,128,2048]{2,1,0:T(8,128)(2,1)S(1)}, bf16[8,128,2048]{2,1,0:T(8,128)(2,1)}, u32[]{:S(2)}) copy-start(bf16[8,128,2048]{2,1,0:T(8,128)(2,1)} %copy-done.4) | copy-start | bytes 12582916
  115.2 2.2 %copy-start.7 = (bf16[1024,2048]{1,0:T(8,128)(2,1)S(1)}, bf16[1024,2048]{1,0:T(8,128)(2,1)}, u32[]{:S(2)}) copy-start(bf16[1024,2048]{1,0:T(8,128)(2,1)} %copy-done.6) | copy-start | bytes 12582916
  117.4 47.8 %copy-start.12 = (f32[2,192,2048]{2,1,0:T(8,128)S(1)}, f32[2,192,2048]{2,1,0:T(8,128)}, u32[]{:S(2)}) copy-start(f32[2,192,2048]{2,1,0:T(8,128)} %param.15) | copy-start | bytes 9437188
  117.4 47.8 %copy-start.13 = (bf16[2,192,2048]{2,1,0:T(8,128)(2,1)S(1)}, bf16[2,192,2048]{2,1,0:T(8,128)(2,1)}, u32[]{:S(2)}) copy-start(bf16[2,192,2048]{2,1,0:T(8,128)(2,1)} %param.17) | copy-start | bytes 4718596
  117.4 47.8 %copy-start.14 = (bf16[2,192,2048]{2,1,0:T(8,128)(2,1)S(1)}, bf16[2,192,2048]{2,1,0:T(8,128)(2,1)}, u32[]{:S(2)}) copy-start(bf16[2,192,2048]{2,1,0:T(8,128)(2,1)} %param.16) | copy-start | bytes 4718596
  129.1 36.0 %collective-permute-start.9 = (bf16[2,192,2048]{2,1,0:T(8,128)(2,1)S(1)}, bf16[2,192,2048]{2,1,0:T(8,128)(2,1)S(1)}, u32[]{:S(2)}, u32[]{:S(2)}) collective-permute-start(bf16[2,192,2048]{2,1,0:T(8,128)(2,1)S(1)} %get-tuple-element.34), channel_id=1, source_target_pairs={{0,2},{2,0},{1,3},{3,1},{4,6},{6,4},{5,7},{7,5},{8,10},{10,8},{9,1... | collective-permute-start | bytes 4718600 | tf_op jit(solution)/shard_map/ppermute | solution.py:443

commit v5 on v4

--- a/solution.py
+++ b/solution.py
@@ -345,11 +345,15 @@
     dy = {(0, 0, 0): out_grad}
     for b in range(1, halves):
         dy[b, 0, 0] = shift(out_grad, "half", b)
+    after, weight_part = lax.optimization_barrier((out_grad, weight_part))
     for i in range(1, line):
-        dy[0, i, 0] = shift(out_grad, "line", i)
+        dy[0, i, 0] = shift(after, "line", i)
     for j in range(1, pair):
-        dy[0, 0, j] = shift(out_grad, "pair", j)
-    dy, spread = lax.optimization_barrier((dy, spread))
+        dy[0, 0, j] = shift(after, "pair", j)
+    keys = [key for key in sorted(dy, reverse=True) if not key[1]]
+    held = lax.optimization_barrier([spread] + [dy[key] for key in keys])
+    spread = held[0]
+    dy.update(zip(keys, held[1:]))
     hid = exchange(spread)
     for b in range(1, halves):
         for i in range(1, line):

time: 189 us -> 188 us (level)
  waiting for transfers between devices: 109 us -> 106 us
    ppermute x6, waiting for transfers between devices: 42.7 us -> 40.2 us  [shift(): return lax.ppermute(x, axis, [(i, (i + by) % size) for i in range(size)])]
    unnamed x32 -> x30, local copies, waits for them, and re-layouts: 10.8 us -> 10.8 us
  transfers between devices with their start and end apart: 12 -> 12, of which waited for: 7 -> 6; matrix products, arithmetic and copies ran while one was open for 5% -> 6% of each run, Pallas kernels for 16% -> 16%
where the time goes in v5:
time: 188 us; the launch traced here: 187 us
  waiting for transfers between devices  106 us (56%)
  Pallas kernels  34.8 us (19%)
  starting transfers between devices  23.8 us (13%)
  local copies, waits for them, and re-layouts  16 us (9%)
  other arithmetic  5.62 us (3%)
    ppermute x6, waiting for transfers between devices, shift(): return lax.ppermute(x, axis, [(i, (i + by) % size) for i in range(size)])  40.2 us
    ppermute x1, waiting for transfers between devices, dense_body(): lax.ppermute(grads[o], 'fsdp', [(f, (f + o) % fsdp) for f in range(fsdp)])  34.6 us
    all_to_all x2, waiting for transfers between devices, exchange(): lax.all_to_all(x, ('replica', 'half', 'line', 'pair'), split_axis=0, conc...  30.7 us
    pallas_call x2, Pallas kernels, dense_body(): pl.pallas_call(lambda *refs: back_kernel((fsdp, replica), *refs), out_sha...  12.6 us
    pallas_call x1, Pallas kernels, dense_body(): pl.pallas_call(lambda *refs: gradient_kernel((fsdp, replica), *refs), out...  11.7 us
    all_to_all x2, starting transfers between devices, exchange(): lax.all_to_all(x, ('replica', 'half', 'line', 'pair'), split_axis=0, conc...  11 us
    unnamed x30, local copies, waits for them, and re-layouts  10.8 us
    ppermute x6, starting transfers between devices, shift(): return lax.ppermute(x, axis, [(i, (i + by) % size) for i in range(size)])  7.34 us
  transfers between devices with their start and end apart: 12, of which 6 were waited for; matrix products, arithmetic and copies ran while one was open for 6% of the time, Pallas kernels for 16%

profile of v5, /device:TPU:8, one launch (start us, length us, event | category | flops | bytes accessed | tf_op | source)
XLA Modules:
  0.0 187.0 jit_solution(18355616636051067726)
XLA Ops:
  0.6 2.7 %collective-permute-start = (bf16[128,2048]{1,0:T(8,128)(2,1)}, bf16[128,2048]{1,0:T(8,128)(2,1)}, u32[]{:S(2)}, u32[]{:S(2)}) collective-permute-start(bf16[128,2048]{1,0:T(8,128)(2,1)} %param.9), channel_id=1, source_target_pairs={{0,16},{16,0},{1,17},{17,1},{2,18},{18,2},{3,19},{19,3},{4,20},{20... | collective-permute-start | bytes 1572872 | tf_op jit(solution)/shard_map/ppermute | solution.py:286
  3.4 1.9 %copy-done.8 = bf16[2,384,2048]{2,1,0:T(8,128)(2,1)S(1)} copy-done((bf16[2,384,2048]{2,1,0:T(8,128)(2,1)S(1)}, bf16[2,384,2048]{2,1,0:T(8,128)(2,1)}, u32[]{:S(2)}) %copy-start.8) | copy-done | bytes 3145752
  5.3 0.8 copy-done.9
  6.1 2.0 %scale.1.refs_2_ = bf16[2,192,2048]{2,1,0:T(8,128)(2,1)S(1)} custom-call(s32[3]{0:T(128)S(1)} %pad_add_fusion.refs_0_.place, bf16[2,384,2048]{2,1,0:T(8,128)(2,1)S(1)} %copy-done.8, s32[2,16,384]{2,1,0:T(8,128)S(1)} %bitcast.32), custom_call_target="tpu_custom_call" | custom-call | tf_op jit(solution)/shard_map/scale/pallas_call | solution.py:307
  8.0 1.6 collective-permute-start.1
  10.1 1.5 collective-permute-start.7
  11.6 3.9 %spread.1 = bf16[2,8,128,768]{3,2,1,0:T(8,128)(2,1)} custom-call(s32[3]{0:T(128)S(1)} %pad_add_fusion.refs_0_.place, s32[8,128]{1,0:T(8,128)S(1)} %bitcast.33, f32[8,128]{1,0:T(8,128)S(1)} %bitcast.35, bf16[128,8,768]{2,1,0:T(8,128)(2,1)S(1)} %copy-done.1), custom_call_target="tpu_custom_call" | custom-call | tf_op jit(solution)/shard_map/spread/pallas_call | solution.py:331
  15.5 10.4 %collective-permute-done = bf16[128,2048]{1,0:T(8,128)(2,1)} collective-permute-done((bf16[128,2048]{1,0:T(8,128)(2,1)}, bf16[128,2048]{1,0:T(8,128)(2,1)}, u32[]{:S(2)}, u32[]{:S(2)}) %collective-permute-start) | collective-permute-done | bytes 524320 | tf_op jit(solution)/shard_map/ppermute | solution.py:286
  26.0 2.4 %collective-permute-start.6 = (bf16[128,2048]{1,0:T(8,128)(2,1)}, bf16[128,2048]{1,0:T(8,128)(2,1)S(1)}, u32[]{:S(2)}, u32[]{:S(2)}) collective-permute-start(bf16[128,2048]{1,0:T(8,128)(2,1)} %collective-permute-done), channel_id=1, source_target_pairs={{0,12},{4,8},{8,4},{12,0},{1,13},{5,9},{9,5},{13,1},{2,14},{6,10},... | collective-permute-start | bytes 1572872 | tf_op jit(solution)/shard_map/ppermute | solution.py:292
  28.3 0.6 collective-permute-start.5
  29.5 7.1 %all-to-all-start = ((bf16[16,128,768]{2,1,0:T(8,128)(2,1)}), bf16[16,128,768]{2,1,0:T(8,128)(2,1)}, u32[]{:S(2)}, u32[]{:S(2)}) async-start(bf16[16,128,768]{2,1,0:T(8,128)(2,1)} %bitcast.14), calls=%async_computation | async-start | bytes 6291456 | tf_op jit(solution)/shard_map/all_to_all | solution.py:303
  36.6 0.5 broadcast_in_dim.28
  37.1 1.1 bitcast_dynamic-update-slice_fusion.7
  38.2 1.5 collective-permute-start.3
  39.8 1.1 bitcast_dynamic-update-slice_fusion.6
  40.9 1.2 bitcast_dynamic-update-slice_fusion.5
  42.1 29.7 %collective-permute-done.3 = bf16[128,2048]{1,0:T(8,128)(2,1)S(1)} collective-permute-done((bf16[128,2048]{1,0:T(8,128)(2,1)}, bf16[128,2048]{1,0:T(8,128)(2,1)S(1)}, u32[]{:S(2)}, u32[]{:S(2)}) %collective-permute-start.3) | collective-permute-done | bytes 524320 | tf_op jit(solution)/shard_map/ppermute | solution.py:286
  71.9 1.1 bitcast_dynamic-update-slice_fusion.3
  73.3 6.7 %back.2.refs_4_ = bf16[2,8,128,768]{3,2,1,0:T(8,128)(2,1)S(1)} custom-call(s32[3]{0:T(128)S(1)} %pad_add_fusion.refs_0_.place, bf16[1024,2048]{1,0:T(8,128)(2,1)S(1)} %bitcast.30, bf16[2,192,2048]{2,1,0:T(8,128)(2,1)S(1)} %copy-done.3, bf16[2,192,2048]{2,1,0:T(8,128)(2,1)} %collective-permute-done.7.refs_3_), custom_call_target="tpu_custom_call" | custom-call | flops 3221225472 | bytes 5767168 | tf_op jit(solution)/shard_map/back/pallas_call | solution.py:385
  80.4 5.9 %back.3 = bf16[2,8,128,768]{3,2,1,0:T(8,128)(2,1)S(1)} custom-call(s32[3]{0:T(128)S(1)} %pad_add_fusion.refs_0_.place, bf16[1024,2048]{1,0:T(8,128)(2,1)S(1)} %collective-permute-done.8.refs_1_.refs_4_, bf16[2,192,2048]{2,1,0:T(8,128)(2,1)S(1)} %copy-done.3, bf16[2,192,2048]{2,1,0:T(8,128)(2,1)} %collective-permute-done.7.refs_3_, ...), custom_call_target="tpu_custom_call", output_to_operand_aliasing={{}: (4, {})} | custom-call | flops 3221225472 | bytes 5767168 | tf_op jit(solution)/shard_map/back/pallas_call | solution.py:385
  86.3 1.7 copy-done
  88.0 2.0 %copy-done.6 = bf16[1024,2048]{1,0:T(8,128)(2,1)} copy-done((bf16[1024,2048]{1,0:T(8,128)(2,1)}, bf16[1024,2048]{1,0:T(8,128)(2,1)S(1)}, u32[]{:S(2)}) %copy-start.6) | copy-done | bytes 4194328
  90.0 17.9 %all-to-all-done = bf16[16,128,768]{2,1,0:T(8,128)(2,1)} async-done(((bf16[16,128,768]{2,1,0:T(8,128)(2,1)}), bf16[16,128,768]{2,1,0:T(8,128)(2,1)}, u32[]{:S(2)}, u32[]{:S(2)}) %all-to-all-start) | async-done | bytes 3145760 | tf_op jit(solution)/shard_map/all_to_all | solution.py:303
  107.9 3.8 %all-to-all-start.1 = ((bf16[16,128,768]{2,1,0:T(8,128)(2,1)}), bf16[16,128,768]{2,1,0:T(8,128)(2,1)S(1)}, u32[]{:S(2)}, u32[]{:S(2)}) async-start(bf16[16,128,768]{2,1,0:T(8,128)(2,1)} %bitcast.28), calls=%async_computation.1 | async-start | bytes 6291456 | tf_op jit(solution)/shard_map/all_to_all | solution.py:303
  111.7 2.2 %copy-done.5 = bf16[8,128,2048]{2,1,0:T(8,128)(2,1)S(1)} copy-done((bf16[8,128,2048]{2,1,0:T(8,128)(2,1)S(1)}, bf16[8,128,2048]{2,1,0:T(8,128)(2,1)}, u32[]{:S(2)}) %copy-start.5) | copy-done | bytes 4194328
  113.9 2.2 %copy-done.7 = bf16[1024,2048]{1,0:T(8,128)(2,1)S(1)} copy-done((bf16[1024,2048]{1,0:T(8,128)(2,1)S(1)}, bf16[1024,2048]{1,0:T(8,128)(2,1)}, u32[]{:S(2)}) %copy-start.7) | copy-done | bytes 4194328
  116.1 11.7 %gradient.1 = (f32[2,192,2048]{2,1,0:T(8,128)S(1)}, bf16[2,192,2048]{2,1,0:T(8,128)(2,1)S(1)}) custom-call(s32[3]{0:T(128)S(1)} %pad_add_fusion.refs_0_.place, bf16[2,8,128,768]{3,2,1,0:T(8,128)(2,1)} %bitcast.15.refs_1_.refs_2_, bf16[2,8,128,768]{3,2,1,0:T(8,128)(2,1)} %bitcast.15.refs_1_.refs_2_, bf16[1024,2048]{1,0:T(8,128)(2,1)S(1)} %bitcast.31, ...), custom_call_target="tpu_custom_call" | custom-call | flops 6442450944 | bytes 11534336 | tf_op jit(solution)/shard_map/gradient/pallas_call | solution.py:417
  127.9 1.6 collective-permute-start.9
  129.4 34.6 %collective-permute-done.9 = bf16[2,192,2048]{2,1,0:T(8,128)(2,1)S(1)} collective-permute-done((bf16[2,192,2048]{2,1,0:T(8,128)(2,1)S(1)}, bf16[2,192,2048]{2,1,0:T(8,128)(2,1)S(1)}, u32[]{:S(2)}, u32[]{:S(2)}) %collective-permute-start.9) | collective-permute-done | bytes 1572896 | tf_op jit(solution)/shard_map/ppermute | solution.py:447
  164.0 5.5 %fusion.2 = (bf16[2,192,2048]{2,1,0:T(8,128)(2,1)}, f32[2,192,2048]{2,1,0:T(8,128)}, bf16[2,192,2048]{2,1,0:T(8,128)(2,1)}) fusion(f32[2,192,2048]{2,1,0:T(8,128)S(1)} %get-tuple-element.35, bf16[2,192,2048]{2,1,0:T(8,128)(2,1)S(1)} %collective-permute-done.9, bf16[2,192,2048]{2,1,0:T(8,128)(2,1)S(1)} %copy-done.13, f32[2,192,2048]{2,1,0:T(8,128)S(1)} %copy-done.12, ...), kind=kLoop, calls=%fused_computation.6 | loop fusion | flops 16515072 | bytes 17301504 | tf_op jit(solution)/shard_map/convert_element_type | solution.py:455
  169.6 12.9 %all-to-all-done.1 = bf16[16,128,768]{2,1,0:T(8,128)(2,1)S(1)} async-done(((bf16[16,128,768]{2,1,0:T(8,128)(2,1)}), bf16[16,128,768]{2,1,0:T(8,128)(2,1)S(1)}, u32[]{:S(2)}, u32[]{:S(2)}) %all-to-all-start.1) | async-done | bytes 3145760 | tf_op jit(solution)/shard_map/all_to_all | solution.py:303
  182.4 4.6 %collect.1 = (bf16[128,8,768]{2,1,0:T(8,128)(2,1)}, f32[8,128]{1,0:T(8,128)}) custom-call(s32[8,128]{1,0:T(8,128)S(1)} %bitcast.34, f32[8,128]{1,0:T(8,128)S(1)} %bitcast.36, bf16[128,8,768]{2,1,0:T(8,128)(2,1)} %refs_2_.1, bf16[2,8,128,768]{3,2,1,0:T(8,128)(2,1)S(1)} %bitcast.27), custom_call_target="tpu_custom_call" | custom-call | tf_op jit(solution)/shard_map/collect/pallas_call | solution.py:457
  (39 shorter events, 1.8 us)
Async XLA Ops:
  0.6 10.9 %copy-start.1 = (bf16[128,8,768]{2,1,0:T(8,128)(2,1)S(1)}, bf16[128,8,768]{2,1,0:T(8,128)(2,1)}, u32[]{:S(2)}) copy-start(bf16[128,8,768]{2,1,0:T(8,128)(2,1)} %refs_2_.1) | copy-start | bytes 4718596
  0.6 25.3 %collective-permute-start = (bf16[128,2048]{1,0:T(8,128)(2,1)}, bf16[128,2048]{1,0:T(8,128)(2,1)}, u32[]{:S(2)}, u32[]{:S(2)}) collective-permute-start(bf16[128,2048]{1,0:T(8,128)(2,1)} %param.9), channel_id=1, source_target_pairs={{0,16},{16,0},{1,17},{17,1},{2,18},{18,2},{3,19},{19,3},{4,20},{20... | collective-permute-start | bytes 1572872 | tf_op jit(solution)/shard_map/ppermute | solution.py:286
  3.4 1.9 %copy-start.8 = (bf16[2,384,2048]{2,1,0:T(8,128)(2,1)S(1)}, bf16[2,384,2048]{2,1,0:T(8,128)(2,1)}, u32[]{:S(2)}) copy-start(bf16[2,384,2048]{2,1,0:T(8,128)(2,1)} %values.1) | copy-start | bytes 9437188
  5.3 0.8 copy-start.9
  6.1 5.5 %copy-start.10 = (s32[128,8]{0,1:T(8,128)S(1)}, s32[128,8]{0,1:T(8,128)}, u32[]{:S(2)}) copy-start(s32[128,8]{0,1:T(8,128)} %param.12) | copy-start | bytes 12292
  6.1 5.5 %copy-start.11 = (f32[128,8]{0,1:T(8,128)S(1)}, f32[128,8]{0,1:T(8,128)}, u32[]{:S(2)}) copy-start(f32[128,8]{0,1:T(8,128)} %param.11) | copy-start | bytes 12292
  8.0 21.4 %copy-start.2 = (bf16[2,192,2048]{2,1,0:T(8,128)(2,1)}, bf16[2,192,2048]{2,1,0:T(8,128)(2,1)S(1)}, u32[]{:S(2)}) copy-start(bf16[2,192,2048]{2,1,0:T(8,128)(2,1)S(1)} %scale.1.refs_2_) | copy-start | bytes 4718596
  8.0 17.9 %collective-permute-start.1 = (bf16[128,2048]{1,0:T(8,128)(2,1)}, bf16[128,2048]{1,0:T(8,128)(2,1)}, u32[]{:S(2)}, u32[]{:S(2)}) collective-permute-start(bf16[128,2048]{1,0:T(8,128)(2,1)} %param.9), channel_id=1, source_target_pairs={{0,4},{4,0},{1,5},{5,1},{2,6},{6,2},{3,7},{7,3},{8,12},{12,8},{9,1... | collective-permute-start | bytes 1572872 | tf_op jit(solution)/shard_map/ppermute | solution.py:286
  9.6 28.6 %collective-permute-start.2 = (bf16[128,2048]{1,0:T(8,128)(2,1)}, bf16[128,2048]{1,0:T(8,128)(2,1)}, u32[]{:S(2)}, u32[]{:S(2)}) collective-permute-start(bf16[128,2048]{1,0:T(8,128)(2,1)} %param.9), channel_id=1, source_target_pairs={{0,8},{8,0},{1,9},{9,1},{2,10},{10,2},{3,11},{11,3},{4,12},{12,4},... | collective-permute-start | bytes 1572872 | tf_op jit(solution)/shard_map/ppermute | solution.py:286
  10.1 63.1 %collective-permute-start.7 = (bf16[2,192,2048]{2,1,0:T(8,128)(2,1)S(1)}, bf16[2,192,2048]{2,1,0:T(8,128)(2,1)}, u32[]{:S(2)}, u32[]{:S(2)}) collective-permute-start(bf16[2,192,2048]{2,1,0:T(8,128)(2,1)S(1)} %scale.1.refs_2_), channel_id=1, source_target_pairs={{0,2},{2,0},{1,3},{3,1},{4,6},{6,4},{5,7},{7,5},{8,10},{10,8},{9,1... | collective-permute-start | bytes 4718600 | tf_op jit(solution)/shard_map/ppermute | solution.py:362
  26.0 47.1 %collective-permute-start.6 = (bf16[128,2048]{1,0:T(8,128)(2,1)}, bf16[128,2048]{1,0:T(8,128)(2,1)S(1)}, u32[]{:S(2)}, u32[]{:S(2)}) collective-permute-start(bf16[128,2048]{1,0:T(8,128)(2,1)} %collective-permute-done), channel_id=1, source_target_pairs={{0,12},{4,8},{8,4},{12,0},{1,13},{5,9},{9,5},{13,1},{2,14},{6,10},... | collective-permute-start | bytes 1572872 | tf_op jit(solution)/shard_map/ppermute | solution.py:292
  28.3 44.7 %collective-permute-start.5 = (bf16[128,2048]{1,0:T(8,128)(2,1)}, bf16[128,2048]{1,0:T(8,128)(2,1)S(1)}, u32[]{:S(2)}, u32[]{:S(2)}) collective-permute-start(bf16[128,2048]{1,0:T(8,128)(2,1)} %collective-permute-done), channel_id=1, source_target_pairs={{0,8},{8,0},{1,9},{9,1},{2,10},{10,2},{3,11},{11,3},{4,12},{12,4},... | collective-permute-start | bytes 1572872 | tf_op jit(solution)/shard_map/ppermute | solution.py:286
  28.9 44.0 %collective-permute-start.4 = (bf16[128,2048]{1,0:T(8,128)(2,1)}, bf16[128,2048]{1,0:T(8,128)(2,1)S(1)}, u32[]{:S(2)}, u32[]{:S(2)}) collective-permute-start(bf16[128,2048]{1,0:T(8,128)(2,1)} %collective-permute-done), channel_id=1, source_target_pairs={{0,4},{4,0},{1,5},{5,1},{2,6},{6,2},{3,7},{7,3},{8,12},{12,8},{9,1... | collective-permute-start | bytes 1572872 | tf_op jit(solution)/shard_map/ppermute | solution.py:286
  29.5 78.4 %all-to-all-start = ((bf16[16,128,768]{2,1,0:T(8,128)(2,1)}), bf16[16,128,768]{2,1,0:T(8,128)(2,1)}, u32[]{:S(2)}, u32[]{:S(2)}) async-start(bf16[16,128,768]{2,1,0:T(8,128)(2,1)} %bitcast.14), calls=%async_computation | async-start | bytes 6291456 | tf_op jit(solution)/shard_map/all_to_all | solution.py:303
  38.2 33.6 %collective-permute-start.3 = (bf16[128,2048]{1,0:T(8,128)(2,1)}, bf16[128,2048]{1,0:T(8,128)(2,1)S(1)}, u32[]{:S(2)}, u32[]{:S(2)}) collective-permute-start(bf16[128,2048]{1,0:T(8,128)(2,1)} %collective-permute-done.2), channel_id=1, source_target_pairs={{0,4},{4,0},{1,5},{5,1},{2,6},{6,2},{3,7},{7,3},{8,12},{12,8},{9,1... | collective-permute-start | bytes 1572872 | tf_op jit(solution)/shard_map/ppermute | solution.py:286
  40.8 32.4 %copy-start.3 = (bf16[2,192,2048]{2,1,0:T(8,128)(2,1)S(1)}, bf16[2,192,2048]{2,1,0:T(8,128)(2,1)}, u32[]{:S(2)}) copy-start(bf16[2,192,2048]{2,1,0:T(8,128)(2,1)} %copy-done.2) | copy-start | bytes 4718596
  73.2 6.8 %copy-start.4 = (bf16[8,128,2048]{2,1,0:T(8,128)(2,1)}, bf16[8,128,2048]{2,1,0:T(8,128)(2,1)S(1)}, u32[]{:S(2)}) copy-start(bf16[8,128,2048]{2,1,0:T(8,128)(2,1)S(1)} %bitcast_dynamic-update-slice_fusion) | copy-start | bytes 12582916
  73.2 7.2 %collective-permute-start.8 = (bf16[1024,2048]{1,0:T(8,128)(2,1)S(1)}, bf16[1024,2048]{1,0:T(8,128)(2,1)S(1)}, u32[]{:S(2)}, u32[]{:S(2)}) collective-permute-start(bf16[1024,2048]{1,0:T(8,128)(2,1)S(1)} %bitcast.29), channel_id=1, source_target_pairs={{0,1},{1,0},{2,3},{3,2},{4,5},{5,4},{6,7},{7,6},{8,9},{9,8},{10,11... | collective-permute-start | bytes 12582920 | tf_op jit(solution)/shard_map/ppermute | solution.py:376
  86.3 1.7 copy-start
  88.0 2.0 %copy-start.6 = (bf16[1024,2048]{1,0:T(8,128)(2,1)}, bf16[1024,2048]{1,0:T(8,128)(2,1)S(1)}, u32[]{:S(2)}) copy-start(bf16[1024,2048]{1,0:T(8,128)(2,1)S(1)} %collective-permute-done.8.refs_1_.refs_4_) | copy-start | bytes 12582916
  107.9 74.5 %all-to-all-start.1 = ((bf16[16,128,768]{2,1,0:T(8,128)(2,1)}), bf16[16,128,768]{2,1,0:T(8,128)(2,1)S(1)}, u32[]{:S(2)}, u32[]{:S(2)}) async-start(bf16[16,128,768]{2,1,0:T(8,128)(2,1)} %bitcast.28), calls=%async_computation.1 | async-start | bytes 6291456 | tf_op jit(solution)/shard_map/all_to_all | solution.py:303
  111.7 2.2 %copy-start.5 = (bf16[8,128,2048]{2,1,0:T(8,128)(2,1)S(1)}, bf16[8,128,2048]{2,1,0:T(8,128)(2,1)}, u32[]{:S(2)}) copy-start(bf16[8,128,2048]{2,1,0:T(8,128)(2,1)} %copy-done.4) | copy-start | bytes 12582916
  113.9 2.2 %copy-start.7 = (bf16[1024,2048]{1,0:T(8,128)(2,1)S(1)}, bf16[1024,2048]{1,0:T(8,128)(2,1)}, u32[]{:S(2)}) copy-start(bf16[1024,2048]{1,0:T(8,128)(2,1)} %copy-done.6) | copy-start | bytes 12582916
  116.1 47.9 %copy-start.12 = (f32[2,192,2048]{2,1,0:T(8,128)S(1)}, f32[2,192,2048]{2,1,0:T(8,128)}, u32[]{:S(2)}) copy-start(f32[2,192,2048]{2,1,0:T(8,128)} %param.15) | copy-start | bytes 9437188
  116.1 47.9 %copy-start.13 = (bf16[2,192,2048]{2,1,0:T(8,128)(2,1)S(1)}, bf16[2,192,2048]{2,1,0:T(8,128)(2,1)}, u32[]{:S(2)}) copy-start(bf16[2,192,2048]{2,1,0:T(8,128)(2,1)} %param.17) | copy-start | bytes 4718596
  116.1 47.9 %copy-start.14 = (bf16[2,192,2048]{2,1,0:T(8,128)(2,1)S(1)}, bf16[2,192,2048]{2,1,0:T(8,128)(2,1)}, u32[]{:S(2)}) copy-start(bf16[2,192,2048]{2,1,0:T(8,128)(2,1)} %param.16) | copy-start | bytes 4718596
  127.9 36.1 %collective-permute-start.9 = (bf16[2,192,2048]{2,1,0:T(8,128)(2,1)S(1)}, bf16[2,192,2048]{2,1,0:T(8,128)(2,1)S(1)}, u32[]{:S(2)}, u32[]{:S(2)}) collective-permute-start(bf16[2,192,2048]{2,1,0:T(8,128)(2,1)S(1)} %get-tuple-element.36), channel_id=1, source_target_pairs={{0,2},{2,0},{1,3},{3,1},{4,6},{6,4},{5,7},{7,5},{8,10},{10,8},{9,1... | collective-permute-start | bytes 4718600 | tf_op jit(solution)/shard_map/ppermute | solution.py:447

commit v6 on v5

--- a/solution.py
+++ b/solution.py
@@ -179,20 +179,24 @@
         inside = slice(part * tokens, (part + 1) * tokens)
         at = rows_of_part(step, part, tokens)
         match = route_match(turned[0, at], groups * here)
-        shares = []
-        for r in range(replica):
-            rows = jnp.concatenate(
-                [
-                    backs[r, g, inside, e * fsdp * unit : (e + 1) * fsdp * unit]
-                    for g in range(groups)
-                    for e in range(here)
-                ],
-                axis=0,
-            )
-            shares.append(jnp.dot(match, rows, preferred_element_type=jnp.float32))
+        rows = jnp.concatenate(
+            [
+                jnp.concatenate(
+                    [
+                        backs[r, g, inside, e * fsdp * unit : (e + 1) * fsdp * unit]
+                        for r in range(replica)
+                    ],
+                    axis=1,
+                )
+                for g in range(groups)
+                for e in range(here)
+            ],
+            axis=0,
+        )
+        found = jnp.dot(match, rows, preferred_element_type=jnp.float32)
         back = jnp.concatenate(
             [
-                shares[r][:, f * unit : (f + 1) * unit]
+                found[:, (r * fsdp + f) * unit : (r * fsdp + f + 1) * unit]
                 for f in range(fsdp)
                 for r in range(replica)
             ],

time: 188 us -> 187 us (level)
  no operation moved by 1% of the time
where the time goes in v6:
time: 187 us; the launch traced here: 186 us
  waiting for transfers between devices  106 us (57%)
  Pallas kernels  34.2 us (18%)
  starting transfers between devices  23.6 us (13%)
  local copies, waits for them, and re-layouts  16 us (9%)
  other arithmetic  5.62 us (3%)
    ppermute x6, waiting for transfers between devices, shift(): return lax.ppermute(x, axis, [(i, (i + by) % size) for i in range(size)])  40.2 us
    ppermute x1, waiting for transfers between devices, dense_body(): lax.ppermute(grads[o], 'fsdp', [(f, (f + o) % fsdp) for f in range(fsdp)])  34.8 us
    all_to_all x2, waiting for transfers between devices, exchange(): lax.all_to_all(x, ('replica', 'half', 'line', 'pair'), split_axis=0, conc...  30.7 us
    pallas_call x2, Pallas kernels, dense_body(): pl.pallas_call(lambda *refs: back_kernel((fsdp, replica), *refs), out_sha...  12.6 us
    pallas_call x1, Pallas kernels, dense_body(): pl.pallas_call(lambda *refs: gradient_kernel((fsdp, replica), *refs), out...  11.7 us
    unnamed x30, local copies, waits for them, and re-layouts  10.8 us
    all_to_all x2, starting transfers between devices, exchange(): lax.all_to_all(x, ('replica', 'half', 'line', 'pair'), split_axis=0, conc...  10.8 us
    ppermute x6, starting transfers between devices, shift(): return lax.ppermute(x, axis, [(i, (i + by) % size) for i in range(size)])  7.34 us
  transfers between devices with their start and end apart: 12, of which 6 were waited for; matrix products, arithmetic and copies ran while one was open for 6% of the time, Pallas kernels for 16%

profile of v6, /device:TPU:8, one launch (start us, length us, event | category | flops | bytes accessed | tf_op | source)
XLA Modules:
  0.0 186.4 jit_solution(13769903248594020653)
XLA Ops:
  0.6 2.7 %collective-permute-start = (bf16[128,2048]{1,0:T(8,128)(2,1)}, bf16[128,2048]{1,0:T(8,128)(2,1)}, u32[]{:S(2)}, u32[]{:S(2)}) collective-permute-start(bf16[128,2048]{1,0:T(8,128)(2,1)} %param.9), channel_id=1, source_target_pairs={{0,16},{16,0},{1,17},{17,1},{2,18},{18,2},{3,19},{19,3},{4,20},{20... | collective-permute-start | bytes 1572872 | tf_op jit(solution)/shard_map/ppermute | solution.py:290
  3.4 1.9 %copy-done.8 = bf16[2,384,2048]{2,1,0:T(8,128)(2,1)S(1)} copy-done((bf16[2,384,2048]{2,1,0:T(8,128)(2,1)S(1)}, bf16[2,384,2048]{2,1,0:T(8,128)(2,1)}, u32[]{:S(2)}) %copy-start.8) | copy-done | bytes 3145752
  5.3 0.8 copy-done.9
  6.1 2.0 %scale.1.refs_2_ = bf16[2,192,2048]{2,1,0:T(8,128)(2,1)S(1)} custom-call(s32[3]{0:T(128)S(1)} %pad_add_fusion.refs_0_.place, bf16[2,384,2048]{2,1,0:T(8,128)(2,1)S(1)} %copy-done.8, s32[2,16,384]{2,1,0:T(8,128)S(1)} %bitcast.32), custom_call_target="tpu_custom_call" | custom-call | tf_op jit(solution)/shard_map/scale/pallas_call | solution.py:311
  8.0 1.6 collective-permute-start.1
  10.1 1.5 collective-permute-start.7
  11.6 3.9 %spread.1 = bf16[2,8,128,768]{3,2,1,0:T(8,128)(2,1)} custom-call(s32[3]{0:T(128)S(1)} %pad_add_fusion.refs_0_.place, s32[8,128]{1,0:T(8,128)S(1)} %bitcast.33, f32[8,128]{1,0:T(8,128)S(1)} %bitcast.35, bf16[128,8,768]{2,1,0:T(8,128)(2,1)S(1)} %copy-done.1), custom_call_target="tpu_custom_call" | custom-call | tf_op jit(solution)/shard_map/spread/pallas_call | solution.py:335
  15.5 10.4 %collective-permute-done = bf16[128,2048]{1,0:T(8,128)(2,1)} collective-permute-done((bf16[128,2048]{1,0:T(8,128)(2,1)}, bf16[128,2048]{1,0:T(8,128)(2,1)}, u32[]{:S(2)}, u32[]{:S(2)}) %collective-permute-start) | collective-permute-done | bytes 524320 | tf_op jit(solution)/shard_map/ppermute | solution.py:290
  26.0 2.4 %collective-permute-start.6 = (bf16[128,2048]{1,0:T(8,128)(2,1)}, bf16[128,2048]{1,0:T(8,128)(2,1)S(1)}, u32[]{:S(2)}, u32[]{:S(2)}) collective-permute-start(bf16[128,2048]{1,0:T(8,128)(2,1)} %collective-permute-done), channel_id=1, source_target_pairs={{0,12},{4,8},{8,4},{12,0},{1,13},{5,9},{9,5},{13,1},{2,14},{6,10},... | collective-permute-start | bytes 1572872 | tf_op jit(solution)/shard_map/ppermute | solution.py:296
  28.3 0.6 collective-permute-start.5
  29.5 7.1 %all-to-all-start = ((bf16[16,128,768]{2,1,0:T(8,128)(2,1)}), bf16[16,128,768]{2,1,0:T(8,128)(2,1)}, u32[]{:S(2)}, u32[]{:S(2)}) async-start(bf16[16,128,768]{2,1,0:T(8,128)(2,1)} %bitcast.14), calls=%async_computation | async-start | bytes 6291456 | tf_op jit(solution)/shard_map/all_to_all | solution.py:307
  36.6 0.5 broadcast_in_dim.28
  37.1 1.1 bitcast_dynamic-update-slice_fusion.7
  38.2 1.5 collective-permute-start.3
  39.8 1.1 bitcast_dynamic-update-slice_fusion.6
  40.9 1.2 bitcast_dynamic-update-slice_fusion.5
  42.1 29.7 %collective-permute-done.3 = bf16[128,2048]{1,0:T(8,128)(2,1)S(1)} collective-permute-done((bf16[128,2048]{1,0:T(8,128)(2,1)}, bf16[128,2048]{1,0:T(8,128)(2,1)S(1)}, u32[]{:S(2)}, u32[]{:S(2)}) %collective-permute-start.3) | collective-permute-done | bytes 524320 | tf_op jit(solution)/shard_map/ppermute | solution.py:290
  71.9 1.1 bitcast_dynamic-update-slice_fusion.3
  73.3 6.7 %back.2.refs_4_ = bf16[2,8,128,768]{3,2,1,0:T(8,128)(2,1)S(1)} custom-call(s32[3]{0:T(128)S(1)} %pad_add_fusion.refs_0_.place, bf16[1024,2048]{1,0:T(8,128)(2,1)S(1)} %bitcast.30, bf16[2,192,2048]{2,1,0:T(8,128)(2,1)S(1)} %copy-done.3, bf16[2,192,2048]{2,1,0:T(8,128)(2,1)} %collective-permute-done.7.refs_3_), custom_call_target="tpu_custom_call" | custom-call | flops 3221225472 | bytes 5767168 | tf_op jit(solution)/shard_map/back/pallas_call | solution.py:389
  80.4 5.9 %back.3 = bf16[2,8,128,768]{3,2,1,0:T(8,128)(2,1)S(1)} custom-call(s32[3]{0:T(128)S(1)} %pad_add_fusion.refs_0_.place, bf16[1024,2048]{1,0:T(8,128)(2,1)S(1)} %collective-permute-done.8.refs_1_.refs_4_, bf16[2,192,2048]{2,1,0:T(8,128)(2,1)S(1)} %copy-done.3, bf16[2,192,2048]{2,1,0:T(8,128)(2,1)} %collective-permute-done.7.refs_3_, ...), custom_call_target="tpu_custom_call", output_to_operand_aliasing={{}: (4, {})} | custom-call | flops 3221225472 | bytes 5767168 | tf_op jit(solution)/shard_map/back/pallas_call | solution.py:389
  86.3 1.7 copy-done
  88.0 2.0 %copy-done.6 = bf16[1024,2048]{1,0:T(8,128)(2,1)} copy-done((bf16[1024,2048]{1,0:T(8,128)(2,1)}, bf16[1024,2048]{1,0:T(8,128)(2,1)S(1)}, u32[]{:S(2)}) %copy-start.6) | copy-done | bytes 4194328
  90.0 17.9 %all-to-all-done = bf16[16,128,768]{2,1,0:T(8,128)(2,1)} async-done(((bf16[16,128,768]{2,1,0:T(8,128)(2,1)}), bf16[16,128,768]{2,1,0:T(8,128)(2,1)}, u32[]{:S(2)}, u32[]{:S(2)}) %all-to-all-start) | async-done | bytes 3145760 | tf_op jit(solution)/shard_map/all_to_all | solution.py:307
  107.9 3.6 %all-to-all-start.1 = ((bf16[16,128,768]{2,1,0:T(8,128)(2,1)}), bf16[16,128,768]{2,1,0:T(8,128)(2,1)S(1)}, u32[]{:S(2)}, u32[]{:S(2)}) async-start(bf16[16,128,768]{2,1,0:T(8,128)(2,1)} %bitcast.28), calls=%async_computation.1 | async-start | bytes 6291456 | tf_op jit(solution)/shard_map/all_to_all | solution.py:307
  111.6 2.2 %copy-done.5 = bf16[8,128,2048]{2,1,0:T(8,128)(2,1)S(1)} copy-done((bf16[8,128,2048]{2,1,0:T(8,128)(2,1)S(1)}, bf16[8,128,2048]{2,1,0:T(8,128)(2,1)}, u32[]{:S(2)}) %copy-start.5) | copy-done | bytes 4194328
  113.7 2.2 %copy-done.7 = bf16[1024,2048]{1,0:T(8,128)(2,1)S(1)} copy-done((bf16[1024,2048]{1,0:T(8,128)(2,1)S(1)}, bf16[1024,2048]{1,0:T(8,128)(2,1)}, u32[]{:S(2)}) %copy-start.7) | copy-done | bytes 4194328
  115.9 11.7 %gradient.1 = (f32[2,192,2048]{2,1,0:T(8,128)S(1)}, bf16[2,192,2048]{2,1,0:T(8,128)(2,1)S(1)}) custom-call(s32[3]{0:T(128)S(1)} %pad_add_fusion.refs_0_.place, bf16[2,8,128,768]{3,2,1,0:T(8,128)(2,1)} %bitcast.15.refs_1_.refs_2_, bf16[2,8,128,768]{3,2,1,0:T(8,128)(2,1)} %bitcast.15.refs_1_.refs_2_, bf16[1024,2048]{1,0:T(8,128)(2,1)S(1)} %bitcast.31, ...), custom_call_target="tpu_custom_call" | custom-call | flops 6442450944 | bytes 11534336 | tf_op jit(solution)/shard_map/gradient/pallas_call | solution.py:421
  127.7 1.6 collective-permute-start.9
  129.3 34.8 %collective-permute-done.9 = bf16[2,192,2048]{2,1,0:T(8,128)(2,1)S(1)} collective-permute-done((bf16[2,192,2048]{2,1,0:T(8,128)(2,1)S(1)}, bf16[2,192,2048]{2,1,0:T(8,128)(2,1)S(1)}, u32[]{:S(2)}, u32[]{:S(2)}) %collective-permute-start.9) | collective-permute-done | bytes 1572896 | tf_op jit(solution)/shard_map/ppermute | solution.py:451
  164.0 5.5 %fusion.2 = (bf16[2,192,2048]{2,1,0:T(8,128)(2,1)}, f32[2,192,2048]{2,1,0:T(8,128)}, bf16[2,192,2048]{2,1,0:T(8,128)(2,1)}) fusion(f32[2,192,2048]{2,1,0:T(8,128)S(1)} %get-tuple-element.35, bf16[2,192,2048]{2,1,0:T(8,128)(2,1)S(1)} %collective-permute-done.9, bf16[2,192,2048]{2,1,0:T(8,128)(2,1)S(1)} %copy-done.13, f32[2,192,2048]{2,1,0:T(8,128)S(1)} %copy-done.12, ...), kind=kLoop, calls=%fused_computation.6 | loop fusion | flops 16515072 | bytes 17301504 | tf_op jit(solution)/shard_map/convert_element_type | solution.py:459
  169.6 12.9 %all-to-all-done.1 = bf16[16,128,768]{2,1,0:T(8,128)(2,1)S(1)} async-done(((bf16[16,128,768]{2,1,0:T(8,128)(2,1)}), bf16[16,128,768]{2,1,0:T(8,128)(2,1)S(1)}, u32[]{:S(2)}, u32[]{:S(2)}) %all-to-all-start.1) | async-done | bytes 3145760 | tf_op jit(solution)/shard_map/all_to_all | solution.py:307
  182.4 4.0 %collect.1 = (bf16[128,8,768]{2,1,0:T(8,128)(2,1)}, f32[8,128]{1,0:T(8,128)}) custom-call(s32[8,128]{1,0:T(8,128)S(1)} %bitcast.34, f32[8,128]{1,0:T(8,128)S(1)} %bitcast.36, bf16[128,8,768]{2,1,0:T(8,128)(2,1)} %refs_2_.1, bf16[2,8,128,768]{3,2,1,0:T(8,128)(2,1)S(1)} %bitcast.27), custom_call_target="tpu_custom_call" | custom-call | tf_op jit(solution)/shard_map/collect/pallas_call | solution.py:461
  (39 shorter events, 1.8 us)
Async XLA Ops:
  0.6 10.9 %copy-start.1 = (bf16[128,8,768]{2,1,0:T(8,128)(2,1)S(1)}, bf16[128,8,768]{2,1,0:T(8,128)(2,1)}, u32[]{:S(2)}) copy-start(bf16[128,8,768]{2,1,0:T(8,128)(2,1)} %refs_2_.1) | copy-start | bytes 4718596
  0.6 25.3 %collective-permute-start = (bf16[128,2048]{1,0:T(8,128)(2,1)}, bf16[128,2048]{1,0:T(8,128)(2,1)}, u32[]{:S(2)}, u32[]{:S(2)}) collective-permute-start(bf16[128,2048]{1,0:T(8,128)(2,1)} %param.9), channel_id=1, source_target_pairs={{0,16},{16,0},{1,17},{17,1},{2,18},{18,2},{3,19},{19,3},{4,20},{20... | collective-permute-start | bytes 1572872 | tf_op jit(solution)/shard_map/ppermute | solution.py:290
  3.4 1.9 %copy-start.8 = (bf16[2,384,2048]{2,1,0:T(8,128)(2,1)S(1)}, bf16[2,384,2048]{2,1,0:T(8,128)(2,1)}, u32[]{:S(2)}) copy-start(bf16[2,384,2048]{2,1,0:T(8,128)(2,1)} %values.1) | copy-start | bytes 9437188
  5.3 0.8 copy-start.9
  6.1 5.5 %copy-start.10 = (s32[128,8]{0,1:T(8,128)S(1)}, s32[128,8]{0,1:T(8,128)}, u32[]{:S(2)}) copy-start(s32[128,8]{0,1:T(8,128)} %param.12) | copy-start | bytes 12292
  6.1 5.5 %copy-start.11 = (f32[128,8]{0,1:T(8,128)S(1)}, f32[128,8]{0,1:T(8,128)}, u32[]{:S(2)}) copy-start(f32[128,8]{0,1:T(8,128)} %param.11) | copy-start | bytes 12292
  8.0 21.4 %copy-start.2 = (bf16[2,192,2048]{2,1,0:T(8,128)(2,1)}, bf16[2,192,2048]{2,1,0:T(8,128)(2,1)S(1)}, u32[]{:S(2)}) copy-start(bf16[2,192,2048]{2,1,0:T(8,128)(2,1)S(1)} %scale.1.refs_2_) | copy-start | bytes 4718596
  8.0 17.9 %collective-permute-start.1 = (bf16[128,2048]{1,0:T(8,128)(2,1)}, bf16[128,2048]{1,0:T(8,128)(2,1)}, u32[]{:S(2)}, u32[]{:S(2)}) collective-permute-start(bf16[128,2048]{1,0:T(8,128)(2,1)} %param.9), channel_id=1, source_target_pairs={{0,4},{4,0},{1,5},{5,1},{2,6},{6,2},{3,7},{7,3},{8,12},{12,8},{9,1... | collective-permute-start | bytes 1572872 | tf_op jit(solution)/shard_map/ppermute | solution.py:290
  9.6 28.6 %collective-permute-start.2 = (bf16[128,2048]{1,0:T(8,128)(2,1)}, bf16[128,2048]{1,0:T(8,128)(2,1)}, u32[]{:S(2)}, u32[]{:S(2)}) collective-permute-start(bf16[128,2048]{1,0:T(8,128)(2,1)} %param.9), channel_id=1, source_target_pairs={{0,8},{8,0},{1,9},{9,1},{2,10},{10,2},{3,11},{11,3},{4,12},{12,4},... | collective-permute-start | bytes 1572872 | tf_op jit(solution)/shard_map/ppermute | solution.py:290
  10.1 63.1 %collective-permute-start.7 = (bf16[2,192,2048]{2,1,0:T(8,128)(2,1)S(1)}, bf16[2,192,2048]{2,1,0:T(8,128)(2,1)}, u32[]{:S(2)}, u32[]{:S(2)}) collective-permute-start(bf16[2,192,2048]{2,1,0:T(8,128)(2,1)S(1)} %scale.1.refs_2_), channel_id=1, source_target_pairs={{0,2},{2,0},{1,3},{3,1},{4,6},{6,4},{5,7},{7,5},{8,10},{10,8},{9,1... | collective-permute-start | bytes 4718600 | tf_op jit(solution)/shard_map/ppermute | solution.py:366
  26.0 47.1 %collective-permute-start.6 = (bf16[128,2048]{1,0:T(8,128)(2,1)}, bf16[128,2048]{1,0:T(8,128)(2,1)S(1)}, u32[]{:S(2)}, u32[]{:S(2)}) collective-permute-start(bf16[128,2048]{1,0:T(8,128)(2,1)} %collective-permute-done), channel_id=1, source_target_pairs={{0,12},{4,8},{8,4},{12,0},{1,13},{5,9},{9,5},{13,1},{2,14},{6,10},... | collective-permute-start | bytes 1572872 | tf_op jit(solution)/shard_map/ppermute | solution.py:296
  28.3 44.7 %collective-permute-start.5 = (bf16[128,2048]{1,0:T(8,128)(2,1)}, bf16[128,2048]{1,0:T(8,128)(2,1)S(1)}, u32[]{:S(2)}, u32[]{:S(2)}) collective-permute-start(bf16[128,2048]{1,0:T(8,128)(2,1)} %collective-permute-done), channel_id=1, source_target_pairs={{0,8},{8,0},{1,9},{9,1},{2,10},{10,2},{3,11},{11,3},{4,12},{12,4},... | collective-permute-start | bytes 1572872 | tf_op jit(solution)/shard_map/ppermute | solution.py:290
  28.9 44.0 %collective-permute-start.4 = (bf16[128,2048]{1,0:T(8,128)(2,1)}, bf16[128,2048]{1,0:T(8,128)(2,1)S(1)}, u32[]{:S(2)}, u32[]{:S(2)}) collective-permute-start(bf16[128,2048]{1,0:T(8,128)(2,1)} %collective-permute-done), channel_id=1, source_target_pairs={{0,4},{4,0},{1,5},{5,1},{2,6},{6,2},{3,7},{7,3},{8,12},{12,8},{9,1... | collective-permute-start | bytes 1572872 | tf_op jit(solution)/shard_map/ppermute | solution.py:290
  29.5 78.4 %all-to-all-start = ((bf16[16,128,768]{2,1,0:T(8,128)(2,1)}), bf16[16,128,768]{2,1,0:T(8,128)(2,1)}, u32[]{:S(2)}, u32[]{:S(2)}) async-start(bf16[16,128,768]{2,1,0:T(8,128)(2,1)} %bitcast.14), calls=%async_computation | async-start | bytes 6291456 | tf_op jit(solution)/shard_map/all_to_all | solution.py:307
  38.2 33.6 %collective-permute-start.3 = (bf16[128,2048]{1,0:T(8,128)(2,1)}, bf16[128,2048]{1,0:T(8,128)(2,1)S(1)}, u32[]{:S(2)}, u32[]{:S(2)}) collective-permute-start(bf16[128,2048]{1,0:T(8,128)(2,1)} %collective-permute-done.2), channel_id=1, source_target_pairs={{0,4},{4,0},{1,5},{5,1},{2,6},{6,2},{3,7},{7,3},{8,12},{12,8},{9,1... | collective-permute-start | bytes 1572872 | tf_op jit(solution)/shard_map/ppermute | solution.py:290
  40.8 32.4 %copy-start.3 = (bf16[2,192,2048]{2,1,0:T(8,128)(2,1)S(1)}, bf16[2,192,2048]{2,1,0:T(8,128)(2,1)}, u32[]{:S(2)}) copy-start(bf16[2,192,2048]{2,1,0:T(8,128)(2,1)} %copy-done.2) | copy-start | bytes 4718596
  73.2 6.8 %copy-start.4 = (bf16[8,128,2048]{2,1,0:T(8,128)(2,1)}, bf16[8,128,2048]{2,1,0:T(8,128)(2,1)S(1)}, u32[]{:S(2)}) copy-start(bf16[8,128,2048]{2,1,0:T(8,128)(2,1)S(1)} %bitcast_dynamic-update-slice_fusion) | copy-start | bytes 12582916
  73.2 7.2 %collective-permute-start.8 = (bf16[1024,2048]{1,0:T(8,128)(2,1)S(1)}, bf16[1024,2048]{1,0:T(8,128)(2,1)S(1)}, u32[]{:S(2)}, u32[]{:S(2)}) collective-permute-start(bf16[1024,2048]{1,0:T(8,128)(2,1)S(1)} %bitcast.29), channel_id=1, source_target_pairs={{0,1},{1,0},{2,3},{3,2},{4,5},{5,4},{6,7},{7,6},{8,9},{9,8},{10,11... | collective-permute-start | bytes 12582920 | tf_op jit(solution)/shard_map/ppermute | solution.py:380
  86.3 1.7 copy-start
  88.0 2.0 %copy-start.6 = (bf16[1024,2048]{1,0:T(8,128)(2,1)}, bf16[1024,2048]{1,0:T(8,128)(2,1)S(1)}, u32[]{:S(2)}) copy-start(bf16[1024,2048]{1,0:T(8,128)(2,1)S(1)} %collective-permute-done.8.refs_1_.refs_4_) | copy-start | bytes 12582916
  107.9 74.5 %all-to-all-start.1 = ((bf16[16,128,768]{2,1,0:T(8,128)(2,1)}), bf16[16,128,768]{2,1,0:T(8,128)(2,1)S(1)}, u32[]{:S(2)}, u32[]{:S(2)}) async-start(bf16[16,128,768]{2,1,0:T(8,128)(2,1)} %bitcast.28), calls=%async_computation.1 | async-start | bytes 6291456 | tf_op jit(solution)/shard_map/all_to_all | solution.py:307
  111.6 2.2 %copy-start.5 = (bf16[8,128,2048]{2,1,0:T(8,128)(2,1)S(1)}, bf16[8,128,2048]{2,1,0:T(8,128)(2,1)}, u32[]{:S(2)}) copy-start(bf16[8,128,2048]{2,1,0:T(8,128)(2,1)} %copy-done.4) | copy-start | bytes 12582916
  113.7 2.2 %copy-start.7 = (bf16[1024,2048]{1,0:T(8,128)(2,1)S(1)}, bf16[1024,2048]{1,0:T(8,128)(2,1)}, u32[]{:S(2)}) copy-start(bf16[1024,2048]{1,0:T(8,128)(2,1)} %copy-done.6) | copy-start | bytes 12582916
  115.9 48.1 %copy-start.12 = (f32[2,192,2048]{2,1,0:T(8,128)S(1)}, f32[2,192,2048]{2,1,0:T(8,128)}, u32[]{:S(2)}) copy-start(f32[2,192,2048]{2,1,0:T(8,128)} %param.15) | copy-start | bytes 9437188
  115.9 48.1 %copy-start.13 = (bf16[2,192,2048]{2,1,0:T(8,128)(2,1)S(1)}, bf16[2,192,2048]{2,1,0:T(8,128)(2,1)}, u32[]{:S(2)}) copy-start(bf16[2,192,2048]{2,1,0:T(8,128)(2,1)} %param.17) | copy-start | bytes 4718596
  115.9 48.1 %copy-start.14 = (bf16[2,192,2048]{2,1,0:T(8,128)(2,1)S(1)}, bf16[2,192,2048]{2,1,0:T(8,128)(2,1)}, u32[]{:S(2)}) copy-start(bf16[2,192,2048]{2,1,0:T(8,128)(2,1)} %param.16) | copy-start | bytes 4718596
  127.7 36.3 %collective-permute-start.9 = (bf16[2,192,2048]{2,1,0:T(8,128)(2,1)S(1)}, bf16[2,192,2048]{2,1,0:T(8,128)(2,1)S(1)}, u32[]{:S(2)}, u32[]{:S(2)}) collective-permute-start(bf16[2,192,2048]{2,1,0:T(8,128)(2,1)S(1)} %get-tuple-element.36), channel_id=1, source_target_pairs={{0,2},{2,0},{1,3},{3,1},{4,6},{6,4},{5,7},{7,5},{8,10},{10,8},{9,1... | collective-permute-start | bytes 4718600 | tf_op jit(solution)/shard_map/ppermute | solution.py:451

commit v7 on v6

--- a/solution.py
+++ b/solution.py
@@ -355,9 +355,9 @@
     for j in range(1, pair):
         dy[0, 0, j] = shift(after, "pair", j)
     keys = [key for key in sorted(dy, reverse=True) if not key[1]]
-    held = lax.optimization_barrier([spread] + [dy[key] for key in keys])
-    spread = held[0]
-    dy.update(zip(keys, held[1:]))
+    held = lax.optimization_barrier([dy[key] for key in keys] + [spread])
+    spread = held[-1]
+    dy.update(zip(keys, held))
     hid = exchange(spread)
     for b in range(1, halves):
         for i in range(1, line):

time: 187 us -> 187 us (level)
  no operation moved by 1% of the time
where the time goes in v7:
time: 187 us; the launch traced here: 186 us
  waiting for transfers between devices  106 us (57%)
  Pallas kernels  34.2 us (18%)
  starting transfers between devices  23.6 us (13%)
  local copies, waits for them, and re-layouts  16 us (9%)
  other arithmetic  5.62 us (3%)
    ppermute x6, waiting for transfers between devices, shift(): return lax.ppermute(x, axis, [(i, (i + by) % size) for i in range(size)])  40.2 us
    ppermute x1, waiting for transfers between devices, dense_body(): lax.ppermute(grads[o], 'fsdp', [(f, (f + o) % fsdp) for f in range(fsdp)])  34.8 us
    all_to_all x2, waiting for transfers between devices, exchange(): lax.all_to_all(x, ('replica', 'half', 'line', 'pair'), split_axis=0, conc...  30.7 us
    pallas_call x2, Pallas kernels, dense_body(): pl.pallas_call(lambda *refs: back_kernel((fsdp, replica), *refs), out_sha...  12.6 us
    pallas_call x1, Pallas kernels, dense_body(): pl.pallas_call(lambda *refs: gradient_kernel((fsdp, replica), *refs), out...  11.7 us
    unnamed x30, local copies, waits for them, and re-layouts  10.8 us
    all_to_all x2, starting transfers between devices, exchange(): lax.all_to_all(x, ('replica', 'half', 'line', 'pair'), split_axis=0, conc...  10.8 us
    ppermute x6, starting transfers between devices, shift(): return lax.ppermute(x, axis, [(i, (i + by) % size) for i in range(size)])  7.34 us
  transfers between devices with their start and end apart: 12, of which 6 were waited for; matrix products, arithmetic and copies ran while one was open for 6% of the time, Pallas kernels for 16%

profile of v7, /device:TPU:8, one launch (start us, length us, event | category | flops | bytes accessed | tf_op | source)
XLA Modules:
  0.0 186.4 jit_solution(13769903248594020653)
XLA Ops:
  0.6 2.7 %collective-permute-start = (bf16[128,2048]{1,0:T(8,128)(2,1)}, bf16[128,2048]{1,0:T(8,128)(2,1)}, u32[]{:S(2)}, u32[]{:S(2)}) collective-permute-start(bf16[128,2048]{1,0:T(8,128)(2,1)} %param.9), channel_id=1, source_target_pairs={{0,16},{16,0},{1,17},{17,1},{2,18},{18,2},{3,19},{19,3},{4,20},{20... | collective-permute-start | bytes 1572872 | tf_op jit(solution)/shard_map/ppermute | solution.py:290
  3.4 1.9 %copy-done.8 = bf16[2,384,2048]{2,1,0:T(8,128)(2,1)S(1)} copy-done((bf16[2,384,2048]{2,1,0:T(8,128)(2,1)S(1)}, bf16[2,384,2048]{2,1,0:T(8,128)(2,1)}, u32[]{:S(2)}) %copy-start.8) | copy-done | bytes 3145752
  5.3 0.8 copy-done.9
  6.1 2.0 %scale.1.refs_2_ = bf16[2,192,2048]{2,1,0:T(8,128)(2,1)S(1)} custom-call(s32[3]{0:T(128)S(1)} %pad_add_fusion.place.refs_0_, bf16[2,384,2048]{2,1,0:T(8,128)(2,1)S(1)} %copy-done.8, s32[2,16,384]{2,1,0:T(8,128)S(1)} %bitcast.32), custom_call_target="tpu_custom_call" | custom-call | tf_op jit(solution)/shard_map/scale/pallas_call | solution.py:311
  8.0 1.6 collective-permute-start.1
  10.1 1.5 collective-permute-start.7
  11.6 3.9 %spread.1 = bf16[2,8,128,768]{3,2,1,0:T(8,128)(2,1)} custom-call(s32[3]{0:T(128)S(1)} %pad_add_fusion.place.refs_0_, s32[8,128]{1,0:T(8,128)S(1)} %bitcast.33, f32[8,128]{1,0:T(8,128)S(1)} %bitcast.35, bf16[128,8,768]{2,1,0:T(8,128)(2,1)S(1)} %copy-done.1), custom_call_target="tpu_custom_call" | custom-call | tf_op jit(solution)/shard_map/spread/pallas_call | solution.py:335
  15.5 10.4 %collective-permute-done = bf16[128,2048]{1,0:T(8,128)(2,1)} collective-permute-done((bf16[128,2048]{1,0:T(8,128)(2,1)}, bf16[128,2048]{1,0:T(8,128)(2,1)}, u32[]{:S(2)}, u32[]{:S(2)}) %collective-permute-start) | collective-permute-done | bytes 524320 | tf_op jit(solution)/shard_map/ppermute | solution.py:290
  26.0 2.4 %collective-permute-start.6 = (bf16[128,2048]{1,0:T(8,128)(2,1)}, bf16[128,2048]{1,0:T(8,128)(2,1)S(1)}, u32[]{:S(2)}, u32[]{:S(2)}) collective-permute-start(bf16[128,2048]{1,0:T(8,128)(2,1)} %collective-permute-done), channel_id=1, source_target_pairs={{0,12},{4,8},{8,4},{12,0},{1,13},{5,9},{9,5},{13,1},{2,14},{6,10},... | collective-permute-start | bytes 1572872 | tf_op jit(solution)/shard_map/ppermute | solution.py:296
  28.3 0.6 collective-permute-start.5
  29.5 7.1 %all-to-all-start = ((bf16[16,128,768]{2,1,0:T(8,128)(2,1)}), bf16[16,128,768]{2,1,0:T(8,128)(2,1)}, u32[]{:S(2)}, u32[]{:S(2)}) async-start(bf16[16,128,768]{2,1,0:T(8,128)(2,1)} %bitcast.14), calls=%async_computation | async-start | bytes 6291456 | tf_op jit(solution)/shard_map/all_to_all | solution.py:307
  36.6 0.5 broadcast_in_dim.28
  37.1 1.1 bitcast_dynamic-update-slice_fusion.7
  38.2 1.5 collective-permute-start.3
  39.8 1.1 bitcast_dynamic-update-slice_fusion.6
  40.9 1.2 bitcast_dynamic-update-slice_fusion.5
  42.1 29.7 %collective-permute-done.3 = bf16[128,2048]{1,0:T(8,128)(2,1)S(1)} collective-permute-done((bf16[128,2048]{1,0:T(8,128)(2,1)}, bf16[128,2048]{1,0:T(8,128)(2,1)S(1)}, u32[]{:S(2)}, u32[]{:S(2)}) %collective-permute-start.3) | collective-permute-done | bytes 524320 | tf_op jit(solution)/shard_map/ppermute | solution.py:290
  71.9 1.1 bitcast_dynamic-update-slice_fusion.3
  73.3 6.7 %back.2.refs_4_ = bf16[2,8,128,768]{3,2,1,0:T(8,128)(2,1)S(1)} custom-call(s32[3]{0:T(128)S(1)} %pad_add_fusion.place.refs_0_, bf16[1024,2048]{1,0:T(8,128)(2,1)S(1)} %bitcast.30, bf16[2,192,2048]{2,1,0:T(8,128)(2,1)S(1)} %copy-done.3, bf16[2,192,2048]{2,1,0:T(8,128)(2,1)} %collective-permute-done.7.refs_3_), custom_call_target="tpu_custom_call" | custom-call | flops 3221225472 | bytes 5767168 | tf_op jit(solution)/shard_map/back/pallas_call | solution.py:389
  80.4 5.9 %back.3 = bf16[2,8,128,768]{3,2,1,0:T(8,128)(2,1)S(1)} custom-call(s32[3]{0:T(128)S(1)} %pad_add_fusion.place.refs_0_, bf16[1024,2048]{1,0:T(8,128)(2,1)S(1)} %collective-permute-done.8.refs_1_.refs_4_, bf16[2,192,2048]{2,1,0:T(8,128)(2,1)S(1)} %copy-done.3, bf16[2,192,2048]{2,1,0:T(8,128)(2,1)} %collective-permute-done.7.refs_3_, ...), custom_call_target="tpu_custom_call", output_to_operand_aliasing={{}: (4, {})} | custom-call | flops 3221225472 | bytes 5767168 | tf_op jit(solution)/shard_map/back/pallas_call | solution.py:389
  86.3 1.7 copy-done
  88.0 2.0 %copy-done.6 = bf16[1024,2048]{1,0:T(8,128)(2,1)} copy-done((bf16[1024,2048]{1,0:T(8,128)(2,1)}, bf16[1024,2048]{1,0:T(8,128)(2,1)S(1)}, u32[]{:S(2)}) %copy-start.6) | copy-done | bytes 4194328
  90.0 17.9 %all-to-all-done = bf16[16,128,768]{2,1,0:T(8,128)(2,1)} async-done(((bf16[16,128,768]{2,1,0:T(8,128)(2,1)}), bf16[16,128,768]{2,1,0:T(8,128)(2,1)}, u32[]{:S(2)}, u32[]{:S(2)}) %all-to-all-start) | async-done | bytes 3145760 | tf_op jit(solution)/shard_map/all_to_all | solution.py:307
  107.9 3.6 %all-to-all-start.1 = ((bf16[16,128,768]{2,1,0:T(8,128)(2,1)}), bf16[16,128,768]{2,1,0:T(8,128)(2,1)S(1)}, u32[]{:S(2)}, u32[]{:S(2)}) async-start(bf16[16,128,768]{2,1,0:T(8,128)(2,1)} %bitcast.28), calls=%async_computation.1 | async-start | bytes 6291456 | tf_op jit(solution)/shard_map/all_to_all | solution.py:307
  111.6 2.2 %copy-done.5 = bf16[8,128,2048]{2,1,0:T(8,128)(2,1)S(1)} copy-done((bf16[8,128,2048]{2,1,0:T(8,128)(2,1)S(1)}, bf16[8,128,2048]{2,1,0:T(8,128)(2,1)}, u32[]{:S(2)}) %copy-start.5) | copy-done | bytes 4194328
  113.7 2.2 %copy-done.7 = bf16[1024,2048]{1,0:T(8,128)(2,1)S(1)} copy-done((bf16[1024,2048]{1,0:T(8,128)(2,1)S(1)}, bf16[1024,2048]{1,0:T(8,128)(2,1)}, u32[]{:S(2)}) %copy-start.7) | copy-done | bytes 4194328
  115.9 11.7 %gradient.1 = (f32[2,192,2048]{2,1,0:T(8,128)S(1)}, bf16[2,192,2048]{2,1,0:T(8,128)(2,1)S(1)}) custom-call(s32[3]{0:T(128)S(1)} %pad_add_fusion.place.refs_0_, bf16[2,8,128,768]{3,2,1,0:T(8,128)(2,1)} %bitcast.15.refs_1_.refs_2_, bf16[2,8,128,768]{3,2,1,0:T(8,128)(2,1)} %bitcast.15.refs_1_.refs_2_, bf16[1024,2048]{1,0:T(8,128)(2,1)S(1)} %bitcast.31, ...), custom_call_target="tpu_custom_call" | custom-call | flops 6442450944 | bytes 11534336 | tf_op jit(solution)/shard_map/gradient/pallas_call | solution.py:421
  127.7 1.6 collective-permute-start.9
  129.3 34.8 %collective-permute-done.9 = bf16[2,192,2048]{2,1,0:T(8,128)(2,1)S(1)} collective-permute-done((bf16[2,192,2048]{2,1,0:T(8,128)(2,1)S(1)}, bf16[2,192,2048]{2,1,0:T(8,128)(2,1)S(1)}, u32[]{:S(2)}, u32[]{:S(2)}) %collective-permute-start.9) | collective-permute-done | bytes 1572896 | tf_op jit(solution)/shard_map/ppermute | solution.py:451
  164.0 5.5 %fusion.2 = (bf16[2,192,2048]{2,1,0:T(8,128)(2,1)}, f32[2,192,2048]{2,1,0:T(8,128)}, bf16[2,192,2048]{2,1,0:T(8,128)(2,1)}) fusion(f32[2,192,2048]{2,1,0:T(8,128)S(1)} %get-tuple-element.35, bf16[2,192,2048]{2,1,0:T(8,128)(2,1)S(1)} %collective-permute-done.9, bf16[2,192,2048]{2,1,0:T(8,128)(2,1)S(1)} %copy-done.13, f32[2,192,2048]{2,1,0:T(8,128)S(1)} %copy-done.12, ...), kind=kLoop, calls=%fused_computation.6 | loop fusion | flops 16515072 | bytes 17301504 | tf_op jit(solution)/shard_map/convert_element_type | solution.py:459
  169.6 12.9 %all-to-all-done.1 = bf16[16,128,768]{2,1,0:T(8,128)(2,1)S(1)} async-done(((bf16[16,128,768]{2,1,0:T(8,128)(2,1)}), bf16[16,128,768]{2,1,0:T(8,128)(2,1)S(1)}, u32[]{:S(2)}, u32[]{:S(2)}) %all-to-all-start.1) | async-done | bytes 3145760 | tf_op jit(solution)/shard_map/all_to_all | solution.py:307
  182.4 4.0 %collect.1 = (bf16[128,8,768]{2,1,0:T(8,128)(2,1)}, f32[8,128]{1,0:T(8,128)}) custom-call(s32[8,128]{1,0:T(8,128)S(1)} %bitcast.34, f32[8,128]{1,0:T(8,128)S(1)} %bitcast.36, bf16[128,8,768]{2,1,0:T(8,128)(2,1)} %refs_2_.1, bf16[2,8,128,768]{3,2,1,0:T(8,128)(2,1)S(1)} %bitcast.27), custom_call_target="tpu_custom_call" | custom-call | tf_op jit(solution)/shard_map/collect/pallas_call | solution.py:461
  (39 shorter events, 1.8 us)
Async XLA Ops:
  0.6 10.9 %copy-start.1 = (bf16[128,8,768]{2,1,0:T(8,128)(2,1)S(1)}, bf16[128,8,768]{2,1,0:T(8,128)(2,1)}, u32[]{:S(2)}) copy-start(bf16[128,8,768]{2,1,0:T(8,128)(2,1)} %refs_2_.1) | copy-start | bytes 4718596
  0.6 25.3 %collective-permute-start = (bf16[128,2048]{1,0:T(8,128)(2,1)}, bf16[128,2048]{1,0:T(8,128)(2,1)}, u32[]{:S(2)}, u32[]{:S(2)}) collective-permute-start(bf16[128,2048]{1,0:T(8,128)(2,1)} %param.9), channel_id=1, source_target_pairs={{0,16},{16,0},{1,17},{17,1},{2,18},{18,2},{3,19},{19,3},{4,20},{20... | collective-permute-start | bytes 1572872 | tf_op jit(solution)/shard_map/ppermute | solution.py:290
  3.4 1.9 %copy-start.8 = (bf16[2,384,2048]{2,1,0:T(8,128)(2,1)S(1)}, bf16[2,384,2048]{2,1,0:T(8,128)(2,1)}, u32[]{:S(2)}) copy-start(bf16[2,384,2048]{2,1,0:T(8,128)(2,1)} %values.1) | copy-start | bytes 9437188
  5.3 0.8 copy-start.9
  6.1 5.5 %copy-start.10 = (s32[128,8]{0,1:T(8,128)S(1)}, s32[128,8]{0,1:T(8,128)}, u32[]{:S(2)}) copy-start(s32[128,8]{0,1:T(8,128)} %param.12) | copy-start | bytes 12292
  6.1 5.5 %copy-start.11 = (f32[128,8]{0,1:T(8,128)S(1)}, f32[128,8]{0,1:T(8,128)}, u32[]{:S(2)}) copy-start(f32[128,8]{0,1:T(8,128)} %param.11) | copy-start | bytes 12292
  8.0 21.4 %copy-start.2 = (bf16[2,192,2048]{2,1,0:T(8,128)(2,1)}, bf16[2,192,2048]{2,1,0:T(8,128)(2,1)S(1)}, u32[]{:S(2)}) copy-start(bf16[2,192,2048]{2,1,0:T(8,128)(2,1)S(1)} %scale.1.refs_2_) | copy-start | bytes 4718596
  8.0 17.9 %collective-permute-start.1 = (bf16[128,2048]{1,0:T(8,128)(2,1)}, bf16[128,2048]{1,0:T(8,128)(2,1)}, u32[]{:S(2)}, u32[]{:S(2)}) collective-permute-start(bf16[128,2048]{1,0:T(8,128)(2,1)} %param.9), channel_id=1, source_target_pairs={{0,4},{4,0},{1,5},{5,1},{2,6},{6,2},{3,7},{7,3},{8,12},{12,8},{9,1... | collective-permute-start | bytes 1572872 | tf_op jit(solution)/shard_map/ppermute | solution.py:290
  9.6 28.6 %collective-permute-start.2 = (bf16[128,2048]{1,0:T(8,128)(2,1)}, bf16[128,2048]{1,0:T(8,128)(2,1)}, u32[]{:S(2)}, u32[]{:S(2)}) collective-permute-start(bf16[128,2048]{1,0:T(8,128)(2,1)} %param.9), channel_id=1, source_target_pairs={{0,8},{8,0},{1,9},{9,1},{2,10},{10,2},{3,11},{11,3},{4,12},{12,4},... | collective-permute-start | bytes 1572872 | tf_op jit(solution)/shard_map/ppermute | solution.py:290
  10.1 63.1 %collective-permute-start.7 = (bf16[2,192,2048]{2,1,0:T(8,128)(2,1)S(1)}, bf16[2,192,2048]{2,1,0:T(8,128)(2,1)}, u32[]{:S(2)}, u32[]{:S(2)}) collective-permute-start(bf16[2,192,2048]{2,1,0:T(8,128)(2,1)S(1)} %scale.1.refs_2_), channel_id=1, source_target_pairs={{0,2},{2,0},{1,3},{3,1},{4,6},{6,4},{5,7},{7,5},{8,10},{10,8},{9,1... | collective-permute-start | bytes 4718600 | tf_op jit(solution)/shard_map/ppermute | solution.py:366
  26.0 47.1 %collective-permute-start.6 = (bf16[128,2048]{1,0:T(8,128)(2,1)}, bf16[128,2048]{1,0:T(8,128)(2,1)S(1)}, u32[]{:S(2)}, u32[]{:S(2)}) collective-permute-start(bf16[128,2048]{1,0:T(8,128)(2,1)} %collective-permute-done), channel_id=1, source_target_pairs={{0,12},{4,8},{8,4},{12,0},{1,13},{5,9},{9,5},{13,1},{2,14},{6,10},... | collective-permute-start | bytes 1572872 | tf_op jit(solution)/shard_map/ppermute | solution.py:296
  28.3 44.7 %collective-permute-start.5 = (bf16[128,2048]{1,0:T(8,128)(2,1)}, bf16[128,2048]{1,0:T(8,128)(2,1)S(1)}, u32[]{:S(2)}, u32[]{:S(2)}) collective-permute-start(bf16[128,2048]{1,0:T(8,128)(2,1)} %collective-permute-done), channel_id=1, source_target_pairs={{0,8},{8,0},{1,9},{9,1},{2,10},{10,2},{3,11},{11,3},{4,12},{12,4},... | collective-permute-start | bytes 1572872 | tf_op jit(solution)/shard_map/ppermute | solution.py:290
  28.9 44.0 %collective-permute-start.4 = (bf16[128,2048]{1,0:T(8,128)(2,1)}, bf16[128,2048]{1,0:T(8,128)(2,1)S(1)}, u32[]{:S(2)}, u32[]{:S(2)}) collective-permute-start(bf16[128,2048]{1,0:T(8,128)(2,1)} %collective-permute-done), channel_id=1, source_target_pairs={{0,4},{4,0},{1,5},{5,1},{2,6},{6,2},{3,7},{7,3},{8,12},{12,8},{9,1... | collective-permute-start | bytes 1572872 | tf_op jit(solution)/shard_map/ppermute | solution.py:290
  29.5 78.4 %all-to-all-start = ((bf16[16,128,768]{2,1,0:T(8,128)(2,1)}), bf16[16,128,768]{2,1,0:T(8,128)(2,1)}, u32[]{:S(2)}, u32[]{:S(2)}) async-start(bf16[16,128,768]{2,1,0:T(8,128)(2,1)} %bitcast.14), calls=%async_computation | async-start | bytes 6291456 | tf_op jit(solution)/shard_map/all_to_all | solution.py:307
  38.2 33.6 %collective-permute-start.3 = (bf16[128,2048]{1,0:T(8,128)(2,1)}, bf16[128,2048]{1,0:T(8,128)(2,1)S(1)}, u32[]{:S(2)}, u32[]{:S(2)}) collective-permute-start(bf16[128,2048]{1,0:T(8,128)(2,1)} %collective-permute-done.2), channel_id=1, source_target_pairs={{0,4},{4,0},{1,5},{5,1},{2,6},{6,2},{3,7},{7,3},{8,12},{12,8},{9,1... | collective-permute-start | bytes 1572872 | tf_op jit(solution)/shard_map/ppermute | solution.py:290
  40.8 32.4 %copy-start.3 = (bf16[2,192,2048]{2,1,0:T(8,128)(2,1)S(1)}, bf16[2,192,2048]{2,1,0:T(8,128)(2,1)}, u32[]{:S(2)}) copy-start(bf16[2,192,2048]{2,1,0:T(8,128)(2,1)} %copy-done.2) | copy-start | bytes 4718596
  73.2 6.8 %copy-start.4 = (bf16[8,128,2048]{2,1,0:T(8,128)(2,1)}, bf16[8,128,2048]{2,1,0:T(8,128)(2,1)S(1)}, u32[]{:S(2)}) copy-start(bf16[8,128,2048]{2,1,0:T(8,128)(2,1)S(1)} %bitcast_dynamic-update-slice_fusion) | copy-start | bytes 12582916
  73.2 7.2 %collective-permute-start.8 = (bf16[1024,2048]{1,0:T(8,128)(2,1)S(1)}, bf16[1024,2048]{1,0:T(8,128)(2,1)S(1)}, u32[]{:S(2)}, u32[]{:S(2)}) collective-permute-start(bf16[1024,2048]{1,0:T(8,128)(2,1)S(1)} %bitcast.29), channel_id=1, source_target_pairs={{0,1},{1,0},{2,3},{3,2},{4,5},{5,4},{6,7},{7,6},{8,9},{9,8},{10,11... | collective-permute-start | bytes 12582920 | tf_op jit(solution)/shard_map/ppermute | solution.py:380
  86.3 1.7 copy-start
  88.0 2.0 %copy-start.6 = (bf16[1024,2048]{1,0:T(8,128)(2,1)}, bf16[1024,2048]{1,0:T(8,128)(2,1)S(1)}, u32[]{:S(2)}) copy-start(bf16[1024,2048]{1,0:T(8,128)(2,1)S(1)} %collective-permute-done.8.refs_1_.refs_4_) | copy-start | bytes 12582916
  107.9 74.5 %all-to-all-start.1 = ((bf16[16,128,768]{2,1,0:T(8,128)(2,1)}), bf16[16,128,768]{2,1,0:T(8,128)(2,1)S(1)}, u32[]{:S(2)}, u32[]{:S(2)}) async-start(bf16[16,128,768]{2,1,0:T(8,128)(2,1)} %bitcast.28), calls=%async_computation.1 | async-start | bytes 6291456 | tf_op jit(solution)/shard_map/all_to_all | solution.py:307
  111.6 2.2 %copy-start.5 = (bf16[8,128,2048]{2,1,0:T(8,128)(2,1)S(1)}, bf16[8,128,2048]{2,1,0:T(8,128)(2,1)}, u32[]{:S(2)}) copy-start(bf16[8,128,2048]{2,1,0:T(8,128)(2,1)} %copy-done.4) | copy-start | bytes 12582916
  113.7 2.2 %copy-start.7 = (bf16[1024,2048]{1,0:T(8,128)(2,1)S(1)}, bf16[1024,2048]{1,0:T(8,128)(2,1)}, u32[]{:S(2)}) copy-start(bf16[1024,2048]{1,0:T(8,128)(2,1)} %copy-done.6) | copy-start | bytes 12582916
  115.9 48.1 %copy-start.12 = (f32[2,192,2048]{2,1,0:T(8,128)S(1)}, f32[2,192,2048]{2,1,0:T(8,128)}, u32[]{:S(2)}) copy-start(f32[2,192,2048]{2,1,0:T(8,128)} %param.15) | copy-start | bytes 9437188
  115.9 48.1 %copy-start.13 = (bf16[2,192,2048]{2,1,0:T(8,128)(2,1)S(1)}, bf16[2,192,2048]{2,1,0:T(8,128)(2,1)}, u32[]{:S(2)}) copy-start(bf16[2,192,2048]{2,1,0:T(8,128)(2,1)} %param.17) | copy-start | bytes 4718596
  115.9 48.1 %copy-start.14 = (bf16[2,192,2048]{2,1,0:T(8,128)(2,1)S(1)}, bf16[2,192,2048]{2,1,0:T(8,128)(2,1)}, u32[]{:S(2)}) copy-start(bf16[2,192,2048]{2,1,0:T(8,128)(2,1)} %param.16) | copy-start | bytes 4718596
  127.7 36.3 %collective-permute-start.9 = (bf16[2,192,2048]{2,1,0:T(8,128)(2,1)S(1)}, bf16[2,192,2048]{2,1,0:T(8,128)(2,1)S(1)}, u32[]{:S(2)}, u32[]{:S(2)}) collective-permute-start(bf16[2,192,2048]{2,1,0:T(8,128)(2,1)S(1)} %get-tuple-element.36), channel_id=1, source_target_pairs={{0,2},{2,0},{1,3},{3,1},{4,6},{6,4},{5,7},{7,5},{8,10},{10,8},{9,1... | collective-permute-start | bytes 4718600 | tf_op jit(solution)/shard_map/ppermute | solution.py:451

commit v8 on v7

--- a/solution.py
+++ b/solution.py
@@ -167,13 +167,23 @@
 
 
 def collect_kernel(
-    here, parts, ids, gate, hidden, backs, hidden_grad, gate_grad, turned, gate_turned
+    here, parts, ids, gate, hidden, backs, hidden_grad, gate_grad, turned, gate_turned, held, sems
 ):
     fsdp, replica = parts
-    step, top, width = hidden.shape
+    step, top, width = hidden_grad.shape
     tokens = min(TOKEN_BLOCK, step)
     groups = backs.shape[1]
     unit = width // (fsdp * replica)
+
+    def fetch(number):
+        rows = pl.ds(pl.multiple_of(number * step, step), step)
+        return pltpu.make_async_copy(hidden.at[rows], held.at[rows], sems.at[number])
+
+    @pl.when(pl.program_id(0) == 0)
+    def _():
+        for number in range(held.shape[0] // step):
+            fetch(number).start()
+
     turn_routes(ids, gate, turned)
     for part in range(step // tokens):
         inside = slice(part * tokens, (part + 1) * tokens)
@@ -202,9 +212,11 @@
             ],
             axis=1,
         )
-        values = hidden[inside].astype(jnp.float32).reshape(tokens * top, width)
         scaled = route_column(turned[1, at]) * back
         hidden_grad[inside] = scaled.reshape(tokens, top, width).astype(jnp.bfloat16)
+        if part == 0:
+            fetch(pl.program_id(0)).wait()
+        values = held[at].astype(jnp.float32).reshape(tokens * top, width)
         column = jnp.sum(values * back, axis=1, keepdims=True)
         gate_turned[at] = route_square(column, tokens, top)
 
@@ -468,14 +480,19 @@
         in_specs=[
             pl.BlockSpec((top, tokens), lambda i: (0, 0)),
             pl.BlockSpec((top, tokens), lambda i: (0, 0)),
-            pl.BlockSpec((block, top, width), lambda i: (i, 0, 0)),
+            pl.BlockSpec(memory_space=pltpu.HBM),
             pl.BlockSpec((replica, groups, block, lanes), lambda i: (0, 0, i, 0)),
         ],
         out_specs=[
             pl.BlockSpec((block, top, width), lambda i: (i, 0, 0)),
             pl.BlockSpec((top, tokens), lambda i: (0, 0)),
         ],
-        scratch_shapes=[turned, pltpu.VMEM((tokens, top), jnp.float32)],
+        scratch_shapes=[
+            turned,
+            pltpu.VMEM((tokens, top), jnp.float32),
+            pltpu.VMEM(hidden_saved.shape, jnp.bfloat16),
+            pltpu.SemaphoreType.DMA((tokens // block,)),
+        ],
         compiler_params=pltpu.CompilerParams(vmem_limit_bytes=20 * 2**20),
         name="collect",
     )(

time: 187 us -> 187 us (level)
  no operation moved by 1% of the time
where the time goes in v8:
time: 187 us; the launch traced here: 186 us
  waiting for transfers between devices  106 us (57%)
  Pallas kernels  34.3 us (18%)
  starting transfers between devices  23.6 us (13%)
  local copies, waits for them, and re-layouts  16 us (9%)
  other arithmetic  5.62 us (3%)
    ppermute x6, waiting for transfers between devices, shift(): return lax.ppermute(x, axis, [(i, (i + by) % size) for i in range(size)])  40.2 us
    ppermute x1, waiting for transfers between devices, dense_body(): lax.ppermute(grads[o], 'fsdp', [(f, (f + o) % fsdp) for f in range(fsdp)])  34.8 us
    all_to_all x2, waiting for transfers between devices, exchange(): lax.all_to_all(x, ('replica', 'half', 'line', 'pair'), split_axis=0, conc...  30.7 us
    pallas_call x2, Pallas kernels, dense_body(): pl.pallas_call(lambda *refs: back_kernel((fsdp, replica), *refs), out_sha...  12.6 us
    pallas_call x1, Pallas kernels, dense_body(): pl.pallas_call(lambda *refs: gradient_kernel((fsdp, replica), *refs), out...  11.7 us
    unnamed x30, local copies, waits for them, and re-layouts  10.8 us
    all_to_all x2, starting transfers between devices, exchange(): lax.all_to_all(x, ('replica', 'half', 'line', 'pair'), split_axis=0, conc...  10.8 us
    ppermute x6, starting transfers between devices, shift(): return lax.ppermute(x, axis, [(i, (i + by) % size) for i in range(size)])  7.34 us
  transfers between devices with their start and end apart: 12, of which 6 were waited for; matrix products, arithmetic and copies ran while one was open for 6% of the time, Pallas kernels for 16%

profile of v8, /device:TPU:8, one launch (start us, length us, event | category | flops | bytes accessed | tf_op | source)
XLA Modules:
  0.0 186.5 jit_solution(14020977107427188584)
XLA Ops:
  0.6 2.7 %collective-permute-start = (bf16[128,2048]{1,0:T(8,128)(2,1)}, bf16[128,2048]{1,0:T(8,128)(2,1)}, u32[]{:S(2)}, u32[]{:S(2)}) collective-permute-start(bf16[128,2048]{1,0:T(8,128)(2,1)} %param.9), channel_id=1, source_target_pairs={{0,16},{16,0},{1,17},{17,1},{2,18},{18,2},{3,19},{19,3},{4,20},{20... | collective-permute-start | bytes 1572872 | tf_op jit(solution)/shard_map/ppermute | solution.py:302
  3.4 1.9 %copy-done.8 = bf16[2,384,2048]{2,1,0:T(8,128)(2,1)S(1)} copy-done((bf16[2,384,2048]{2,1,0:T(8,128)(2,1)S(1)}, bf16[2,384,2048]{2,1,0:T(8,128)(2,1)}, u32[]{:S(2)}) %copy-start.8) | copy-done | bytes 3145752
  5.3 0.8 copy-done.9
  6.1 2.0 %scale.1.refs_2_ = bf16[2,192,2048]{2,1,0:T(8,128)(2,1)S(1)} custom-call(s32[3]{0:T(128)S(1)} %pad_add_fusion.place.refs_0_, bf16[2,384,2048]{2,1,0:T(8,128)(2,1)S(1)} %copy-done.8, s32[2,16,384]{2,1,0:T(8,128)S(1)} %bitcast.32), custom_call_target="tpu_custom_call" | custom-call | tf_op jit(solution)/shard_map/scale/pallas_call | solution.py:323
  8.0 1.6 collective-permute-start.1
  10.1 1.5 collective-permute-start.7
  11.6 3.9 %spread.1 = bf16[2,8,128,768]{3,2,1,0:T(8,128)(2,1)} custom-call(s32[3]{0:T(128)S(1)} %pad_add_fusion.place.refs_0_, s32[8,128]{1,0:T(8,128)S(1)} %bitcast.33, f32[8,128]{1,0:T(8,128)S(1)} %bitcast.35, bf16[128,8,768]{2,1,0:T(8,128)(2,1)S(1)} %copy-done.1), custom_call_target="tpu_custom_call" | custom-call | tf_op jit(solution)/shard_map/spread/pallas_call | solution.py:347
  15.5 10.4 %collective-permute-done = bf16[128,2048]{1,0:T(8,128)(2,1)} collective-permute-done((bf16[128,2048]{1,0:T(8,128)(2,1)}, bf16[128,2048]{1,0:T(8,128)(2,1)}, u32[]{:S(2)}, u32[]{:S(2)}) %collective-permute-start) | collective-permute-done | bytes 524320 | tf_op jit(solution)/shard_map/ppermute | solution.py:302
  26.0 2.4 %collective-permute-start.6 = (bf16[128,2048]{1,0:T(8,128)(2,1)}, bf16[128,2048]{1,0:T(8,128)(2,1)S(1)}, u32[]{:S(2)}, u32[]{:S(2)}) collective-permute-start(bf16[128,2048]{1,0:T(8,128)(2,1)} %collective-permute-done), channel_id=1, source_target_pairs={{0,12},{4,8},{8,4},{12,0},{1,13},{5,9},{9,5},{13,1},{2,14},{6,10},... | collective-permute-start | bytes 1572872 | tf_op jit(solution)/shard_map/ppermute | solution.py:308
  28.3 0.6 collective-permute-start.5
  29.5 7.1 %all-to-all-start = ((bf16[16,128,768]{2,1,0:T(8,128)(2,1)}), bf16[16,128,768]{2,1,0:T(8,128)(2,1)}, u32[]{:S(2)}, u32[]{:S(2)}) async-start(bf16[16,128,768]{2,1,0:T(8,128)(2,1)} %bitcast.14), calls=%async_computation | async-start | bytes 6291456 | tf_op jit(solution)/shard_map/all_to_all | solution.py:319
  36.6 0.5 broadcast_in_dim.28
  37.1 1.1 bitcast_dynamic-update-slice_fusion.7
  38.2 1.5 collective-permute-start.3
  39.8 1.1 bitcast_dynamic-update-slice_fusion.6
  40.9 1.2 bitcast_dynamic-update-slice_fusion.5
  42.1 29.7 %collective-permute-done.3 = bf16[128,2048]{1,0:T(8,128)(2,1)S(1)} collective-permute-done((bf16[128,2048]{1,0:T(8,128)(2,1)}, bf16[128,2048]{1,0:T(8,128)(2,1)S(1)}, u32[]{:S(2)}, u32[]{:S(2)}) %collective-permute-start.3) | collective-permute-done | bytes 524320 | tf_op jit(solution)/shard_map/ppermute | solution.py:302
  71.9 1.1 bitcast_dynamic-update-slice_fusion.3
  73.3 6.7 %back.2.refs_4_ = bf16[2,8,128,768]{3,2,1,0:T(8,128)(2,1)S(1)} custom-call(s32[3]{0:T(128)S(1)} %pad_add_fusion.place.refs_0_, bf16[1024,2048]{1,0:T(8,128)(2,1)S(1)} %bitcast.30, bf16[2,192,2048]{2,1,0:T(8,128)(2,1)S(1)} %copy-done.3, bf16[2,192,2048]{2,1,0:T(8,128)(2,1)} %collective-permute-done.7.refs_3_), custom_call_target="tpu_custom_call" | custom-call | flops 3221225472 | bytes 5767168 | tf_op jit(solution)/shard_map/back/pallas_call | solution.py:401
  80.4 5.9 %back.3 = bf16[2,8,128,768]{3,2,1,0:T(8,128)(2,1)S(1)} custom-call(s32[3]{0:T(128)S(1)} %pad_add_fusion.place.refs_0_, bf16[1024,2048]{1,0:T(8,128)(2,1)S(1)} %collective-permute-done.8.refs_1_.refs_4_, bf16[2,192,2048]{2,1,0:T(8,128)(2,1)S(1)} %copy-done.3, bf16[2,192,2048]{2,1,0:T(8,128)(2,1)} %collective-permute-done.7.refs_3_, ...), custom_call_target="tpu_custom_call", output_to_operand_aliasing={{}: (4, {})} | custom-call | flops 3221225472 | bytes 5767168 | tf_op jit(solution)/shard_map/back/pallas_call | solution.py:401
  86.3 1.7 copy-done
  88.0 2.0 %copy-done.6 = bf16[1024,2048]{1,0:T(8,128)(2,1)} copy-done((bf16[1024,2048]{1,0:T(8,128)(2,1)}, bf16[1024,2048]{1,0:T(8,128)(2,1)S(1)}, u32[]{:S(2)}) %copy-start.6) | copy-done | bytes 4194328
  90.0 17.9 %all-to-all-done = bf16[16,128,768]{2,1,0:T(8,128)(2,1)} async-done(((bf16[16,128,768]{2,1,0:T(8,128)(2,1)}), bf16[16,128,768]{2,1,0:T(8,128)(2,1)}, u32[]{:S(2)}, u32[]{:S(2)}) %all-to-all-start) | async-done | bytes 3145760 | tf_op jit(solution)/shard_map/all_to_all | solution.py:319
  107.9 3.6 %all-to-all-start.1 = ((bf16[16,128,768]{2,1,0:T(8,128)(2,1)}), bf16[16,128,768]{2,1,0:T(8,128)(2,1)S(1)}, u32[]{:S(2)}, u32[]{:S(2)}) async-start(bf16[16,128,768]{2,1,0:T(8,128)(2,1)} %bitcast.28), calls=%async_computation.1 | async-start | bytes 6291456 | tf_op jit(solution)/shard_map/all_to_all | solution.py:319
  111.6 2.2 %copy-done.5 = bf16[8,128,2048]{2,1,0:T(8,128)(2,1)S(1)} copy-done((bf16[8,128,2048]{2,1,0:T(8,128)(2,1)S(1)}, bf16[8,128,2048]{2,1,0:T(8,128)(2,1)}, u32[]{:S(2)}) %copy-start.5) | copy-done | bytes 4194328
  113.7 2.2 %copy-done.7 = bf16[1024,2048]{1,0:T(8,128)(2,1)S(1)} copy-done((bf16[1024,2048]{1,0:T(8,128)(2,1)S(1)}, bf16[1024,2048]{1,0:T(8,128)(2,1)}, u32[]{:S(2)}) %copy-start.7) | copy-done | bytes 4194328
  115.9 11.7 %gradient.1 = (f32[2,192,2048]{2,1,0:T(8,128)S(1)}, bf16[2,192,2048]{2,1,0:T(8,128)(2,1)S(1)}) custom-call(s32[3]{0:T(128)S(1)} %pad_add_fusion.place.refs_0_, bf16[2,8,128,768]{3,2,1,0:T(8,128)(2,1)} %bitcast.15.refs_1_.refs_2_, bf16[2,8,128,768]{3,2,1,0:T(8,128)(2,1)} %bitcast.15.refs_1_.refs_2_, bf16[1024,2048]{1,0:T(8,128)(2,1)S(1)} %bitcast.31, ...), custom_call_target="tpu_custom_call" | custom-call | flops 6442450944 | bytes 11534336 | tf_op jit(solution)/shard_map/gradient/pallas_call | solution.py:433
  127.7 1.6 collective-permute-start.9
  129.3 34.8 %collective-permute-done.9 = bf16[2,192,2048]{2,1,0:T(8,128)(2,1)S(1)} collective-permute-done((bf16[2,192,2048]{2,1,0:T(8,128)(2,1)S(1)}, bf16[2,192,2048]{2,1,0:T(8,128)(2,1)S(1)}, u32[]{:S(2)}, u32[]{:S(2)}) %collective-permute-start.9) | collective-permute-done | bytes 1572896 | tf_op jit(solution)/shard_map/ppermute | solution.py:463
  164.0 5.5 %fusion.2 = (bf16[2,192,2048]{2,1,0:T(8,128)(2,1)}, f32[2,192,2048]{2,1,0:T(8,128)}, bf16[2,192,2048]{2,1,0:T(8,128)(2,1)}) fusion(f32[2,192,2048]{2,1,0:T(8,128)S(1)} %get-tuple-element.35, bf16[2,192,2048]{2,1,0:T(8,128)(2,1)S(1)} %collective-permute-done.9, bf16[2,192,2048]{2,1,0:T(8,128)(2,1)S(1)} %copy-done.13, f32[2,192,2048]{2,1,0:T(8,128)S(1)} %copy-done.12, ...), kind=kLoop, calls=%fused_computation.6 | loop fusion | flops 16515072 | bytes 17301504 | tf_op jit(solution)/shard_map/convert_element_type | solution.py:471
  169.6 12.9 %all-to-all-done.1 = bf16[16,128,768]{2,1,0:T(8,128)(2,1)S(1)} async-done(((bf16[16,128,768]{2,1,0:T(8,128)(2,1)}), bf16[16,128,768]{2,1,0:T(8,128)(2,1)S(1)}, u32[]{:S(2)}, u32[]{:S(2)}) %all-to-all-start.1) | async-done | bytes 3145760 | tf_op jit(solution)/shard_map/all_to_all | solution.py:319
  182.4 4.1 %collect.1 = (bf16[128,8,768]{2,1,0:T(8,128)(2,1)}, f32[8,128]{1,0:T(8,128)}) custom-call(s32[8,128]{1,0:T(8,128)S(1)} %bitcast.34, f32[8,128]{1,0:T(8,128)S(1)} %bitcast.36, bf16[128,8,768]{2,1,0:T(8,128)(2,1)} %refs_2_.1, bf16[2,8,128,768]{3,2,1,0:T(8,128)(2,1)S(1)} %bitcast.27), custom_call_target="tpu_custom_call" | custom-call | tf_op jit(solution)/shard_map/collect/pallas_call | solution.py:473
  (39 shorter events, 1.8 us)
Async XLA Ops:
  0.6 10.9 %copy-start.1 = (bf16[128,8,768]{2,1,0:T(8,128)(2,1)S(1)}, bf16[128,8,768]{2,1,0:T(8,128)(2,1)}, u32[]{:S(2)}) copy-start(bf16[128,8,768]{2,1,0:T(8,128)(2,1)} %refs_2_.1) | copy-start | bytes 4718596
  0.6 25.3 %collective-permute-start = (bf16[128,2048]{1,0:T(8,128)(2,1)}, bf16[128,2048]{1,0:T(8,128)(2,1)}, u32[]{:S(2)}, u32[]{:S(2)}) collective-permute-start(bf16[128,2048]{1,0:T(8,128)(2,1)} %param.9), channel_id=1, source_target_pairs={{0,16},{16,0},{1,17},{17,1},{2,18},{18,2},{3,19},{19,3},{4,20},{20... | collective-permute-start | bytes 1572872 | tf_op jit(solution)/shard_map/ppermute | solution.py:302
  3.4 1.9 %copy-start.8 = (bf16[2,384,2048]{2,1,0:T(8,128)(2,1)S(1)}, bf16[2,384,2048]{2,1,0:T(8,128)(2,1)}, u32[]{:S(2)}) copy-start(bf16[2,384,2048]{2,1,0:T(8,128)(2,1)} %values.1) | copy-start | bytes 9437188
  5.3 0.8 copy-start.9
  6.1 5.5 %copy-start.10 = (s32[128,8]{0,1:T(8,128)S(1)}, s32[128,8]{0,1:T(8,128)}, u32[]{:S(2)}) copy-start(s32[128,8]{0,1:T(8,128)} %param.12) | copy-start | bytes 12292
  6.1 5.5 %copy-start.11 = (f32[128,8]{0,1:T(8,128)S(1)}, f32[128,8]{0,1:T(8,128)}, u32[]{:S(2)}) copy-start(f32[128,8]{0,1:T(8,128)} %param.11) | copy-start | bytes 12292
  8.0 21.4 %copy-start.2 = (bf16[2,192,2048]{2,1,0:T(8,128)(2,1)}, bf16[2,192,2048]{2,1,0:T(8,128)(2,1)S(1)}, u32[]{:S(2)}) copy-start(bf16[2,192,2048]{2,1,0:T(8,128)(2,1)S(1)} %scale.1.refs_2_) | copy-start | bytes 4718596
  8.0 17.9 %collective-permute-start.1 = (bf16[128,2048]{1,0:T(8,128)(2,1)}, bf16[128,2048]{1,0:T(8,128)(2,1)}, u32[]{:S(2)}, u32[]{:S(2)}) collective-permute-start(bf16[128,2048]{1,0:T(8,128)(2,1)} %param.9), channel_id=1, source_target_pairs={{0,4},{4,0},{1,5},{5,1},{2,6},{6,2},{3,7},{7,3},{8,12},{12,8},{9,1... | collective-permute-start | bytes 1572872 | tf_op jit(solution)/shard_map/ppermute | solution.py:302
  9.6 28.6 %collective-permute-start.2 = (bf16[128,2048]{1,0:T(8,128)(2,1)}, bf16[128,2048]{1,0:T(8,128)(2,1)}, u32[]{:S(2)}, u32[]{:S(2)}) collective-permute-start(bf16[128,2048]{1,0:T(8,128)(2,1)} %param.9), channel_id=1, source_target_pairs={{0,8},{8,0},{1,9},{9,1},{2,10},{10,2},{3,11},{11,3},{4,12},{12,4},... | collective-permute-start | bytes 1572872 | tf_op jit(solution)/shard_map/ppermute | solution.py:302
  10.1 63.1 %collective-permute-start.7 = (bf16[2,192,2048]{2,1,0:T(8,128)(2,1)S(1)}, bf16[2,192,2048]{2,1,0:T(8,128)(2,1)}, u32[]{:S(2)}, u32[]{:S(2)}) collective-permute-start(bf16[2,192,2048]{2,1,0:T(8,128)(2,1)S(1)} %scale.1.refs_2_), channel_id=1, source_target_pairs={{0,2},{2,0},{1,3},{3,1},{4,6},{6,4},{5,7},{7,5},{8,10},{10,8},{9,1... | collective-permute-start | bytes 4718600 | tf_op jit(solution)/shard_map/ppermute | solution.py:378
  26.0 47.1 %collective-permute-start.6 = (bf16[128,2048]{1,0:T(8,128)(2,1)}, bf16[128,2048]{1,0:T(8,128)(2,1)S(1)}, u32[]{:S(2)}, u32[]{:S(2)}) collective-permute-start(bf16[128,2048]{1,0:T(8,128)(2,1)} %collective-permute-done), channel_id=1, source_target_pairs={{0,12},{4,8},{8,4},{12,0},{1,13},{5,9},{9,5},{13,1},{2,14},{6,10},... | collective-permute-start | bytes 1572872 | tf_op jit(solution)/shard_map/ppermute | solution.py:308
  28.3 44.7 %collective-permute-start.5 = (bf16[128,2048]{1,0:T(8,128)(2,1)}, bf16[128,2048]{1,0:T(8,128)(2,1)S(1)}, u32[]{:S(2)}, u32[]{:S(2)}) collective-permute-start(bf16[128,2048]{1,0:T(8,128)(2,1)} %collective-permute-done), channel_id=1, source_target_pairs={{0,8},{8,0},{1,9},{9,1},{2,10},{10,2},{3,11},{11,3},{4,12},{12,4},... | collective-permute-start | bytes 1572872 | tf_op jit(solution)/shard_map/ppermute | solution.py:302
  28.9 44.0 %collective-permute-start.4 = (bf16[128,2048]{1,0:T(8,128)(2,1)}, bf16[128,2048]{1,0:T(8,128)(2,1)S(1)}, u32[]{:S(2)}, u32[]{:S(2)}) collective-permute-start(bf16[128,2048]{1,0:T(8,128)(2,1)} %collective-permute-done), channel_id=1, source_target_pairs={{0,4},{4,0},{1,5},{5,1},{2,6},{6,2},{3,7},{7,3},{8,12},{12,8},{9,1... | collective-permute-start | bytes 1572872 | tf_op jit(solution)/shard_map/ppermute | solution.py:302
  29.5 78.4 %all-to-all-start = ((bf16[16,128,768]{2,1,0:T(8,128)(2,1)}), bf16[16,128,768]{2,1,0:T(8,128)(2,1)}, u32[]{:S(2)}, u32[]{:S(2)}) async-start(bf16[16,128,768]{2,1,0:T(8,128)(2,1)} %bitcast.14), calls=%async_computation | async-start | bytes 6291456 | tf_op jit(solution)/shard_map/all_to_all | solution.py:319
  38.2 33.6 %collective-permute-start.3 = (bf16[128,2048]{1,0:T(8,128)(2,1)}, bf16[128,2048]{1,0:T(8,128)(2,1)S(1)}, u32[]{:S(2)}, u32[]{:S(2)}) collective-permute-start(bf16[128,2048]{1,0:T(8,128)(2,1)} %collective-permute-done.2), channel_id=1, source_target_pairs={{0,4},{4,0},{1,5},{5,1},{2,6},{6,2},{3,7},{7,3},{8,12},{12,8},{9,1... | collective-permute-start | bytes 1572872 | tf_op jit(solution)/shard_map/ppermute | solution.py:302
  40.8 32.4 %copy-start.3 = (bf16[2,192,2048]{2,1,0:T(8,128)(2,1)S(1)}, bf16[2,192,2048]{2,1,0:T(8,128)(2,1)}, u32[]{:S(2)}) copy-start(bf16[2,192,2048]{2,1,0:T(8,128)(2,1)} %copy-done.2) | copy-start | bytes 4718596
  73.2 6.8 %copy-start.4 = (bf16[8,128,2048]{2,1,0:T(8,128)(2,1)}, bf16[8,128,2048]{2,1,0:T(8,128)(2,1)S(1)}, u32[]{:S(2)}) copy-start(bf16[8,128,2048]{2,1,0:T(8,128)(2,1)S(1)} %bitcast_dynamic-update-slice_fusion) | copy-start | bytes 12582916
  73.2 7.2 %collective-permute-start.8 = (bf16[1024,2048]{1,0:T(8,128)(2,1)S(1)}, bf16[1024,2048]{1,0:T(8,128)(2,1)S(1)}, u32[]{:S(2)}, u32[]{:S(2)}) collective-permute-start(bf16[1024,2048]{1,0:T(8,128)(2,1)S(1)} %bitcast.29), channel_id=1, source_target_pairs={{0,1},{1,0},{2,3},{3,2},{4,5},{5,4},{6,7},{7,6},{8,9},{9,8},{10,11... | collective-permute-start | bytes 12582920 | tf_op jit(solution)/shard_map/ppermute | solution.py:392
  86.3 1.7 copy-start
  88.0 2.0 %copy-start.6 = (bf16[1024,2048]{1,0:T(8,128)(2,1)}, bf16[1024,2048]{1,0:T(8,128)(2,1)S(1)}, u32[]{:S(2)}) copy-start(bf16[1024,2048]{1,0:T(8,128)(2,1)S(1)} %collective-permute-done.8.refs_1_.refs_4_) | copy-start | bytes 12582916
  107.9 74.5 %all-to-all-start.1 = ((bf16[16,128,768]{2,1,0:T(8,128)(2,1)}), bf16[16,128,768]{2,1,0:T(8,128)(2,1)S(1)}, u32[]{:S(2)}, u32[]{:S(2)}) async-start(bf16[16,128,768]{2,1,0:T(8,128)(2,1)} %bitcast.28), calls=%async_computation.1 | async-start | bytes 6291456 | tf_op jit(solution)/shard_map/all_to_all | solution.py:319
  111.6 2.2 %copy-start.5 = (bf16[8,128,2048]{2,1,0:T(8,128)(2,1)S(1)}, bf16[8,128,2048]{2,1,0:T(8,128)(2,1)}, u32[]{:S(2)}) copy-start(bf16[8,128,2048]{2,1,0:T(8,128)(2,1)} %copy-done.4) | copy-start | bytes 12582916
  113.7 2.2 %copy-start.7 = (bf16[1024,2048]{1,0:T(8,128)(2,1)S(1)}, bf16[1024,2048]{1,0:T(8,128)(2,1)}, u32[]{:S(2)}) copy-start(bf16[1024,2048]{1,0:T(8,128)(2,1)} %copy-done.6) | copy-start | bytes 12582916
  115.9 48.1 %copy-start.12 = (f32[2,192,2048]{2,1,0:T(8,128)S(1)}, f32[2,192,2048]{2,1,0:T(8,128)}, u32[]{:S(2)}) copy-start(f32[2,192,2048]{2,1,0:T(8,128)} %param.15) | copy-start | bytes 9437188
  115.9 48.1 %copy-start.13 = (bf16[2,192,2048]{2,1,0:T(8,128)(2,1)S(1)}, bf16[2,192,2048]{2,1,0:T(8,128)(2,1)}, u32[]{:S(2)}) copy-start(bf16[2,192,2048]{2,1,0:T(8,128)(2,1)} %param.17) | copy-start | bytes 4718596
  115.9 48.1 %copy-start.14 = (bf16[2,192,2048]{2,1,0:T(8,128)(2,1)S(1)}, bf16[2,192,2048]{2,1,0:T(8,128)(2,1)}, u32[]{:S(2)}) copy-start(bf16[2,192,2048]{2,1,0:T(8,128)(2,1)} %param.16) | copy-start | bytes 4718596
  127.7 36.3 %collective-permute-start.9 = (bf16[2,192,2048]{2,1,0:T(8,128)(2,1)S(1)}, bf16[2,192,2048]{2,1,0:T(8,128)(2,1)S(1)}, u32[]{:S(2)}, u32[]{:S(2)}) collective-permute-start(bf16[2,192,2048]{2,1,0:T(8,128)(2,1)S(1)} %get-tuple-element.36), channel_id=1, source_target_pairs={{0,2},{2,0},{1,3},{3,1},{4,6},{6,4},{5,7},{7,5},{8,10},{10,8},{9,1... | collective-permute-start | bytes 4718600 | tf_op jit(solution)/shard_map/ppermute | solution.py:463
